TPU v7x, 256 devices: a whole 4x4x8 slice. The times are simulated.
256 devices in a mesh: row: 32 (over y_hi, z, core), col: 8 (over y_lo, x).
Axes of the slice: x: 4, y: 4 (y_hi: 2, y_lo: 2; y = y_hi * 2 + y_lo), z: 8, core: 2. Of those that a mesh axis runs over, the one named last changes fastest.
Arguments:
- tokens: bfloat16 [256, 128, 256], P('row', 'col'), may hold values from -6 to 6
- gain_fine: float32 [256], replicated, may hold values from 0.1 to 1.9
- qkv_fine: bfloat16 [256, 768], replicated, may hold values from -0.375 to 0.375
- out_fine: bfloat16 [256, 256], replicated, may hold values from -0.375 to 0.375
- w_merge: bfloat16 [1024, 512], replicated, may hold values from -0.1875 to 0.1875
- gain_coarse: float32 [512], replicated, may hold values from 0.1 to 1.9
- qkv_coarse: bfloat16 [512, 1536], replicated, may hold values from -0.25 to 0.25
- out_coarse: bfloat16 [512, 512], replicated, may hold values from -0.25 to 0.25
- grad_fine: bfloat16 [256, 128, 256], P('row', 'col'), may hold values from -6 to 6
- grad_coarse: bfloat16 [128, 64, 512], P('row', 'col'), may hold values from -6 to 6
Outputs:
- grad_tokens: bfloat16 [256, 128, 256], P('row', 'col')
- grad_gain_fine: float32 [256], replicated
- grad_qkv_fine: bfloat16 [256, 768], replicated
- grad_out_fine: bfloat16 [256, 256], replicated
- grad_merge: bfloat16 [1024, 512], replicated
- grad_gain_coarse: float32 [512], replicated
- grad_qkv_coarse: bfloat16 [512, 1536], replicated
- grad_out_coarse: bfloat16 [512, 512], replicated
All inputs are finite; a program needn't handle non-finite values.
Results may differ from a plain program's by a relative error of at most 0.035.
Values may be sent and summed in bfloat16 or wider, within the bound.
No kernel may reach another device: no remote copies, remote signals or barrier semaphores. Data moves between devices by JAX's collectives and lax.ppermute only.
A program may use at most 64 MiB of HBM per device.

v0:
```python
import math

import jax
import jax.numpy as jnp
from jax import lax
from jax.sharding import PartitionSpec as P

HEAD = 64
RADIUS = 3


norm_eps = 1e-06


def shifted(x, axis, by):
    count = lax.axis_size(axis)
    pairs = [(i, i + by) for i in range(count) if 0 <= i + by < count]
    return lax.ppermute(x, axis, pairs)


def extended_2(x, sides, width):
    for axis, dim in sides:
        count, length = (lax.axis_size(axis), x.shape[dim])
        up = [(i, (i + 1) % count) for i in range(count - 1)]
        down = [(j, i) for i, j in up]
        last = lax.slice_in_dim(x, length - width, length, axis=dim)
        leading = lax.slice_in_dim(x, 0, width, axis=dim)
        before = lax.ppermute(last, axis, up)
        after = lax.ppermute(leading, axis, down)
        x = jnp.concatenate([before, x, after], axis=dim)
    return x


def norm_forward(tokens, gain):
    values = tokens.astype(jnp.float32)
    scale = lax.rsqrt(jnp.mean(values * values, axis=-1, keepdims=True) + norm_eps)
    normed = (values * scale * gain).astype(jnp.bfloat16)
    return (values, scale, normed)


def norm_backward(values, scale, gain, upstream):
    gain_part = jnp.sum(upstream * values * scale, axis=(0, 1))
    weighted = upstream * gain
    inner = jnp.mean(weighted * values, axis=-1, keepdims=True)
    return (weighted * scale - values * (scale * scale * scale) * inner, gain_part)


def key_validity(rows, columns):
    row_ids = lax.axis_index("row") * rows - RADIUS + jnp.arange(rows + 2 * RADIUS)
    col_ids = lax.axis_index("col") * columns - RADIUS + jnp.arange(columns + 2 * RADIUS)
    row_ok = (row_ids >= 0) & (row_ids < rows * lax.axis_size("row"))
    col_ok = (col_ids >= 0) & (col_ids < columns * lax.axis_size("col"))
    return row_ok[:, None] & col_ok[None, :]


def block_layout(columns):
    block = math.gcd(columns, 16)
    return (block, columns // block, block + 2 * RADIUS)


def split_blocks(extended):
    return jnp.stack([extended], axis=1)


def stack_window(extended, rows):
    return jnp.stack([extended[down : down + rows] for down in range(2 * RADIUS + 1)], axis=2)


def attention_forward(query, kv_ext, valid_ext, heads):
    rows, columns, width = query.shape
    head_dim = width // heads
    extent = 2 * RADIUS + 1
    block, count, wide = block_layout(columns)
    keys_all = extent * wide
    factor = 1.0 / math.sqrt(head_dim)
    window = stack_window(split_blocks(kv_ext), rows).reshape(
        rows, count, keys_all, 2, heads, head_dim
    )
    keys = window[:, :, :, 0]
    values_win = window[:, :, :, 1]
    seen = stack_window(split_blocks(valid_ext), rows).reshape(rows, count, 1, 1, keys_all)
    key_col = jnp.tile(jnp.arange(wide), extent)
    offset = key_col[None, :] - jnp.arange(block)[:, None]
    band = (offset >= 0) & (offset <= 2 * RADIUS)
    mask = band[None, None, None] & seen
    query_heads = query.reshape(rows, count, block, heads, head_dim)
    scores = (
        jnp.einsum("rnchd,rnkhd->rnhck", query_heads, keys, preferred_element_type=jnp.float32)
        * factor
    )
    weights = jnp.where(mask, jnp.exp(scores), 0.0)
    probability = weights / jnp.sum(weights, axis=-1, keepdims=True)
    probability_b = probability.astype(jnp.bfloat16)
    attended = jnp.einsum(
        "rnhck,rnkhd->rnchd", probability_b, values_win, preferred_element_type=jnp.float32
    )
    attended = attended.astype(jnp.bfloat16).reshape(rows, columns, width)
    return (attended, (query_heads, keys, values_win, probability, probability_b, factor))


def attention_backward(saved, grad_att):
    query_heads, keys, values_win, probability, probability_b, factor = saved
    rows, count, block, heads, head_dim = query_heads.shape
    width = heads * head_dim
    columns = count * block
    extent = 2 * RADIUS + 1
    wide = block + 2 * RADIUS
    span = columns + 2 * RADIUS
    grad_heads = grad_att.reshape(rows, count, block, heads, head_dim)
    dprob = jnp.einsum(
        "rnchd,rnkhd->rnhck", grad_heads, values_win, preferred_element_type=jnp.float32
    )
    total = jnp.sum(probability * dprob, axis=-1, keepdims=True)
    dscore = (probability * (dprob - total) * factor).astype(jnp.bfloat16)
    grad_query = jnp.einsum(
        "rnhck,rnkhd->rnchd", dscore, keys, preferred_element_type=jnp.float32
    ).reshape(rows, columns, width)
    grad_keys = jnp.einsum(
        "rnhck,rnchd->rnkhd", dscore, query_heads, preferred_element_type=jnp.float32
    )
    grad_values = jnp.einsum(
        "rnhck,rnchd->rnkhd", probability_b, grad_heads, preferred_element_type=jnp.float32
    )
    grad_window = jnp.concatenate(
        [
            grad_keys.reshape(rows, count, extent, wide, width),
            grad_values.reshape(rows, count, extent, wide, width),
        ],
        axis=-1,
    )
    grad_blocks = jnp.zeros((rows + 2 * RADIUS, count, wide, 2 * width), jnp.float32)
    for down in range(extent):
        grad_blocks = grad_blocks.at[down : down + rows].add(grad_window[:, :, down])
    grad_ext = jnp.zeros((rows + 2 * RADIUS, span, 2 * width), jnp.float32)
    grad_ext = grad_ext.at[:, 0:wide].add(grad_blocks[:, 0])
    return (grad_query, grad_ext)


def fold_rims(grad_ext):
    rows = grad_ext.shape[0] - 2 * RADIUS
    columns = grad_ext.shape[1] - 2 * RADIUS
    left_rim = grad_ext[:, :RADIUS]
    right_rim = grad_ext[:, columns + RADIUS :]
    middle = grad_ext[:, RADIUS : columns + RADIUS]
    from_next = shifted(left_rim.astype(jnp.bfloat16), "col", -1).astype(left_rim.dtype)
    from_prev = shifted(right_rim.astype(jnp.bfloat16), "col", 1).astype(right_rim.dtype)
    middle = middle.at[:, columns - RADIUS :].add(from_next).at[:, :RADIUS].add(from_prev)
    top_rim = middle[:RADIUS]
    bottom_rim = middle[rows + RADIUS :]
    center = middle[RADIUS : rows + RADIUS]
    from_below = shifted(top_rim.astype(jnp.bfloat16), "row", -1).astype(top_rim.dtype)
    from_above = shifted(bottom_rim.astype(jnp.bfloat16), "row", 1).astype(bottom_rim.dtype)
    return center.at[rows - RADIUS :].add(from_below).at[:RADIUS].add(from_above)


def level_forward(tokens, gain, w_qkv):
    rows, columns, width = tokens.shape
    heads = width // HEAD
    values, scale, normed = norm_forward(tokens, gain)
    projected = jnp.dot(normed, w_qkv, preferred_element_type=jnp.float32).astype(jnp.bfloat16)
    query = projected[..., :width]
    kv_ext = extended_2(projected[..., width:], (("row", 0), ("col", 1)), RADIUS)
    attended, saved = attention_forward(query, kv_ext, key_validity(rows, columns), heads)
    return (attended, (values, scale, normed, attended, saved))


def level_backward(stored, upstream, gain, w_qkv, w_out):
    values, scale, normed, attended, saved = stored
    upstream_b = upstream.astype(jnp.bfloat16)
    grad_out = jnp.einsum("rcd,rce->de", attended, upstream_b, preferred_element_type=jnp.float32)
    grad_att = jnp.einsum(
        "rce,de->rcd", upstream_b, w_out, preferred_element_type=jnp.float32
    ).astype(jnp.bfloat16)
    grad_query, grad_ext = attention_backward(saved, grad_att)
    grad_kv = fold_rims(grad_ext)
    grad_proj = jnp.concatenate([grad_query, grad_kv], axis=-1).astype(jnp.bfloat16)
    grad_qkv = jnp.einsum("rcd,rce->de", normed, grad_proj, preferred_element_type=jnp.float32)
    grad_normed = jnp.einsum("rce,de->rcd", grad_proj, w_qkv, preferred_element_type=jnp.float32)
    grad_inputs, grad_gain = norm_backward(values, scale, gain, grad_normed)
    return (upstream + grad_inputs, grad_qkv, grad_out, grad_gain)


def merge_tokens(field):
    rows, columns, width = field.shape
    shaped = field.reshape(rows // 2, 2, columns // 2, 2, width).transpose(0, 2, 1, 3, 4)
    return shaped.reshape(rows // 2, columns // 2, 4 * width)


def split_tokens(field):
    rows, columns, width = field.shape
    shaped = field.reshape(rows, columns, 2, 2, width // 4).transpose(0, 2, 1, 3, 4)
    return shaped.reshape(2 * rows, 2 * columns, width // 4)


def per_device(
    tokens,
    gain_fine,
    qkv_fine,
    out_fine,
    w_merge,
    gain_coarse,
    qkv_coarse,
    out_coarse,
    grad_fine,
    grad_coarse,
):
    rows, columns, width_fine = tokens.shape
    attended_fine, stored_fine = level_forward(tokens, gain_fine, qkv_fine)
    fine_out = (
        stored_fine[0] + jnp.dot(attended_fine, out_fine, preferred_element_type=jnp.float32)
    ).astype(jnp.bfloat16)
    merged = merge_tokens(fine_out)
    coarse_in = jnp.dot(merged, w_merge, preferred_element_type=jnp.float32).astype(jnp.bfloat16)
    attended_coarse, stored_coarse = level_forward(coarse_in, gain_coarse, qkv_coarse)
    grad_coarse_in, grad_qkv1, grad_out1, grad_gain1 = level_backward(
        stored_coarse, grad_coarse.astype(jnp.float32), gain_coarse, qkv_coarse, out_coarse
    )
    coarse_b = grad_coarse_in.astype(jnp.bfloat16)
    grad_merge = jnp.einsum("rcm,rce->me", merged, coarse_b, preferred_element_type=jnp.float32)
    grad_merged = jnp.einsum("rce,me->rcm", coarse_b, w_merge, preferred_element_type=jnp.float32)
    grad_fine_total = grad_fine.astype(jnp.float32) + split_tokens(grad_merged)
    grad_tokens, grad_qkv0, grad_out0, grad_gain0 = level_backward(
        stored_fine, grad_fine_total, gain_fine, qkv_fine, out_fine
    )
    summed = lax.psum(
        (grad_qkv0, grad_out0, grad_gain0, grad_merge, grad_qkv1, grad_out1, grad_gain1),
        ("row", "col"),
    )
    grad_qkv0, grad_out0, grad_gain0, grad_merge, grad_qkv1, grad_out1, grad_gain1 = summed
    factor = 1.0 / math.sqrt(rows * lax.axis_size("row") * columns * lax.axis_size("col"))
    return (
        grad_tokens.astype(jnp.bfloat16),
        grad_gain0 * factor,
        (grad_qkv0 * factor).astype(jnp.bfloat16),
        (grad_out0 * factor).astype(jnp.bfloat16),
        (grad_merge * factor).astype(jnp.bfloat16),
        grad_gain1 * factor,
        (grad_qkv1 * factor).astype(jnp.bfloat16),
        (grad_out1 * factor).astype(jnp.bfloat16),
    )


def solution(mesh):
    in_specs = (
        P("row", "col", None),
        P(),
        P(),
        P(),
        P(),
        P(),
        P(),
        P(),
        P("row", "col", None),
        P("row", "col", None),
    )
    out_specs = (P("row", "col", None), P(), P(), P(), P(), P(), P(), P())
    return jax.shard_map(
        per_device, mesh=mesh, in_specs=in_specs, out_specs=out_specs, check_vma=False
    )
```

profile of v0, /device:TPU:1, one launch (start us, length us, event | category | flops | bytes accessed | tf_op | source)
XLA Modules:
  0.0 485.2 jit_solution(8791523386691594565)
XLA Ops:
  9.6 4.9 %collective-permute-start = (bf16[3,16,512]{2,1,0:T(8,128)(2,1)S(1)}, bf16[3,16,512]{2,1,0:T(8,128)(2,1)S(1)}, u32[]{:S(2)}, u32[]{:S(2)}) collective-permute-start(bf16[3,16,512]{2,1,0:T(8,128)(2,1)S(1)} %get-tuple-element.335), channel_id=1, source_target_pairs={{0,8},{8,16},{16,24},{24,32},{32,40},{40,48},{48,56},{56,64},{64,7... | collective-permute-start | bytes 147464 | tf_op jit(solution)/shard_map/ppermute | solution.py:28
  20.0 3.1 collective-permute-start.2
  25.2 2.8 collective-permute-done.3
  31.2 4.0 fusion.147
  35.2 2.9 copy.68
  38.1 3.5 copy.69
  47.6 4.7 collective-permute-start.4
  54.4 3.3 collective-permute-done.5
  57.8 3.1 collective-permute-start.6
  69.0 2.8 fusion.148
  73.9 2.8 copy.70
  83.1 3.6 copy.53
  88.6 3.6 copy.55
  92.3 2.7 reshape.1207
  100.4 5.9 %collective-permute-start.9 = (bf16[10,3,1024]{2,1,0:T(4,128)(2,1)}, bf16[10,3,1024]{2,1,0:T(4,128)(2,1)}, u32[]{:S(2)}, u32[]{:S(2)}) collective-permute-start(bf16[10,3,1024]{2,1,0:T(4,128)(2,1)} %get-tuple-element.329), channel_id=1, source_target_pairs={{0,1},{1,2},{2,3},{3,4},{4,5},{5,6},{6,7},{8,9},{9,10},{10,11},{11... | collective-permute-start | bytes 184328 | tf_op jit(solution)/shard_map/ppermute | solution.py:18
  119.0 4.0 collective-permute-start.11
  134.9 4.4 copy.62
  139.3 2.7 reshape.1220
  142.0 4.4 copy.64
  146.4 2.7 reshape.1221
  154.1 4.0 collective-permute-start.13
  162.9 5.3 %collective-permute-start.15 = (bf16[3,16,512]{2,1,0:T(8,128)(2,1)S(1)}, bf16[3,16,512]{2,1,0:T(8,128)(2,1)S(1)}, u32[]{:S(2)}, u32[]{:S(2)}) collective-permute-start(bf16[3,16,512]{2,1,0:T(8,128)(2,1)S(1)} %get-tuple-element.331), channel_id=1, source_target_pairs={{0,8},{8,16},{16,24},{24,32},{32,40},{40,48},{48,56},{56,64},{64,7... | collective-permute-start | bytes 147464 | tf_op jit(solution)/shard_map/ppermute | solution.py:18
  172.0 100.7 %all-reduce.2 = (f32[256]{0:T(256)S(1)}, f32[512]{0:T(512)S(1)}) all-reduce(f32[256]{0:T(256)S(1)} %get-tuple-element.312, f32[512]{0:T(512)S(1)} %get-tuple-element.314), channel_id=1, replica_groups=mesh['row'=32,'col'=8] {'row','col'}, use_global_device_ids=true, to_apply=%region_9.10 | all-reduce | flops 768 | bytes 6144 | tf_op jit(solution)/shard_map/psum | solution.py:225
  274.7 194.0 %all-reduce.6.cloned.1.call-done = (f32[256,768]{1,0:T(8,128)}, f32[256,256]{1,0:T(8,128)}, f32[1024,512]{1,0:T(8,128)}, f32[512,1536]{1,0:T(8,128)}, f32[512,512]{1,0:T(8,128)}) async-done(((f32[256,768]{1,0:T(8,128)}, f32[256,256]{1,0:T(8,128)}, f32[1024,512]{1,0:T(8,128)}, f32[512,1536]{1,0:T(8,128)}, f32[512,512]{1,0:T(8,128)}), (f32[256,768]{1,0:T(8,128)}, f32[256,256]{1,0:T(8,128)}, ...) | async-done | bytes 7340048 | tf_op jit(solution)/shard_map/psum | solution.py:225
  (260 shorter events, 93.9 us)
Async XLA Ops:
  7.2 40.0 %copy-start = (bf16[512,1536]{1,0:T(8,128)(2,1)S(1)}, bf16[512,1536]{1,0:T(8,128)(2,1)}, u32[]{:S(2)}) copy-start(bf16[512,1536]{1,0:T(8,128)(2,1)} %param.68) | copy-start | bytes 4718596
  7.2 461.5 %all-reduce.6.cloned.1.call-start = ((), (), s32[]{:S(2)}) async-start(), calls=%async_computation | async-start | bytes 14680064 | tf_op jit(solution)/shard_map/psum | solution.py:225
  9.6 9.4 %collective-permute-start = (bf16[3,16,512]{2,1,0:T(8,128)(2,1)S(1)}, bf16[3,16,512]{2,1,0:T(8,128)(2,1)S(1)}, u32[]{:S(2)}, u32[]{:S(2)}) collective-permute-start(bf16[3,16,512]{2,1,0:T(8,128)(2,1)S(1)} %get-tuple-element.335), channel_id=1, source_target_pairs={{0,8},{8,16},{16,24},{24,32},{32,40},{40,48},{48,56},{56,64},{64,7... | collective-permute-start | bytes 147464 | tf_op jit(solution)/shard_map/ppermute | solution.py:28
  14.6 5.4 %collective-permute-start.1 = (bf16[3,16,512]{2,1,0:T(8,128)(2,1)S(1)}, bf16[3,16,512]{2,1,0:T(8,128)(2,1)S(1)}, u32[]{:S(2)}, u32[]{:S(2)}) collective-permute-start(bf16[3,16,512]{2,1,0:T(8,128)(2,1)S(1)} %get-tuple-element.336), channel_id=1, source_target_pairs={{8,0},{16,8},{24,16},{32,24},{40,32},{48,40},{56,48},{64,56},{72,6... | collective-permute-start | bytes 147464 | tf_op jit(solution)/shard_map/ppermute | solution.py:29
  20.0 5.2 %collective-permute-start.2 = (bf16[14,3,512]{2,1,0:T(4,128)(2,1)S(1)}, bf16[14,3,512]{2,1,0:T(4,128)(2,1)S(1)}, u32[]{:S(2)}, u32[]{:S(2)}) collective-permute-start(bf16[14,3,512]{2,1,0:T(4,128)(2,1)S(1)} %get-tuple-element.333), channel_id=1, source_target_pairs={{0,1},{1,2},{2,3},{3,4},{4,5},{5,6},{6,7},{8,9},{9,10},{10,11},{11... | collective-permute-start | bytes 129032 | tf_op jit(solution)/shard_map/ppermute | solution.py:28
  23.1 4.9 %collective-permute-start.3 = (bf16[14,3,512]{2,1,0:T(4,128)(2,1)S(1)}, bf16[14,3,512]{2,1,0:T(4,128)(2,1)S(1)}, u32[]{:S(2)}, u32[]{:S(2)}) collective-permute-start(bf16[14,3,512]{2,1,0:T(4,128)(2,1)S(1)} %get-tuple-element.334), channel_id=1, source_target_pairs={{1,0},{2,1},{3,2},{4,3},{5,4},{6,5},{7,6},{9,8},{10,9},{11,10},{12... | collective-permute-start | bytes 129032 | tf_op jit(solution)/shard_map/ppermute | solution.py:29
  25.2 16.4 %copy-start.18 = (bf16[8,16,4,64]{3,2,1,0:T(4,128)(2,1)}, bf16[8,16,4,64]{3,2,1,0:T(4,128)(2,1)S(1)}, u32[]{:S(2)}) copy-start(bf16[8,16,4,64]{3,2,1,0:T(4,128)(2,1)S(1)} %reshape.1195) | copy-start | bytes 196612
  44.5 9.8 %copy-start.34 = (s32[98]{0:T(128)S(1)}, s32[98]{0:T(128)}, u32[]{:S(2)}) copy-start(s32[98]{0:T(128)} %sub.80) | copy-start | bytes 1180
  44.5 9.8 %copy-start.33 = (pred[4,1,7,14]{3,0,2,1:T(4,128)(4,1)S(1)}, pred[4,1,7,14]{3,0,2,1:T(4,128)(4,1)}, u32[]{:S(2)}) copy-start(pred[4,1,7,14]{3,0,2,1:T(4,128)(4,1)} %copy-done.32) | copy-start | bytes 1180
  44.9 12.9 %copy-start.23 = (bf16[4,8,2,2,256]{4,1,3,2,0:T(8,128)(2,1)}, bf16[4,8,2,2,256]{4,1,3,2,0:T(8,128)(2,1)S(1)}, u32[]{:S(2)}) copy-start(bf16[4,8,2,2,256]{4,1,3,2,0:T(8,128)(2,1)S(1)} %copy.44) | copy-start | bytes 196612
  44.9 18.1 %copy-start.28 = (bf16[4,8,512]{2,1,0:T(8,128)(2,1)S(1)}, bf16[4,8,512]{2,1,0:T(8,128)(2,1)}, u32[]{:S(2)}) copy-start(bf16[4,8,512]{2,1,0:T(8,128)(2,1)} %convolution_convert_fusion.8) | copy-start | bytes 98308
  47.6 6.8 %collective-permute-start.4 = (bf16[3,8,1024]{2,1,0:T(8,128)(2,1)S(1)}, bf16[3,8,1024]{2,1,0:T(8,128)(2,1)S(1)}, u32[]{:S(2)}, u32[]{:S(2)}) collective-permute-start(bf16[3,8,1024]{2,1,0:T(8,128)(2,1)S(1)} %get-tuple-element.341), channel_id=1, source_target_pairs={{0,8},{8,16},{16,24},{24,32},{32,40},{40,48},{48,56},{56,64},{64,7... | collective-permute-start | bytes 147464 | tf_op jit(solution)/shard_map/ppermute | solution.py:28
  52.3 5.4 %collective-permute-start.5 = (bf16[3,8,1024]{2,1,0:T(8,128)(2,1)S(1)}, bf16[3,8,1024]{2,1,0:T(8,128)(2,1)S(1)}, u32[]{:S(2)}, u32[]{:S(2)}) collective-permute-start(bf16[3,8,1024]{2,1,0:T(8,128)(2,1)S(1)} %get-tuple-element.342), channel_id=1, source_target_pairs={{8,0},{16,8},{24,16},{32,24},{40,32},{48,40},{56,48},{64,56},{72,6... | collective-permute-start | bytes 147464 | tf_op jit(solution)/shard_map/ppermute | solution.py:29
  57.8 6.7 %collective-permute-start.6 = (bf16[10,3,1024]{2,1,0:T(4,128)(2,1)S(1)}, bf16[10,3,1024]{2,1,0:T(4,128)(2,1)S(1)}, u32[]{:S(2)}, u32[]{:S(2)}) collective-permute-start(bf16[10,3,1024]{2,1,0:T(4,128)(2,1)S(1)} %get-tuple-element.339), channel_id=1, source_target_pairs={{0,1},{1,2},{2,3},{3,4},{4,5},{5,6},{6,7},{8,9},{9,10},{10,11},{11... | collective-permute-start | bytes 184328 | tf_op jit(solution)/shard_map/ppermute | solution.py:28
  61.0 5.2 %collective-permute-start.7 = (bf16[10,3,1024]{2,1,0:T(4,128)(2,1)S(1)}, bf16[10,3,1024]{2,1,0:T(4,128)(2,1)S(1)}, u32[]{:S(2)}, u32[]{:S(2)}) collective-permute-start(bf16[10,3,1024]{2,1,0:T(4,128)(2,1)S(1)} %get-tuple-element.340), channel_id=1, source_target_pairs={{1,0},{2,1},{3,2},{4,3},{5,4},{6,5},{7,6},{9,8},{10,9},{11,10},{12... | collective-permute-start | bytes 184328 | tf_op jit(solution)/shard_map/ppermute | solution.py:29
  97.6 18.1 %copy-start.9 = (bf16[4,1,98,1,8,64]{2,5,4,0,3,1:T(8,128)(2,1)S(1)}, bf16[4,1,98,1,8,64]{2,5,4,0,3,1:T(8,128)(2,1)}, u32[]{:S(2)}) copy-start(bf16[4,1,98,1,8,64]{2,5,4,0,3,1:T(8,128)(2,1)} %copy.70) | copy-start | bytes 1204228
  97.6 8.7 %collective-permute-start.8 = (bf16[10,3,1024]{2,1,0:T(4,128)(2,1)S(1)}, bf16[10,3,1024]{2,1,0:T(4,128)(2,1)S(1)}, u32[]{:S(2)}, u32[]{:S(2)}) collective-permute-start(bf16[10,3,1024]{2,1,0:T(4,128)(2,1)S(1)} %get-tuple-element.330), channel_id=1, source_target_pairs={{1,0},{2,1},{3,2},{4,3},{5,4},{6,5},{7,6},{9,8},{10,9},{11,10},{12... | collective-permute-start | bytes 184328 | tf_op jit(solution)/shard_map/ppermute | solution.py:18
  100.4 8.9 %collective-permute-start.9 = (bf16[10,3,1024]{2,1,0:T(4,128)(2,1)}, bf16[10,3,1024]{2,1,0:T(4,128)(2,1)}, u32[]{:S(2)}, u32[]{:S(2)}) collective-permute-start(bf16[10,3,1024]{2,1,0:T(4,128)(2,1)} %get-tuple-element.329), channel_id=1, source_target_pairs={{0,1},{1,2},{2,3},{3,4},{4,5},{5,6},{6,7},{8,9},{9,10},{10,11},{11... | collective-permute-start | bytes 184328 | tf_op jit(solution)/shard_map/ppermute | solution.py:18
  113.9 9.1 %collective-permute-start.10 = (bf16[3,8,1024]{2,1,0:T(8,128)(2,1)}, bf16[3,8,1024]{2,1,0:T(8,128)(2,1)}, u32[]{:S(2)}, u32[]{:S(2)}) collective-permute-start(bf16[3,8,1024]{2,1,0:T(8,128)(2,1)} %get-tuple-element.338), channel_id=1, source_target_pairs={{8,0},{16,8},{24,16},{32,24},{40,32},{48,40},{56,48},{64,56},{72,6... | collective-permute-start | bytes 147464 | tf_op jit(solution)/shard_map/ppermute | solution.py:18
  119.0 5.3 %collective-permute-start.11 = (bf16[3,8,1024]{2,1,0:T(8,128)(2,1)}, bf16[3,8,1024]{2,1,0:T(8,128)(2,1)S(1)}, u32[]{:S(2)}, u32[]{:S(2)}) collective-permute-start(bf16[3,8,1024]{2,1,0:T(8,128)(2,1)} %get-tuple-element.337), channel_id=1, source_target_pairs={{0,8},{8,16},{16,24},{24,32},{32,40},{40,48},{48,56},{56,64},{64,7... | collective-permute-start | bytes 147464 | tf_op jit(solution)/shard_map/ppermute | solution.py:18
  150.8 7.2 %collective-permute-start.12 = (bf16[14,3,512]{2,1,0:T(4,128)(2,1)S(1)}, bf16[14,3,512]{2,1,0:T(4,128)(2,1)S(1)}, u32[]{:S(2)}, u32[]{:S(2)}) collective-permute-start(bf16[14,3,512]{2,1,0:T(4,128)(2,1)S(1)} %get-tuple-element.328), channel_id=1, source_target_pairs={{1,0},{2,1},{3,2},{4,3},{5,4},{6,5},{7,6},{9,8},{10,9},{11,10},{12... | collective-permute-start | bytes 129032 | tf_op jit(solution)/shard_map/ppermute | solution.py:18
  154.1 5.2 %collective-permute-start.13 = (bf16[14,3,512]{2,1,0:T(4,128)(2,1)S(1)}, bf16[14,3,512]{2,1,0:T(4,128)(2,1)S(1)}, u32[]{:S(2)}, u32[]{:S(2)}) collective-permute-start(bf16[14,3,512]{2,1,0:T(4,128)(2,1)S(1)} %get-tuple-element.327), channel_id=1, source_target_pairs={{0,1},{1,2},{2,3},{3,4},{4,5},{5,6},{6,7},{8,9},{9,10},{10,11},{11... | collective-permute-start | bytes 129032 | tf_op jit(solution)/shard_map/ppermute | solution.py:18
  159.8 8.4 %collective-permute-start.14 = (bf16[3,16,512]{2,1,0:T(8,128)(2,1)S(1)}, bf16[3,16,512]{2,1,0:T(8,128)(2,1)S(1)}, u32[]{:S(2)}, u32[]{:S(2)}) collective-permute-start(bf16[3,16,512]{2,1,0:T(8,128)(2,1)S(1)} %get-tuple-element.332), channel_id=1, source_target_pairs={{8,0},{16,8},{24,16},{32,24},{40,32},{48,40},{56,48},{64,56},{72,6... | collective-permute-start | bytes 147464 | tf_op jit(solution)/shard_map/ppermute | solution.py:18
  162.9 6.4 %collective-permute-start.15 = (bf16[3,16,512]{2,1,0:T(8,128)(2,1)S(1)}, bf16[3,16,512]{2,1,0:T(8,128)(2,1)S(1)}, u32[]{:S(2)}, u32[]{:S(2)}) collective-permute-start(bf16[3,16,512]{2,1,0:T(8,128)(2,1)S(1)} %get-tuple-element.331), channel_id=1, source_target_pairs={{0,8},{8,16},{16,24},{24,32},{32,40},{40,48},{48,56},{56,64},{64,7... | collective-permute-start | bytes 147464 | tf_op jit(solution)/shard_map/ppermute | solution.py:18
  (28 other events, 105.3 us)
Sparse Core Ops, SparseCore 0:
  170.8 297.8 all-reduce.5
where the time goes:
time: 488 us; the launch traced here: 485 us
  waiting for transfers between devices  205 us (42%)
  blocking collectives  101 us (21%)
  local copies, waits for them, and re-layouts  67 us (14%)
  starting transfers between devices  48.4 us (10%)
  matrix products  30.2 us (6%)
  other arithmetic  18.5 us (4%)
  between operations  15.2 us (3%)
    psum x1, waiting for transfers between devices, per_device(): lax.psum((grad_qkv0, grad_out0, grad_gain0, grad_merge, grad_qkv1, grad_o...  194 us
    psum x1, blocking collectives, per_device(): lax.psum((grad_qkv0, grad_out0, grad_gain0, grad_merge, grad_qkv1, grad_o...  101 us
    ppermute x8, starting transfers between devices, shifted(): return lax.ppermute(x, axis, pairs)  25.9 us
    unnamed x102, local copies, waits for them, and re-layouts  16.1 us
    ppermute x4, starting transfers between devices, extended_2(): before = lax.ppermute(last, axis, up)  15.9 us
  transfers between devices with their start and end apart: 17, of which 8 were waited for; matrix products, arithmetic and copies ran while one was open for 4% of the time, Pallas kernels for 0%

commit v1 on v0

--- a/solution.py
+++ b/solution.py
@@ -190,6 +190,85 @@
     rows, columns, width = field.shape
     shaped = field.reshape(rows, columns, 2, 2, width // 4).transpose(0, 2, 1, 3, 4)
     return shaped.reshape(2 * rows, 2 * columns, width // 4)
+
+
+def flip(x, axis, bit):
+    return lax.ppermute(x, axis, [(i, i ^ bit) for i in range(lax.axis_size(axis))])
+
+
+def to_rows(field):
+    rows, columns = field.shape
+    if columns == 256:
+        return field.reshape(2, rows // 2, 256).transpose(1, 0, 2).reshape(rows // 2, 512)
+    if columns == 768:
+        return jnp.concatenate([field[:, :512], to_rows(field[:, 512:])], axis=0)
+    return jnp.concatenate([field[:, c : c + 512] for c in range(0, columns, 512)], axis=0)
+
+
+def from_rows(flat, rows, columns):
+    if columns == 256:
+        return flat.reshape(rows // 2, 2, 256).transpose(1, 0, 2).reshape(rows, 256)
+    if columns == 768:
+        return jnp.concatenate([flat[:rows], from_rows(flat[rows:], rows, 256)], axis=1)
+    parts = [flat[r : r + rows] for r in range(0, flat.shape[0], rows)]
+    return jnp.concatenate(parts, axis=1)
+
+
+def own_half(x, axis, bit):
+    half = x.shape[0] // 2
+    mine = (lax.axis_index(axis) // bit) % 2
+    keep = lax.dynamic_slice_in_dim(x, mine * half, half, axis=0)
+    send = lax.dynamic_slice_in_dim(x, (1 - mine) * half, half, axis=0)
+    return keep, send
+
+
+def add_b(a, b):
+    return (a.astype(jnp.float32) + b.astype(jnp.float32)).astype(jnp.bfloat16)
+
+
+def halve(x, small, axis, bit):
+    keep, send = own_half(x, axis, bit)
+    got = flip(jnp.concatenate([send, small], axis=0), axis, bit)
+    half = keep.shape[0]
+    return add_b(keep, got[:half]), add_b(small, got[half:])
+
+
+def rejoin(x, axis, bit):
+    mine = (lax.axis_index(axis) // bit) % 2
+    other = flip(x, axis, bit)
+    return jnp.where(mine == 0, jnp.concatenate([x, other]), jnp.concatenate([other, x]))
+
+
+def reduce_weights(grads, gains):
+    packed = jnp.concatenate([to_rows(g.astype(jnp.bfloat16)) for g in grads], axis=0)
+    lengths = [g.shape[0] for g in gains]
+    small = jnp.pad(jnp.concatenate(gains), (0, 16 * 512 - sum(lengths)))
+    small = small.reshape(16, 512).astype(jnp.bfloat16)
+    x, small = halve(packed, small, "row", 1)
+    count = lax.axis_size("col")
+    pieces = x.reshape(count, -1, 512)
+    pieces = jnp.concatenate([pieces, jnp.broadcast_to(small, (count, 16, 512))], axis=1)
+    pieces = lax.all_to_all(pieces, "col", 0, 0)
+    total = jnp.sum(pieces.astype(jnp.float32), axis=0).astype(jnp.bfloat16)
+    x, small = total[:-16], total[-16:]
+    x, small = halve(x, small, "row", 2)
+    x = jnp.concatenate([x, small], axis=0)
+    for bit in (4, 8, 16):
+        x = add_b(x, flip(x, "row", bit))
+    x, small = x[:-16], x[-16:]
+    x = rejoin(x, "row", 2)
+    x = lax.all_to_all(jnp.broadcast_to(x, (count,) + x.shape), "col", 0, 0)
+    x = rejoin(x.reshape(-1, 512), "row", 1)
+    out, place = [], 0
+    for g in grads:
+        rows = g.shape[0] * g.shape[1] // 512
+        out.append(from_rows(x[place : place + rows], *g.shape))
+        place += rows
+    small = small.astype(jnp.float32).reshape(-1)
+    ends = [0]
+    for n in lengths:
+        ends.append(ends[-1] + n)
+    return out, [small[a:b] for a, b in zip(ends, ends[1:])]
 
 
 def per_device(
@@ -222,11 +301,10 @@
     grad_tokens, grad_qkv0, grad_out0, grad_gain0 = level_backward(
         stored_fine, grad_fine_total, gain_fine, qkv_fine, out_fine
     )
-    summed = lax.psum(
-        (grad_qkv0, grad_out0, grad_gain0, grad_merge, grad_qkv1, grad_out1, grad_gain1),
-        ("row", "col"),
-    )
-    grad_qkv0, grad_out0, grad_gain0, grad_merge, grad_qkv1, grad_out1, grad_gain1 = summed
+    grads = (grad_qkv0, grad_out0, grad_merge, grad_qkv1, grad_out1)
+    summed, gains = reduce_weights(grads, (grad_gain0, grad_gain1))
+    grad_qkv0, grad_out0, grad_merge, grad_qkv1, grad_out1 = summed
+    grad_gain0, grad_gain1 = gains
     factor = 1.0 / math.sqrt(rows * lax.axis_size("row") * columns * lax.axis_size("col"))
     return (
         grad_tokens.astype(jnp.bfloat16),

time: 488 us -> 306 us (0.63)
  waiting for transfers between devices: 205 us -> 60 us
  blocking collectives: 101 us -> 20.5 us
  starting transfers between devices: 48.4 us -> 99.1 us
  between operations: 15.2 us -> 2.14 us
    psum x1 -> x0, waiting for transfers between devices: 194 us -> none  [per_device(): lax.psum((grad_qkv0, grad_out0, grad_gain0, grad_merge, grad_qkv1, grad_o...]
    psum x1 -> x0, blocking collectives: 101 us -> none  [per_device(): lax.psum((grad_qkv0, grad_out0, grad_gain0, grad_merge, grad_qkv1, grad_o...]
    ppermute x0 -> x7, starting transfers between devices: none -> 38 us  [flip(): lax.ppermute(x, axis, [(i, i ^ bit) for i in range(lax.axis_size(axis))])]
    all_to_all x0 -> x1, waiting for transfers between devices: none -> 25.7 us  [reduce_weights(): pieces = lax.all_to_all(pieces, 'col', 0, 0)]
    ppermute x0 -> x7, waiting for transfers between devices: none -> 22.9 us  [flip(): lax.ppermute(x, axis, [(i, i ^ bit) for i in range(lax.axis_size(axis))])]
    all_to_all x0 -> x1, blocking collectives: none -> 20.5 us  [reduce_weights(): x = lax.all_to_all(jnp.broadcast_to(x, (count,) + x.shape), 'col', 0, 0)]
    all_to_all x0 -> x1, starting transfers between devices: none -> 11.4 us  [reduce_weights(): pieces = lax.all_to_all(pieces, 'col', 0, 0)]
    convert_element_type x5 -> x7, other arithmetic: 8.64 us -> 2.17 us  [add_b(): return (a.astype(jnp.float32) + b.astype(jnp.float32)).astype(jnp.bfloat16)]
  transfers between devices with their start and end apart: 17 -> 24, of which waited for: 8 -> 16; matrix products, arithmetic and copies ran while one was open for 4% -> 6% of each run, Pallas kernels for 0% -> 0%
where the time goes in v1:
time: 306 us; the launch traced here: 304 us
  starting transfers between devices  99.1 us (32%)
  local copies, waits for them, and re-layouts  71.3 us (23%)
  waiting for transfers between devices  60 us (20%)
  matrix products  30.1 us (10%)
  other arithmetic  20.6 us (7%)
  blocking collectives  20.5 us (7%)
    ppermute x7, starting transfers between devices, flip(): lax.ppermute(x, axis, [(i, i ^ bit) for i in range(lax.axis_size(axis))])  38 us
    ppermute x8, starting transfers between devices, shifted(): return lax.ppermute(x, axis, pairs)  27.1 us
    all_to_all x1, waiting for transfers between devices, reduce_weights(): pieces = lax.all_to_all(pieces, 'col', 0, 0)  25.7 us
    ppermute x7, waiting for transfers between devices, flip(): lax.ppermute(x, axis, [(i, i ^ bit) for i in range(lax.axis_size(axis))])  22.9 us
    all_to_all x1, blocking collectives, reduce_weights(): x = lax.all_to_all(jnp.broadcast_to(x, (count,) + x.shape), 'col', 0, 0)  20.5 us
    unnamed x131, local copies, waits for them, and re-layouts  18.8 us
    ppermute x4, starting transfers between devices, extended_2(): before = lax.ppermute(last, axis, up)  15.9 us
    all_to_all x1, starting transfers between devices, reduce_weights(): pieces = lax.all_to_all(pieces, 'col', 0, 0)  11.4 us
  transfers between devices with their start and end apart: 24, of which 16 were waited for; matrix products, arithmetic and copies ran while one was open for 6% of the time, Pallas kernels for 0%

profile of v1, /device:TPU:1, one launch (start us, length us, event | category | flops | bytes accessed | tf_op | source)
XLA Modules:
  0.0 303.8 jit_solution(16560055627907898455)
XLA Ops:
  3.6 4.9 %collective-permute-start = (bf16[3,16,512]{2,1,0:T(8,128)(2,1)S(1)}, bf16[3,16,512]{2,1,0:T(8,128)(2,1)S(1)}, u32[]{:S(2)}, u32[]{:S(2)}) collective-permute-start(bf16[3,16,512]{2,1,0:T(8,128)(2,1)S(1)} %get-tuple-element.334), channel_id=1, source_target_pairs={{0,8},{8,16},{16,24},{24,32},{32,40},{40,48},{48,56},{56,64},{64,7... | collective-permute-start | bytes 147464 | tf_op jit(solution)/shard_map/ppermute | solution.py:28
  25.2 4.0 %fusion.156 = (bf16[8,1,154,1,4,64]{5,4,3,0,2,1:T(4,128)(2,1)}, bf16[8,1,154,1,4,64]{5,4,3,0,2,1:T(4,128)(2,1)}) fusion(bf16[8,1,154,2,4,64]{5,4,3,0,2,1:T(4,128)(2,1)} %reshape.1231), kind=kLoop, calls=%fused_computation.305 | loop fusion | bytes 2523136 | tf_op jit(solution)/shard_map/slice | solution.py:80
  32.1 3.5 %copy.77 = bf16[8,1,154,1,4,64]{2,5,4,0,3,1:T(8,128)(2,1)} copy(bf16[8,1,154,1,4,64]{5,4,3,0,2,1:T(4,128)(2,1)} %get-tuple-element.323) | data formatting | bytes 1261568
  41.2 4.7 %collective-permute-start.4 = (bf16[3,8,1024]{2,1,0:T(8,128)(2,1)S(1)}, bf16[3,8,1024]{2,1,0:T(8,128)(2,1)S(1)}, u32[]{:S(2)}, u32[]{:S(2)}) collective-permute-start(bf16[3,8,1024]{2,1,0:T(8,128)(2,1)S(1)} %get-tuple-element.340), channel_id=1, source_target_pairs={{0,8},{8,16},{16,24},{24,32},{32,40},{40,48},{48,56},{56,64},{64,7... | collective-permute-start | bytes 147464 | tf_op jit(solution)/shard_map/ppermute | solution.py:28
  48.0 3.3 %collective-permute-done.5 = bf16[3,8,1024]{2,1,0:T(8,128)(2,1)S(1)} collective-permute-done((bf16[3,8,1024]{2,1,0:T(8,128)(2,1)S(1)}, bf16[3,8,1024]{2,1,0:T(8,128)(2,1)S(1)}, u32[]{:S(2)}, u32[]{:S(2)}) %collective-permute-start.5) | collective-permute-done | bytes 49184 | tf_op jit(solution)/shard_map/ppermute | solution.py:29
  51.4 3.1 %collective-permute-start.6 = (bf16[10,3,1024]{2,1,0:T(4,128)(2,1)S(1)}, bf16[10,3,1024]{2,1,0:T(4,128)(2,1)S(1)}, u32[]{:S(2)}, u32[]{:S(2)}) collective-permute-start(bf16[10,3,1024]{2,1,0:T(4,128)(2,1)S(1)} %get-tuple-element.338), channel_id=1, source_target_pairs={{0,1},{1,2},{2,3},{3,4},{4,5},{5,6},{6,7},{8,9},{9,10},{10,11},{11... | collective-permute-start | bytes 184328 | tf_op jit(solution)/shard_map/ppermute | solution.py:28
  76.3 3.6 %copy.57 = f32[4,1,98,8,64]{4,3,0,2,1:T(8,128)} copy(f32[4,1,98,8,64]{2,4,3,0,1:T(8,128)} %convolution_bitcast_fusion.5) | data formatting | bytes 1605632 | tf_op jit(solution)/shard_map/rnhck,rnchd->rnkhd/transpose | solution.py:118
  82.6 3.6 %copy.59 = f32[4,1,98,8,64]{4,3,0,2,1:T(8,128)} copy(f32[4,1,98,8,64]{2,4,3,0,1:T(8,128)} %convolution_bitcast_fusion.4) | data formatting | bytes 1605632 | tf_op jit(solution)/shard_map/rnhck,rnchd->rnkhd/transpose | solution.py:121
  94.3 6.0 %collective-permute-start.9 = (bf16[10,3,1024]{2,1,0:T(4,128)(2,1)}, bf16[10,3,1024]{2,1,0:T(4,128)(2,1)}, u32[]{:S(2)}, u32[]{:S(2)}) collective-permute-start(bf16[10,3,1024]{2,1,0:T(4,128)(2,1)} %get-tuple-element.328), channel_id=1, source_target_pairs={{0,1},{1,2},{2,3},{3,4},{4,5},{5,6},{6,7},{8,9},{9,10},{10,11},{11... | collective-permute-start | bytes 184328 | tf_op jit(solution)/shard_map/ppermute | solution.py:18
  109.1 4.7 %collective-permute-start.11 = (bf16[3,8,1024]{2,1,0:T(8,128)(2,1)}, bf16[3,8,1024]{2,1,0:T(8,128)(2,1)S(1)}, u32[]{:S(2)}, u32[]{:S(2)}) collective-permute-start(bf16[3,8,1024]{2,1,0:T(8,128)(2,1)} %get-tuple-element.336), channel_id=1, source_target_pairs={{0,8},{8,16},{16,24},{24,32},{32,40},{40,48},{48,56},{56,64},{64,7... | collective-permute-start | bytes 147464 | tf_op jit(solution)/shard_map/ppermute | solution.py:18
  123.5 4.4 %copy.66 = f32[8,1,154,4,64]{4,3,0,2,1:T(4,128)} copy(f32[8,1,154,4,64]{2,4,3,0,1:T(8,128)} %convolution_bitcast_fusion.2) | data formatting | bytes 2523136 | tf_op jit(solution)/shard_map/rnhck,rnchd->rnkhd/transpose | solution.py:118
  130.6 4.4 %copy.68 = f32[8,1,154,4,64]{4,3,0,2,1:T(4,128)} copy(f32[8,1,154,4,64]{2,4,3,0,1:T(8,128)} %convolution_bitcast_fusion.1) | data formatting | bytes 2523136 | tf_op jit(solution)/shard_map/rnhck,rnchd->rnkhd/transpose | solution.py:121
  141.8 4.7 %collective-permute-start.13 = (bf16[14,3,512]{2,1,0:T(4,128)(2,1)S(1)}, bf16[14,3,512]{2,1,0:T(4,128)(2,1)S(1)}, u32[]{:S(2)}, u32[]{:S(2)}) collective-permute-start(bf16[14,3,512]{2,1,0:T(4,128)(2,1)S(1)} %get-tuple-element.326), channel_id=1, source_target_pairs={{0,1},{1,2},{2,3},{3,4},{4,5},{5,6},{6,7},{8,9},{9,10},{10,11},{11... | collective-permute-start | bytes 129032 | tf_op jit(solution)/shard_map/ppermute | solution.py:18
  153.4 5.0 %collective-permute-start.15 = (bf16[3,16,512]{2,1,0:T(8,128)(2,1)S(1)}, bf16[3,16,512]{2,1,0:T(8,128)(2,1)S(1)}, u32[]{:S(2)}, u32[]{:S(2)}) collective-permute-start(bf16[3,16,512]{2,1,0:T(8,128)(2,1)S(1)} %get-tuple-element.330), channel_id=1, source_target_pairs={{0,8},{8,16},{16,24},{24,32},{32,40},{40,48},{48,56},{56,64},{64,7... | collective-permute-start | bytes 147464 | tf_op jit(solution)/shard_map/ppermute | solution.py:18
  171.2 4.0 %collective-permute-done.16 = bf16[1808,512]{1,0:T(8,128)(2,1)S(1)} collective-permute-done((bf16[1808,512]{1,0:T(8,128)(2,1)}, bf16[1808,512]{1,0:T(8,128)(2,1)S(1)}, u32[]{:S(2)}, u32[]{:S(2)}) %collective-permute-start.16) | collective-permute-done | bytes 1851424 | tf_op jit(solution)/shard_map/ppermute | solution.py:196
  178.7 11.4 %all-to-all-start = ((bf16[8,240,512]{2,1,0:T(8,128)(2,1)}), bf16[8,240,512]{2,1,0:T(8,128)(2,1)S(1)}, u32[]{:S(2)}, u32[]{:S(2)}) async-start(bf16[8,240,512]{2,1,0:T(8,128)(2,1)} %pad_maximum_fusion), calls=%async_computation | async-start | bytes 3932160 | tf_op jit(solution)/shard_map/all_to_all | solution.py:251
  190.2 25.7 %all-to-all-done = bf16[8,240,512]{2,1,0:T(8,128)(2,1)S(1)} async-done(((bf16[8,240,512]{2,1,0:T(8,128)(2,1)}), bf16[8,240,512]{2,1,0:T(8,128)(2,1)S(1)}, u32[]{:S(2)}, u32[]{:S(2)}) %all-to-all-start) | async-done | bytes 1966112 | tf_op jit(solution)/shard_map/all_to_all | solution.py:251
  221.6 6.9 %collective-permute-start.18 = (bf16[128,512]{1,0:T(8,128)(2,1)S(1)}, bf16[128,512]{1,0:T(8,128)(2,1)S(1)}, u32[]{:S(2)}, u32[]{:S(2)}) collective-permute-start(bf16[128,512]{1,0:T(8,128)(2,1)S(1)} %pad_maximum_fusion.7), channel_id=1, source_target_pairs={{0,32},{8,40},{16,48},{24,56},{32,0},{40,8},{48,16},{56,24},{64,96... | collective-permute-start | bytes 393224 | tf_op jit(solution)/shard_map/ppermute | solution.py:196
  228.5 5.8 %collective-permute-done.18 = bf16[128,512]{1,0:T(8,128)(2,1)S(1)} collective-permute-done((bf16[128,512]{1,0:T(8,128)(2,1)S(1)}, bf16[128,512]{1,0:T(8,128)(2,1)S(1)}, u32[]{:S(2)}, u32[]{:S(2)}) %collective-permute-start.18) | collective-permute-done | bytes 131104 | tf_op jit(solution)/shard_map/ppermute | solution.py:196
  234.4 11.1 %collective-permute-start.19 = (bf16[128,512]{1,0:T(8,128)(2,1)S(1)}, bf16[128,512]{1,0:T(8,128)(2,1)S(1)}, u32[]{:S(2)}, u32[]{:S(2)}) collective-permute-start(bf16[128,512]{1,0:T(8,128)(2,1)S(1)} %add_convert_fusion.3), channel_id=1, source_target_pairs={{0,64},{8,72},{16,80},{24,88},{32,96},{40,104},{48,112},{56,120},{... | collective-permute-start | bytes 393224 | tf_op jit(solution)/shard_map/ppermute | solution.py:196
  247.9 10.1 %collective-permute-start.20 = (bf16[128,512]{1,0:T(8,128)(2,1)S(1)}, bf16[128,512]{1,0:T(8,128)(2,1)S(1)}, u32[]{:S(2)}, u32[]{:S(2)}) collective-permute-start(bf16[128,512]{1,0:T(8,128)(2,1)S(1)} %add_convert_fusion.2), channel_id=1, source_target_pairs={{0,128},{8,136},{16,144},{24,152},{32,160},{40,168},{48,176},{56,1... | collective-permute-start | bytes 393224 | tf_op jit(solution)/shard_map/ppermute | solution.py:196
  260.5 3.6 %collective-permute-done.21 = bf16[112,512]{1,0:T(8,128)(2,1)S(1)} collective-permute-done((bf16[112,512]{1,0:T(8,128)(2,1)S(1)}, bf16[112,512]{1,0:T(8,128)(2,1)S(1)}, u32[]{:S(2)}, u32[]{:S(2)}) %collective-permute-start.21) | collective-permute-done | bytes 114720 | tf_op jit(solution)/shard_map/ppermute | solution.py:196
  264.4 20.5 %all_to_all.10 = bf16[8,224,512]{2,1,0:T(8,128)(2,1)S(1)} all-to-all(bf16[8,224,512]{2,1,0:T(8,128)(2,1)S(1)} %broadcast_in_dim.33), channel_id=1, replica_groups=mesh['row'=32,'col'=8] {'col'}, dimensions={0} | all-to-all | bytes 3670016 | tf_op jit(solution)/shard_map/all_to_all | solution.py:260
  284.9 7.8 %collective-permute-start.22 = (bf16[1792,512]{1,0:T(8,128)(2,1)S(1)}, bf16[1792,512]{1,0:T(8,128)(2,1)}, u32[]{:S(2)}, u32[]{:S(2)}) collective-permute-start(bf16[1792,512]{1,0:T(8,128)(2,1)S(1)} %bitcast.379), channel_id=1, source_target_pairs={{0,8},{8,0},{16,24},{24,16},{32,40},{40,32},{48,56},{56,48},{64,72... | collective-permute-start | bytes 5505032 | tf_op jit(solution)/shard_map/ppermute | solution.py:196
  (334 shorter events, 134.6 us)
Async XLA Ops:
  3.6 9.4 %collective-permute-start = (bf16[3,16,512]{2,1,0:T(8,128)(2,1)S(1)}, bf16[3,16,512]{2,1,0:T(8,128)(2,1)S(1)}, u32[]{:S(2)}, u32[]{:S(2)}) collective-permute-start(bf16[3,16,512]{2,1,0:T(8,128)(2,1)S(1)} %get-tuple-element.334), channel_id=1, source_target_pairs={{0,8},{8,16},{16,24},{24,32},{32,40},{40,48},{48,56},{56,64},{64,7... | collective-permute-start | bytes 147464 | tf_op jit(solution)/shard_map/ppermute | solution.py:28
  8.6 5.4 %collective-permute-start.1 = (bf16[3,16,512]{2,1,0:T(8,128)(2,1)S(1)}, bf16[3,16,512]{2,1,0:T(8,128)(2,1)S(1)}, u32[]{:S(2)}, u32[]{:S(2)}) collective-permute-start(bf16[3,16,512]{2,1,0:T(8,128)(2,1)S(1)} %get-tuple-element.335), channel_id=1, source_target_pairs={{8,0},{16,8},{24,16},{32,24},{40,32},{48,40},{56,48},{64,56},{72,6... | collective-permute-start | bytes 147464 | tf_op jit(solution)/shard_map/ppermute | solution.py:29
  14.0 5.2 %collective-permute-start.2 = (bf16[14,3,512]{2,1,0:T(4,128)(2,1)S(1)}, bf16[14,3,512]{2,1,0:T(4,128)(2,1)S(1)}, u32[]{:S(2)}, u32[]{:S(2)}) collective-permute-start(bf16[14,3,512]{2,1,0:T(4,128)(2,1)S(1)} %get-tuple-element.332), channel_id=1, source_target_pairs={{0,1},{1,2},{2,3},{3,4},{4,5},{5,6},{6,7},{8,9},{9,10},{10,11},{11... | collective-permute-start | bytes 129032 | tf_op jit(solution)/shard_map/ppermute | solution.py:28
  17.2 4.9 %collective-permute-start.3 = (bf16[14,3,512]{2,1,0:T(4,128)(2,1)S(1)}, bf16[14,3,512]{2,1,0:T(4,128)(2,1)S(1)}, u32[]{:S(2)}, u32[]{:S(2)}) collective-permute-start(bf16[14,3,512]{2,1,0:T(4,128)(2,1)S(1)} %get-tuple-element.333), channel_id=1, source_target_pairs={{1,0},{2,1},{3,2},{4,3},{5,4},{6,5},{7,6},{9,8},{10,9},{11,10},{12... | collective-permute-start | bytes 129032 | tf_op jit(solution)/shard_map/ppermute | solution.py:29
  41.2 6.8 %collective-permute-start.4 = (bf16[3,8,1024]{2,1,0:T(8,128)(2,1)S(1)}, bf16[3,8,1024]{2,1,0:T(8,128)(2,1)S(1)}, u32[]{:S(2)}, u32[]{:S(2)}) collective-permute-start(bf16[3,8,1024]{2,1,0:T(8,128)(2,1)S(1)} %get-tuple-element.340), channel_id=1, source_target_pairs={{0,8},{8,16},{16,24},{24,32},{32,40},{40,48},{48,56},{56,64},{64,7... | collective-permute-start | bytes 147464 | tf_op jit(solution)/shard_map/ppermute | solution.py:28
  45.9 5.4 %collective-permute-start.5 = (bf16[3,8,1024]{2,1,0:T(8,128)(2,1)S(1)}, bf16[3,8,1024]{2,1,0:T(8,128)(2,1)S(1)}, u32[]{:S(2)}, u32[]{:S(2)}) collective-permute-start(bf16[3,8,1024]{2,1,0:T(8,128)(2,1)S(1)} %get-tuple-element.341), channel_id=1, source_target_pairs={{8,0},{16,8},{24,16},{32,24},{40,32},{48,40},{56,48},{64,56},{72,6... | collective-permute-start | bytes 147464 | tf_op jit(solution)/shard_map/ppermute | solution.py:29
  51.4 6.7 %collective-permute-start.6 = (bf16[10,3,1024]{2,1,0:T(4,128)(2,1)S(1)}, bf16[10,3,1024]{2,1,0:T(4,128)(2,1)S(1)}, u32[]{:S(2)}, u32[]{:S(2)}) collective-permute-start(bf16[10,3,1024]{2,1,0:T(4,128)(2,1)S(1)} %get-tuple-element.338), channel_id=1, source_target_pairs={{0,1},{1,2},{2,3},{3,4},{4,5},{5,6},{6,7},{8,9},{9,10},{10,11},{11... | collective-permute-start | bytes 184328 | tf_op jit(solution)/shard_map/ppermute | solution.py:28
  54.6 5.2 %collective-permute-start.7 = (bf16[10,3,1024]{2,1,0:T(4,128)(2,1)S(1)}, bf16[10,3,1024]{2,1,0:T(4,128)(2,1)S(1)}, u32[]{:S(2)}, u32[]{:S(2)}) collective-permute-start(bf16[10,3,1024]{2,1,0:T(4,128)(2,1)S(1)} %get-tuple-element.339), channel_id=1, source_target_pairs={{1,0},{2,1},{3,2},{4,3},{5,4},{6,5},{7,6},{9,8},{10,9},{11,10},{12... | collective-permute-start | bytes 184328 | tf_op jit(solution)/shard_map/ppermute | solution.py:29
  91.9 8.3 %collective-permute-start.8 = (bf16[10,3,1024]{2,1,0:T(4,128)(2,1)S(1)}, bf16[10,3,1024]{2,1,0:T(4,128)(2,1)S(1)}, u32[]{:S(2)}, u32[]{:S(2)}) collective-permute-start(bf16[10,3,1024]{2,1,0:T(4,128)(2,1)S(1)} %get-tuple-element.329), channel_id=1, source_target_pairs={{1,0},{2,1},{3,2},{4,3},{5,4},{6,5},{7,6},{9,8},{10,9},{11,10},{12... | collective-permute-start | bytes 184328 | tf_op jit(solution)/shard_map/ppermute | solution.py:18
  94.3 7.2 %collective-permute-start.9 = (bf16[10,3,1024]{2,1,0:T(4,128)(2,1)}, bf16[10,3,1024]{2,1,0:T(4,128)(2,1)}, u32[]{:S(2)}, u32[]{:S(2)}) collective-permute-start(bf16[10,3,1024]{2,1,0:T(4,128)(2,1)} %get-tuple-element.328), channel_id=1, source_target_pairs={{0,1},{1,2},{2,3},{3,4},{4,5},{5,6},{6,7},{8,9},{9,10},{10,11},{11... | collective-permute-start | bytes 184328 | tf_op jit(solution)/shard_map/ppermute | solution.py:18
  104.0 9.9 %collective-permute-start.10 = (bf16[3,8,1024]{2,1,0:T(8,128)(2,1)}, bf16[3,8,1024]{2,1,0:T(8,128)(2,1)}, u32[]{:S(2)}, u32[]{:S(2)}) collective-permute-start(bf16[3,8,1024]{2,1,0:T(8,128)(2,1)} %get-tuple-element.337), channel_id=1, source_target_pairs={{8,0},{16,8},{24,16},{32,24},{40,32},{48,40},{56,48},{64,56},{72,6... | collective-permute-start | bytes 147464 | tf_op jit(solution)/shard_map/ppermute | solution.py:18
  109.1 6.0 %collective-permute-start.11 = (bf16[3,8,1024]{2,1,0:T(8,128)(2,1)}, bf16[3,8,1024]{2,1,0:T(8,128)(2,1)S(1)}, u32[]{:S(2)}, u32[]{:S(2)}) collective-permute-start(bf16[3,8,1024]{2,1,0:T(8,128)(2,1)} %get-tuple-element.336), channel_id=1, source_target_pairs={{0,8},{8,16},{16,24},{24,32},{32,40},{40,48},{48,56},{56,64},{64,7... | collective-permute-start | bytes 147464 | tf_op jit(solution)/shard_map/ppermute | solution.py:18
  139.4 7.1 %collective-permute-start.12 = (bf16[14,3,512]{2,1,0:T(4,128)(2,1)S(1)}, bf16[14,3,512]{2,1,0:T(4,128)(2,1)S(1)}, u32[]{:S(2)}, u32[]{:S(2)}) collective-permute-start(bf16[14,3,512]{2,1,0:T(4,128)(2,1)S(1)} %get-tuple-element.327), channel_id=1, source_target_pairs={{1,0},{2,1},{3,2},{4,3},{5,4},{6,5},{7,6},{9,8},{10,9},{11,10},{12... | collective-permute-start | bytes 129032 | tf_op jit(solution)/shard_map/ppermute | solution.py:18
  141.8 6.0 %collective-permute-start.13 = (bf16[14,3,512]{2,1,0:T(4,128)(2,1)S(1)}, bf16[14,3,512]{2,1,0:T(4,128)(2,1)S(1)}, u32[]{:S(2)}, u32[]{:S(2)}) collective-permute-start(bf16[14,3,512]{2,1,0:T(4,128)(2,1)S(1)} %get-tuple-element.326), channel_id=1, source_target_pairs={{0,1},{1,2},{2,3},{3,4},{4,5},{5,6},{6,7},{8,9},{9,10},{10,11},{11... | collective-permute-start | bytes 129032 | tf_op jit(solution)/shard_map/ppermute | solution.py:18
  148.3 10.1 %collective-permute-start.14 = (bf16[3,16,512]{2,1,0:T(8,128)(2,1)S(1)}, bf16[3,16,512]{2,1,0:T(8,128)(2,1)S(1)}, u32[]{:S(2)}, u32[]{:S(2)}) collective-permute-start(bf16[3,16,512]{2,1,0:T(8,128)(2,1)S(1)} %get-tuple-element.331), channel_id=1, source_target_pairs={{8,0},{16,8},{24,16},{32,24},{40,32},{48,40},{56,48},{64,56},{72,6... | collective-permute-start | bytes 147464 | tf_op jit(solution)/shard_map/ppermute | solution.py:18
  153.4 6.2 %collective-permute-start.15 = (bf16[3,16,512]{2,1,0:T(8,128)(2,1)S(1)}, bf16[3,16,512]{2,1,0:T(8,128)(2,1)S(1)}, u32[]{:S(2)}, u32[]{:S(2)}) collective-permute-start(bf16[3,16,512]{2,1,0:T(8,128)(2,1)S(1)} %get-tuple-element.330), channel_id=1, source_target_pairs={{0,8},{8,16},{16,24},{24,32},{32,40},{40,48},{48,56},{56,64},{64,7... | collective-permute-start | bytes 147464 | tf_op jit(solution)/shard_map/ppermute | solution.py:18
  171.2 4.0 %collective-permute-start.16 = (bf16[1808,512]{1,0:T(8,128)(2,1)}, bf16[1808,512]{1,0:T(8,128)(2,1)S(1)}, u32[]{:S(2)}, u32[]{:S(2)}) collective-permute-start(bf16[1808,512]{1,0:T(8,128)(2,1)} %pad_maximum_fusion.1), channel_id=1, source_target_pairs={{0,8},{8,0},{16,24},{24,16},{32,40},{40,32},{48,56},{56,48},{64,72... | collective-permute-start | bytes 5554184 | tf_op jit(solution)/shard_map/ppermute | solution.py:196
  178.7 37.2 %all-to-all-start = ((bf16[8,240,512]{2,1,0:T(8,128)(2,1)}), bf16[8,240,512]{2,1,0:T(8,128)(2,1)S(1)}, u32[]{:S(2)}, u32[]{:S(2)}) async-start(bf16[8,240,512]{2,1,0:T(8,128)(2,1)} %pad_maximum_fusion), calls=%async_computation | async-start | bytes 3932160 | tf_op jit(solution)/shard_map/all_to_all | solution.py:251
  216.3 5.2 %collective-permute-start.17 = (bf16[128,512]{1,0:T(8,128)(2,1)S(1)}, bf16[128,512]{1,0:T(8,128)(2,1)S(1)}, u32[]{:S(2)}, u32[]{:S(2)}) collective-permute-start(bf16[128,512]{1,0:T(8,128)(2,1)S(1)} %pad_maximum_fusion.6), channel_id=1, source_target_pairs={{0,16},{8,24},{16,0},{24,8},{32,48},{40,56},{48,32},{56,40},{64,80... | collective-permute-start | bytes 393224 | tf_op jit(solution)/shard_map/ppermute | solution.py:196
  221.6 12.7 %collective-permute-start.18 = (bf16[128,512]{1,0:T(8,128)(2,1)S(1)}, bf16[128,512]{1,0:T(8,128)(2,1)S(1)}, u32[]{:S(2)}, u32[]{:S(2)}) collective-permute-start(bf16[128,512]{1,0:T(8,128)(2,1)S(1)} %pad_maximum_fusion.7), channel_id=1, source_target_pairs={{0,32},{8,40},{16,48},{24,56},{32,0},{40,8},{48,16},{56,24},{64,96... | collective-permute-start | bytes 393224 | tf_op jit(solution)/shard_map/ppermute | solution.py:196
  234.4 13.5 %collective-permute-start.19 = (bf16[128,512]{1,0:T(8,128)(2,1)S(1)}, bf16[128,512]{1,0:T(8,128)(2,1)S(1)}, u32[]{:S(2)}, u32[]{:S(2)}) collective-permute-start(bf16[128,512]{1,0:T(8,128)(2,1)S(1)} %add_convert_fusion.3), channel_id=1, source_target_pairs={{0,64},{8,72},{16,80},{24,88},{32,96},{40,104},{48,112},{56,120},{... | collective-permute-start | bytes 393224 | tf_op jit(solution)/shard_map/ppermute | solution.py:196
  247.9 12.4 %collective-permute-start.20 = (bf16[128,512]{1,0:T(8,128)(2,1)S(1)}, bf16[128,512]{1,0:T(8,128)(2,1)S(1)}, u32[]{:S(2)}, u32[]{:S(2)}) collective-permute-start(bf16[128,512]{1,0:T(8,128)(2,1)S(1)} %add_convert_fusion.2), channel_id=1, source_target_pairs={{0,128},{8,136},{16,144},{24,152},{32,160},{40,168},{48,176},{56,1... | collective-permute-start | bytes 393224 | tf_op jit(solution)/shard_map/ppermute | solution.py:196
  260.4 3.7 %collective-permute-start.21 = (bf16[112,512]{1,0:T(8,128)(2,1)S(1)}, bf16[112,512]{1,0:T(8,128)(2,1)S(1)}, u32[]{:S(2)}, u32[]{:S(2)}) collective-permute-start(bf16[112,512]{1,0:T(8,128)(2,1)S(1)} %slice.1172), channel_id=1, source_target_pairs={{0,16},{8,24},{16,0},{24,8},{32,48},{40,56},{48,32},{56,40},{64,80... | collective-permute-start | bytes 344072 | tf_op jit(solution)/shard_map/ppermute | solution.py:196
  284.9 11.3 %collective-permute-start.22 = (bf16[1792,512]{1,0:T(8,128)(2,1)S(1)}, bf16[1792,512]{1,0:T(8,128)(2,1)}, u32[]{:S(2)}, u32[]{:S(2)}) collective-permute-start(bf16[1792,512]{1,0:T(8,128)(2,1)S(1)} %bitcast.379), channel_id=1, source_target_pairs={{0,8},{8,0},{16,24},{24,16},{32,40},{40,32},{48,56},{56,48},{64,72... | collective-permute-start | bytes 5505032 | tf_op jit(solution)/shard_map/ppermute | solution.py:196
  (46 other events, 412.5 us)

commit v2 on v0

v2 whole, which is shorter than its diff:
```python
import functools
import math

import jax
import jax.numpy as jnp
import numpy as np
from jax import lax
from jax.experimental import pallas as pl
from jax.experimental.pallas import tpu as pltpu
from jax.sharding import PartitionSpec as P

HEAD = 64
RADIUS = 3
PAIR = 2 * HEAD
NEG = -1e30
norm_eps = 1e-06
f32 = jnp.float32
bf16 = jnp.bfloat16


def shifted(x, axis, by):
    count = lax.axis_size(axis)
    pairs = [(i, i + by) for i in range(count) if 0 <= i + by < count]
    return lax.ppermute(x, axis, pairs)


def flip(x, axis, bit):
    return lax.ppermute(x, axis, [(i, i ^ bit) for i in range(lax.axis_size(axis))])


def add_b(a, b):
    return (a.astype(f32) + b.astype(f32)).astype(bf16)


def grid_piece(rows, columns, length=None):
    piece = [(r, c) for r in rows for c in columns]
    return piece + [None] * ((length or len(piece)) - len(piece))


def merge_order(rows, columns):
    return [
        (2 * a + rp, 2 * b + cp)
        for rp in (0, 1)
        for cp in (0, 1)
        for a in range(rows // 2)
        for b in range(columns // 2)
    ]


def fine_keys(rows, columns):
    reach = RADIUS
    tall = range(-reach, rows + reach)
    side = -(-len(tall) * reach // 16) * 16
    return [
        merge_order(rows, columns),
        grid_piece(range(-reach, 0), range(columns)),
        grid_piece(range(rows, rows + reach), range(columns)),
        grid_piece(tall, range(-reach, 0), side),
        grid_piece(tall, range(columns, columns + reach), side),
    ]


def coarse_keys(rows, columns):
    reach = 2 * RADIUS
    tall = range(-reach, rows + reach)
    return [
        grid_piece(range(rows), range(columns)),
        grid_piece(range(-rows, 0), range(columns)),
        grid_piece(range(rows, 2 * rows), range(columns)),
        grid_piece(range(-reach, -rows), range(columns)),
        grid_piece(range(2 * rows, rows + reach), range(columns)),
        grid_piece(tall, range(-reach, 0)),
        grid_piece(tall, range(columns, columns + reach)),
    ]


def coarse_queries(rows, columns):
    reach = RADIUS
    tall = range(-reach, rows + reach)
    side = -(-len(tall) * reach // 8) * 8
    return [
        grid_piece(range(rows), range(columns)),
        grid_piece(range(-reach, 0), range(columns)),
        grid_piece(range(rows, rows + reach), range(columns)),
        grid_piece(tall, range(-reach, 0), side),
        grid_piece(tall, range(columns, columns + reach), side),
    ]


def joined(pieces):
    return [place for piece in pieces for place in piece]


def band_bias(queries, keys):
    bias = np.full((len(queries), len(keys)), NEG, np.float32)
    for i, q in enumerate(queries):
        for j, k in enumerate(keys):
            if q is None:
                inside = j == 0
            else:
                inside = k is not None and max(abs(q[0] - k[0]), abs(q[1] - k[1])) <= RADIUS
            if inside:
                bias[i, j] = 0.0
    return bias


def key_bias(keys, rows, columns):
    row = np.array([k[0] if k else 0 for k in keys], np.int32)
    col = np.array([k[1] if k else 0 for k in keys], np.int32)
    row_ids = lax.axis_index("row") * rows + row
    col_ids = lax.axis_index("col") * columns + col
    ok = (row_ids >= 0) & (row_ids < rows * lax.axis_size("row"))
    ok &= (col_ids >= 0) & (col_ids < columns * lax.axis_size("col"))
    return jnp.where(ok, 0.0, NEG).astype(f32)[None, :]


def one_hot(targets, sources):
    place = {s: j for j, s in enumerate(sources) if s is not None}
    matrix = np.zeros((len(targets), len(sources)), np.float32)
    for i, t in enumerate(targets):
        if t is not None and t in place:
            matrix[i, place[t]] = 1.0
    return matrix.astype(jnp.bfloat16)


def dot(a, b):
    return jnp.dot(a, b, preferred_element_type=f32)


def dot_nt(a, b):
    return lax.dot_general(a, b, (((1,), (1,)), ((), ())), preferred_element_type=f32)


def dot_tn(a, b):
    return lax.dot_general(a, b, (((0,), (0,)), ((), ())), preferred_element_type=f32)


def norm_forward(x, gain):
    values = x.astype(f32)
    scale = lax.rsqrt(jnp.mean(values * values, axis=-1, keepdims=True) + norm_eps)
    return values, scale, (values * scale * gain).astype(bf16)


def norm_backward(values, scale, gain, upstream):
    gain_part = jnp.sum(upstream * values * scale, axis=0, keepdims=True)
    weighted = upstream * gain
    inner = jnp.mean(weighted * values, axis=-1, keepdims=True)
    return weighted * scale - values * (scale * scale * scale) * inner, gain_part


def head_masks():
    lane = lax.broadcasted_iota(jnp.int32, (1, PAIR), 1)
    return [(lane < HEAD).astype(f32), (lane >= HEAD).astype(f32)]


def masked(x, mask):
    return (x.astype(f32) * mask).astype(bf16)


def probabilities(query, keys, bias):
    weights = jnp.exp(dot_nt(query, keys) * (1.0 / math.sqrt(HEAD)) + bias)
    return weights / jnp.sum(weights, axis=-1, keepdims=True)


def score_gradient(prob, dprob):
    total = jnp.sum(prob * dprob, axis=-1, keepdims=True)
    return (prob * (dprob - total) * (1.0 / math.sqrt(HEAD))).astype(bf16)


def lanes(x, place):
    return x[:, place * PAIR : (place + 1) * PAIR]


def fine_forward_kernel(
    tok, top, bottom, left, right, perm, gain, w_qkv, w_out, w_merge, band, valid,
    merged_out, coarse_out, normed_out, proj_out, kv_out, att_out,
):
    width = tok.shape[1]
    own = dot(perm[...], tok[...]).astype(bf16)
    field = jnp.concatenate([own, top[...], bottom[...], left[...], right[...]], axis=0)
    _, _, normed = norm_forward(field, gain[...])
    count = own.shape[0]
    normed_out[...] = normed[:count]
    query = dot(normed[:count], w_qkv[:, :width]).astype(bf16)
    kv = dot(normed, w_qkv[:, width:]).astype(bf16)
    proj_out[...] = query
    kv_out[...] = kv
    bias = band[...] + valid[...]
    masks = head_masks()
    parts = []
    for p in range(width // PAIR):
        keys, vals, q = lanes(kv, p), lanes(kv, width // PAIR + p), lanes(query, p)
        total = None
        for mask in masks:
            prob = probabilities(masked(q, mask), keys, bias)
            part = dot(prob.astype(bf16), vals) * mask
            total = part if total is None else total + part
        parts.append(total.astype(bf16))
    attended = jnp.concatenate(parts, axis=1)
    att_out[...] = attended
    fine = (own.astype(f32) + dot(attended, w_out[...])).astype(bf16)
    quarter = count // 4
    acc = None
    for p in range(4):
        block = fine[p * quarter : (p + 1) * quarter]
        merged_out[:, p * width : (p + 1) * width] = block
        part = dot(block, w_merge[p * width : (p + 1) * width, :])
        acc = part if acc is None else acc + part
    coarse_out[...] = acc.astype(bf16)


def coarse_kernel(
    field, upstream, merged, pick, gain, w_qkv, w_out, w_merge, band, valid, parity,
    keep_out, send_out, gain_out, grad_merged_out,
):
    own, width = merged.shape[0], field.shape[1]
    pairs = width // PAIR
    values, scale, normed = norm_forward(field[...], gain[...])
    kv = dot(normed, w_qkv[:, width:]).astype(bf16)
    picked = dot(pick[...], normed).astype(bf16)
    query = dot(picked, w_qkv[:, :width]).astype(bf16)
    u_b = upstream[...]
    grad_att = dot_nt(u_b, w_out[...]).astype(bf16)
    bias = band[...] + valid[...]
    masks = head_masks()
    att, gq, gk, gv = [], [], [], []
    for p in range(pairs):
        keys, vals = lanes(kv, p), lanes(kv, pairs + p)
        q, g = lanes(query, p), lanes(grad_att, p)
        sums = None
        for mask in masks:
            qm, gm = masked(q, mask), masked(g, mask)
            prob = probabilities(qm, keys, bias)
            prob_b = prob.astype(bf16)
            dscore = score_gradient(prob, dot_nt(gm, vals))
            new = (
                dot(prob_b[:own], vals) * mask,
                dot(dscore[:own], keys) * mask,
                dot_tn(dscore[:, :PAIR], qm)[:own],
                dot_tn(prob_b[:, :PAIR], gm)[:own],
            )
            sums = new if sums is None else tuple(a + b for a, b in zip(sums, new))
        for group, part in zip((att, gq, gk, gv), sums):
            group.append(part.astype(bf16))
    attended = jnp.concatenate(att, axis=1)
    grad_proj = jnp.concatenate(gq + gk + gv, axis=1)
    grad_normed = dot_nt(grad_proj, w_qkv[...])
    grad_in, gain_part = norm_backward(values[:own], scale[:own], gain[...], grad_normed)
    gain_out[...] = gain_part
    c_b = (u_b[:own].astype(f32) + grad_in).astype(bf16)
    grad_merged_out[...] = dot_nt(c_b, w_merge[...])
    first = parity[0] == 0
    place = 0
    for x in (merged[...], normed[:own], attended):
        half = x.shape[1] // 2
        low, high = x[:, :half].astype(f32), x[:, half:].astype(f32)
        keep_out[:, place : place + half] = jnp.where(first, low, high).astype(bf16)
        send_out[:, place : place + half] = jnp.where(first, high, low).astype(bf16)
        place += half
    for g in (c_b, grad_proj, u_b[:own]):
        send_out[:, place : place + g.shape[1]] = g
        place += g.shape[1]


def coarse_weights_kernel(factor, keep, sent, got, out):
    half = keep.shape[1]
    width = half // 2
    x = jnp.concatenate([keep[...], got[:, :half]], axis=0)
    g = jnp.concatenate([sent[:, half:], got[:, half:]], axis=0)
    wide = x.shape[1] // 2
    narrow = wide // 2
    cols = width
    out[:wide] = (dot_tn(x[:, :wide], g[:, :cols]) * factor).astype(bf16)
    normed, attended = x[:, wide : wide + narrow], x[:, wide + narrow :]
    for b in range(3):
        rows = slice(wide + b * narrow, wide + (b + 1) * narrow)
        out[rows] = (dot_tn(normed, g[:, (b + 1) * cols : (b + 2) * cols]) * factor).astype(bf16)
    out[wide + 3 * narrow :] = (dot_tn(attended, g[:, 4 * cols :]) * factor).astype(bf16)


def fine_backward_kernel(
    grad_fine, grad_merged, perm, query_in, kv_in, w_out, band, valid,
    up_out, gq_out, mid_out, left_out, right_out,
):
    width = grad_fine.shape[1]
    pairs = width // PAIR
    total = jnp.concatenate([grad_merged[:, p * width : (p + 1) * width] for p in range(4)], axis=0)
    up = dot(perm[...], grad_fine[...]) + total
    up_out[...] = up
    grad_att = dot_nt(up.astype(bf16), w_out[...]).astype(bf16)
    query, kv = query_in[...], kv_in[...]
    bias = band[...] + valid[...]
    masks = head_masks()
    middle, side = mid_out.shape[0], left_out.shape[0]
    for p in range(pairs):
        keys, vals = lanes(kv, p), lanes(kv, pairs + p)
        q, g = lanes(query, p), lanes(grad_att, p)
        sums = None
        for mask in masks:
            qm, gm = masked(q, mask), masked(g, mask)
            prob = probabilities(qm, keys, bias)
            dscore = score_gradient(prob, dot_nt(gm, vals))
            new = (
                dot(dscore, keys) * mask,
                dot_tn(dscore, qm),
                dot_tn(prob.astype(bf16), gm),
            )
            sums = new if sums is None else tuple(a + b for a, b in zip(sums, new))
        gq_out[:, p * PAIR : (p + 1) * PAIR] = sums[0].astype(bf16)
        for part, at in ((sums[1], p), (sums[2], pairs + p)):
            where = slice(at * PAIR, (at + 1) * PAIR)
            mid_out[:, where] = part[:middle]
            left_out[:, where] = part[middle : middle + side].astype(bf16)
            right_out[:, where] = part[middle + side :].astype(bf16)


def fine_fold_kernel(mid, from_left, from_right, place_left, place_right, own_out, top_out, bottom_out):
    folded = mid[...] + dot(place_left[...], from_left[...]) + dot(place_right[...], from_right[...])
    own, rim = own_out.shape[0], top_out.shape[0]
    own_out[...] = folded[:own]
    top_out[...] = folded[own : own + rim].astype(bf16)
    bottom_out[...] = folded[own + rim :].astype(bf16)


def fine_last_kernel(
    own, from_above, from_below, place_above, place_below, gq, up, tok, perm, normed, att, gain, w_qkv, parity,
    grad_out, gain_out, keep_out, send_out,
):
    width = tok.shape[1]
    kv = own[...] + dot(place_above[...], from_above[...]) + dot(place_below[...], from_below[...])
    grad_proj = jnp.concatenate([gq[...], kv.astype(bf16)], axis=1)
    values, scale, _ = norm_forward(dot(perm[...], tok[...]), gain[...])
    grad_in, gain_part = norm_backward(values, scale, gain[...], dot_nt(grad_proj, w_qkv[...]))
    gain_out[...] = gain_part
    grad_out[...] = dot_tn(perm[...], (up[...] + grad_in).astype(bf16)).astype(bf16)
    first = parity[0] == 0
    half = width // 2
    place = 0
    for x in (normed[...], att[...]):
        low, high = x[:, :half].astype(f32), x[:, half:].astype(f32)
        keep_out[:, place : place + half] = jnp.where(first, low, high).astype(bf16)
        send_out[:, place : place + half] = jnp.where(first, high, low).astype(bf16)
        place += half
    send_out[:, place : place + 3 * width] = grad_proj
    send_out[:, place + 3 * width :] = up[...].astype(bf16)


def fine_weights_kernel(factor, keep, sent, got, out):
    wide = keep.shape[1]
    half = wide // 2
    x = jnp.concatenate([keep[...], got[:, :wide]], axis=0)
    g = jnp.concatenate([sent[:, wide:], got[:, wide:]], axis=0)
    qkv = (dot_tn(x[:, :half], g[:, : 3 * wide]) * factor).astype(bf16)
    last = (dot_tn(x[:, half:], g[:, 3 * wide :]) * factor).astype(bf16)
    out[:half] = qkv[:, : 2 * wide]
    out[half:, :wide] = qkv[:, 2 * wide :]
    out[half:, wide:] = last


def call(kernel, outs, flops=1 << 28):
    vmem = pl.BlockSpec(memory_space=pltpu.VMEM)
    smem = pl.BlockSpec(memory_space=pltpu.SMEM)

    def run(*args):
        return pl.pallas_call(
            kernel,
            out_shape=[jax.ShapeDtypeStruct(shape, dtype) for shape, dtype in outs],
            in_specs=[smem if a.ndim == 1 else vmem for a in args],
            out_specs=[vmem] * len(outs),
            compiler_params=pltpu.CompilerParams(vmem_limit_bytes=48 << 20),
            cost_estimate=pl.CostEstimate(flops=flops, bytes_accessed=4 << 20, transcendentals=0),
        )(*args)

    return run


def scatter_over_columns(x):
    count = lax.axis_size("col")
    pieces = lax.all_to_all(x, "col", 0, 0)
    return jnp.sum(pieces.reshape(count, -1, x.shape[-1]).astype(f32), axis=0).astype(bf16)


def reduce_rows(x, small):
    half = x.shape[0] // 2
    mine = (lax.axis_index("row") // 2) % 2
    keep = lax.dynamic_slice_in_dim(x, mine * half, half, axis=0)
    send = lax.dynamic_slice_in_dim(x, (1 - mine) * half, half, axis=0)
    got = flip(jnp.concatenate([send, small], axis=0), "row", 2)
    x = add_b(jnp.concatenate([keep, small], axis=0), got)
    bit = 4
    while bit < lax.axis_size("row"):
        x = add_b(x, flip(x, "row", bit))
        bit *= 2
    x, small = x[:half], x[half:]
    other = flip(x, "row", 2)
    return jnp.where(mine == 0, jnp.concatenate([x, other]), jnp.concatenate([other, x])), small


def per_device(
    tokens,
    gain_fine,
    qkv_fine,
    out_fine,
    w_merge,
    gain_coarse,
    qkv_coarse,
    out_coarse,
    grad_fine,
    grad_coarse,
):
    rows, columns, width = tokens.shape
    crows, ccolumns, cwidth = grad_coarse.shape
    reach = RADIUS
    count, ccount = rows * columns, crows * ccolumns
    parity = (lax.axis_index("row") % 2).astype(jnp.int32)[None]
    factor = 1.0 / math.sqrt(rows * lax.axis_size("row") * columns * lax.axis_size("col"))
    tok = tokens.reshape(count, width)
    gc = grad_coarse.reshape(ccount, cwidth)

    rim, crim = reach * columns, reach * ccolumns

    def pack(a, b):
        return jnp.concatenate([a, b[:, :width], b[:, width:]], axis=0)

    def unpack(x, n):
        m = n + (x.shape[0] - n) // 2
        return x[:n], jnp.concatenate([x[n:m], x[m:]], axis=1)

    top, ctop = unpack(shifted(pack(tok[-rim:], gc[-crim:]), "row", 1), rim)
    bottom, cbottom = unpack(shifted(pack(tok[:rim], gc[:crim]), "row", -1), rim)
    tall = jnp.concatenate([top, tok, bottom], axis=0).reshape(-1, columns, width)
    ctall = jnp.concatenate([ctop, gc, cbottom], axis=0).reshape(-1, ccolumns, cwidth)
    keys0 = fine_keys(rows, columns)
    side = len(keys0[3])
    queries1 = coarse_queries(crows, ccolumns)
    cside = len(queries1[3])

    def edge(x, start, stop, length):
        flat = x[:, start:stop].reshape(-1, x.shape[-1])
        return jnp.pad(flat, ((0, length - flat.shape[0]), (0, 0)))

    left, cleft = unpack(
        shifted(
            pack(
                edge(tall, columns - reach, columns, side),
                edge(ctall, ccolumns - reach, ccolumns, cside),
            ),
            "col",
            1,
        ),
        side,
    )
    right, cright = unpack(
        shifted(pack(edge(tall, 0, reach, side), edge(ctall, 0, reach, cside)), "col", -1), side
    )
    upstream1 = jnp.concatenate([gc, ctop, cbottom, cleft, cright], axis=0)

    flat0 = joined(keys0)
    own0 = keys0[0]
    natural = grid_piece(range(rows), range(columns))
    perm = jnp.asarray(one_hot(own0, natural))
    band0 = jnp.asarray(band_bias(own0, flat0))
    valid0 = key_bias(flat0, rows, columns)
    gain0, gain1 = gain_fine[None, :], gain_coarse[None, :]
    merged, coarse_in, normed0, query0, kv0, att0 = call(
        fine_forward_kernel,
        [
            ((ccount, 4 * width), bf16),
            ((ccount, cwidth), bf16),
            ((count, width), bf16),
            ((count, width), bf16),
            ((len(flat0), 2 * width), bf16),
            ((count, width), bf16),
        ],
    )(tok, top, bottom, left, right, perm, gain0, qkv_fine, out_fine, w_merge, band0, valid0)

    wide = 2 * reach
    part = (wide - crows) * ccolumns
    up1 = shifted(coarse_in, "row", 1)
    up2 = shifted(coarse_in[-part:], "row", 2)
    down1 = shifted(coarse_in, "row", -1)
    down2 = shifted(coarse_in[:part], "row", -2)
    tall = jnp.concatenate([up2, up1, coarse_in, down1, down2], axis=0)
    tall = tall.reshape(-1, ccolumns, cwidth)
    cl = shifted(tall[:, ccolumns - wide :].reshape(-1, cwidth), "col", 1)
    cr = shifted(tall[:, :wide].reshape(-1, cwidth), "col", -1)
    field = jnp.concatenate([coarse_in, up1, down1, up2, down2, cl, cr], axis=0)

    flat1, ask1 = joined(coarse_keys(crows, ccolumns)), joined(queries1)
    band1 = jnp.asarray(band_bias(ask1, flat1))
    valid1 = key_bias(flat1, crows, ccolumns)
    pick = jnp.asarray(one_hot(ask1, flat1))
    kept = (4 * width + 2 * cwidth) // 2
    keep1, send1, gain_part1, grad_merged = call(
        coarse_kernel,
        [
            ((ccount, kept), bf16),
            ((ccount, kept + 5 * cwidth), bf16),
            ((1, cwidth), f32),
            ((ccount, 4 * width), f32),
        ],
    )(field, upstream1, merged, pick, gain1, qkv_coarse, out_coarse, w_merge, band1, valid1, parity)
    (packed1,) = call(
        functools.partial(coarse_weights_kernel, factor),
        [((2 * width + 4 * cwidth // 2, cwidth), bf16)],
    )(keep1, send1, flip(send1, "row", 1))
    cols = lax.axis_size("col")
    sums1 = scatter_over_columns(packed1.reshape(cols, -1, cwidth))

    rims = len(keys0[1])
    middle = count + 2 * rims
    up0, gq0, mid, left_rim, right_rim = call(
        fine_backward_kernel,
        [
            ((count, width), f32),
            ((count, width), bf16),
            ((middle, 2 * width), f32),
            ((side, 2 * width), bf16),
            ((side, 2 * width), bf16),
        ],
    )(grad_fine.reshape(count, width), grad_merged, perm, query0, kv0, out_fine, band0, valid0)
    from_right = shifted(left_rim, "col", -1)
    from_left = shifted(right_rim, "col", 1)
    mids = joined(keys0[:3])

    def moved(piece, dr, dc):
        return [None if p is None else (p[0] + dr, p[1] + dc) for p in piece]

    own, top_rim, bottom_rim = call(
        fine_fold_kernel,
        [((count, 2 * width), f32), ((rims, 2 * width), bf16), ((rims, 2 * width), bf16)],
    )(
        mid,
        from_left,
        from_right,
        jnp.asarray(one_hot(mids, moved(keys0[4], 0, -columns))),
        jnp.asarray(one_hot(mids, moved(keys0[3], 0, columns))),
    )
    from_below = shifted(top_rim, "row", -1)
    from_above = shifted(bottom_rim, "row", 1)
    grad_tokens, gain_part0, keep0, send0 = call(
        fine_last_kernel,
        [
            ((count, width), bf16),
            ((1, width), f32),
            ((count, width), bf16),
            ((count, 5 * width), bf16),
        ],
    )(
        own,
        from_above,
        from_below,
        jnp.asarray(one_hot(own0, moved(keys0[2], -rows, 0))),
        jnp.asarray(one_hot(own0, moved(keys0[1], rows, 0))),
        gq0,
        up0,
        tok,
        perm,
        normed0,
        att0,
        gain0,
        qkv_fine,
        parity,
    )
    (packed0,) = call(
        functools.partial(fine_weights_kernel, factor), [((width, 2 * width), bf16)]
    )(keep0, send0, flip(send0, "row", 1))
    gains = jnp.concatenate([gain_part0[0], gain_part1[0]]) * factor
    gains = jnp.pad(gains, (0, 16 * cwidth - gains.shape[0])).reshape(16, cwidth).astype(bf16)
    pieces0 = packed0.reshape(cols, -1, cwidth)
    pieces0 = jnp.concatenate([pieces0, jnp.broadcast_to(gains, (cols, 16, cwidth))], axis=1)
    sums0 = scatter_over_columns(pieces0)

    n1, n0 = sums1.shape[0], sums0.shape[0] - 16
    x, small = reduce_rows(jnp.concatenate([sums1, sums0[:n0]], axis=0), sums0[n0:])
    x = lax.all_to_all(jnp.broadcast_to(x, (cols,) + x.shape), "col", 0, 0).reshape(-1, cwidth)
    got = flip(jnp.concatenate([x, small], axis=0), "row", 1)
    other = got[: x.shape[0]]
    gains = (small.astype(f32) + got[x.shape[0] :].astype(f32)).reshape(-1)
    first = parity[0] == 0

    def halves(start, stop, place, length):
        def take(a):
            block = a.reshape(cols, n1 + n0, cwidth)[:, start:stop].reshape(-1, cwidth)
            return block[place : place + length]

        mine, others = take(x), take(other)
        return jnp.where(first, mine, others), jnp.where(first, others, mine)

    def whole(start, stop, place, length):
        return jnp.concatenate(halves(start, stop, place, length), axis=0)

    half = cwidth // 2
    grad_merge = whole(0, n1, 0, 2 * width)
    blocks = [whole(0, n1, 2 * width + b * half, half) for b in range(4)]
    low = whole(n1, n1 + n0, 0, width // 2)
    high = whole(n1, n1 + n0, width // 2, width // 2)
    return (
        grad_tokens.reshape(rows, columns, width),
        gains[:width],
        jnp.concatenate([low, high[:, :width]], axis=1),
        high[:, width:],
        grad_merge,
        gains[width : width + cwidth],
        jnp.concatenate(blocks[:3], axis=1),
        blocks[3],
    )


def solution(mesh):
    in_specs = (
        P("row", "col", None),
        P(),
        P(),
        P(),
        P(),
        P(),
        P(),
        P(),
        P("row", "col", None),
        P("row", "col", None),
    )
    out_specs = (P("row", "col", None), P(), P(), P(), P(), P(), P(), P())
    return jax.shard_map(
        per_device, mesh=mesh, in_specs=in_specs, out_specs=out_specs, check_vma=False
    )
```

time: 488 us -> 221 us (0.45)
  waiting for transfers between devices: 205 us -> 91.1 us
  blocking collectives: 101 us -> 0 us
  local copies, waits for them, and re-layouts: 67 us -> 19.3 us
  starting transfers between devices: 48.4 us -> 81.7 us
  matrix products: 30.2 us -> 0 us
  between operations: 15.2 us -> 1.59 us
  Pallas kernels: 0 us -> 12.8 us
  other arithmetic: 18.5 us -> 12.2 us
    psum x1 -> x0, waiting for transfers between devices: 194 us -> none  [per_device(): lax.psum((grad_qkv0, grad_out0, grad_gain0, grad_merge, grad_qkv1, grad_o...]
    psum x1 -> x0, blocking collectives: 101 us -> none  [per_device(): lax.psum((grad_qkv0, grad_out0, grad_gain0, grad_merge, grad_qkv1, grad_o...]
    all_to_all x0 -> x3, waiting for transfers between devices: none -> 50.8 us  [the longest x2 26.7 us: scatter_over_columns(): pieces = lax.all_to_all(x, 'col', 0, 0)]
    dot_general x24 -> x0, matrix products: 27.2 us -> none  [the longest x2 4.16 us: attention_backward(): jnp.einsum('rnhck,rnchd->rnkhd', dscore, query_heads, preferred_element_t...]
    ppermute x8 -> x14, starting transfers between devices: 25.9 us -> 43.6 us  [shifted(): return lax.ppermute(x, axis, pairs)]
    transpose x7 -> x0, local copies, waits for them, and re-layouts: 16.9 us -> none  [the longest x2 8 us: attention_backward(): jnp.einsum('rnhck,rnchd->rnkhd', probability_b, grad_heads, preferred_ele...]
    ppermute x8 -> x14, waiting for transfers between devices: 2.41 us -> 17.1 us  [shifted(): return lax.ppermute(x, axis, pairs)]
    ppermute x8, waiting for transfers between devices: 8.71 us -> 23.2 us  [flip(): lax.ppermute(x, axis, [(i, i ^ bit) for i in range(lax.axis_size(axis))])]
  transfers between devices with their start and end apart: 17 -> 25, of which waited for: 8 -> 17; matrix products, arithmetic and copies ran while one was open for 4% -> 3% of each run, Pallas kernels for 0% -> 1%
where the time goes in v2:
time: 221 us; the launch traced here: 219 us
  waiting for transfers between devices  91.1 us (41%)
  starting transfers between devices  81.7 us (37%)
  local copies, waits for them, and re-layouts  19.3 us (9%)
  Pallas kernels  12.8 us (6%)
  other arithmetic  12.2 us (6%)
    ppermute x14, starting transfers between devices, shifted(): return lax.ppermute(x, axis, pairs)  43.6 us
    all_to_all x2, waiting for transfers between devices, scatter_over_columns(): pieces = lax.all_to_all(x, 'col', 0, 0)  26.7 us
    ppermute x8, starting transfers between devices, flip(): lax.ppermute(x, axis, [(i, i ^ bit) for i in range(lax.axis_size(axis))])  25 us
    all_to_all x1, waiting for transfers between devices, per_device(): lax.all_to_all(jnp.broadcast_to(x, (cols,) + x.shape), 'col', 0, 0)  24 us
    ppermute x8, waiting for transfers between devices, flip(): lax.ppermute(x, axis, [(i, i ^ bit) for i in range(lax.axis_size(axis))])  23.2 us
    ppermute x14, waiting for transfers between devices, shifted(): return lax.ppermute(x, axis, pairs)  17.1 us
    pallas_call x7, Pallas kernels, run(): pl.pallas_call(kernel, out_shape=[jax.ShapeDtypeStruct(shape, dtype) for...  12.8 us
    all_to_all x2, starting transfers between devices, scatter_over_columns(): pieces = lax.all_to_all(x, 'col', 0, 0)  9.42 us
  transfers between devices with their start and end apart: 25, of which 17 were waited for; matrix products, arithmetic and copies ran while one was open for 3% of the time, Pallas kernels for 1%

profile of v2, /device:TPU:1, one launch (start us, length us, event | category | flops | bytes accessed | tf_op | source)
XLA Modules:
  0.0 218.6 jit_solution(1801863763505051598)
XLA Ops:
  2.4 4.9 %collective-permute-start = (bf16[96,256]{1,0:T(8,128)(2,1)S(1)}, bf16[96,256]{1,0:T(8,128)(2,1)S(1)}, u32[]{:S(2)}, u32[]{:S(2)}) collective-permute-start(bf16[96,256]{1,0:T(8,128)(2,1)S(1)} %pad_maximum_fusion.9), channel_id=1, source_target_pairs={{0,8},{8,16},{16,24},{24,32},{32,40},{40,48},{48,56},{56,64},{64,7... | collective-permute-start | bytes 147464 | tf_op jit(solution)/shard_map/ppermute | solution.py:24
  14.5 3.1 %collective-permute-start.2 = (bf16[112,256]{1,0:T(8,128)(2,1)S(1)}, bf16[112,256]{1,0:T(8,128)(2,1)S(1)}, u32[]{:S(2)}, u32[]{:S(2)}) collective-permute-start(bf16[112,256]{1,0:T(8,128)(2,1)S(1)} %fusion.6), channel_id=1, source_target_pairs={{0,1},{1,2},{2,3},{3,4},{4,5},{5,6},{6,7},{8,9},{9,10},{10,11},{11... | collective-permute-start | bytes 172040 | tf_op jit(solution)/shard_map/ppermute | solution.py:24
  19.1 3.6 %collective-permute-done.3 = bf16[112,256]{1,0:T(8,128)(2,1)S(1)} collective-permute-done((bf16[112,256]{1,0:T(8,128)(2,1)S(1)}, bf16[112,256]{1,0:T(8,128)(2,1)S(1)}, u32[]{:S(2)}, u32[]{:S(2)}) %collective-permute-start.3) | collective-permute-done | bytes 57376 | tf_op jit(solution)/shard_map/ppermute | solution.py:24
  25.7 4.7 %collective-permute-start.4 = (bf16[32,512]{1,0:T(8,128)(2,1)S(1)}, bf16[32,512]{1,0:T(8,128)(2,1)S(1)}, u32[]{:S(2)}, u32[]{:S(2)}) collective-permute-start(bf16[32,512]{1,0:T(8,128)(2,1)S(1)} %get-tuple-element.30), channel_id=1, source_target_pairs={{0,8},{8,16},{16,24},{24,32},{32,40},{40,48},{48,56},{56,64},{64,7... | collective-permute-start | bytes 98312 | tf_op jit(solution)/shard_map/ppermute | solution.py:24
  32.4 3.5 %collective-permute-start.6 = (bf16[16,512]{1,0:T(8,128)(2,1)S(1)}, bf16[16,512]{1,0:T(8,128)(2,1)S(1)}, u32[]{:S(2)}, u32[]{:S(2)}) collective-permute-start(bf16[16,512]{1,0:T(8,128)(2,1)S(1)} %get-tuple-element.91), channel_id=1, source_target_pairs={{0,16},{8,24},{16,32},{24,40},{32,48},{40,56},{48,64},{56,72},{64,... | collective-permute-start | bytes 49160 | tf_op jit(solution)/shard_map/ppermute | solution.py:24
  42.7 3.8 %collective-permute-start.8 = (bf16[96,512]{1,0:T(8,128)(2,1)}, bf16[96,512]{1,0:T(8,128)(2,1)}, u32[]{:S(2)}, u32[]{:S(2)}) collective-permute-start(bf16[96,512]{1,0:T(8,128)(2,1)} %reshape.122), channel_id=1, source_target_pairs={{0,1},{1,2},{2,3},{3,4},{4,5},{5,6},{6,7},{8,9},{9,10},{10,11},{11... | collective-permute-start | bytes 294920 | tf_op jit(solution)/shard_map/ppermute | solution.py:24
  51.0 3.4 %collective-permute-done.9 = bf16[96,512]{1,0:T(8,128)(2,1)S(1)} collective-permute-done((bf16[96,512]{1,0:T(8,128)(2,1)}, bf16[96,512]{1,0:T(8,128)(2,1)S(1)}, u32[]{:S(2)}, u32[]{:S(2)}) %collective-permute-start.9) | collective-permute-done | bytes 98336 | tf_op jit(solution)/shard_map/ppermute | solution.py:24
  59.6 5.3 %shard_map.270 = (bf16[32,1024]{1,0:T(8,128)(2,1)S(1)}, bf16[32,3584]{1,0:T(8,128)(2,1)S(1)}, f32[1,512]{1,0:T(1,128)S(1)}, f32[32,1024]{1,0:T(8,128)S(1)}) custom-call(bf16[320,512]{1,0:T(8,128)(2,1)S(1)} %constant_dynamic-update-slice_fusion.5.field, bf16[144,512]{1,0:T(8,128)(2,1)S(1)} %constant_dynamic-update-slice_fusion.12.upstream, ...), custom_call_target="tpu_custom_call" | custom-call | flops 268435456 | bytes 4194304 | tf_op jit(solution)/shard_map/pallas_call | solution.py:365
  67.0 4.1 %collective-permute-start.10 = (bf16[48,512]{1,0:T(8,128)(2,1)S(1)}, bf16[48,512]{1,0:T(8,128)(2,1)S(1)}, u32[]{:S(2)}, u32[]{:S(2)}) collective-permute-start(bf16[48,512]{1,0:T(8,128)(2,1)S(1)} %get-tuple-element.36), channel_id=1, source_target_pairs={{0,1},{1,2},{2,3},{3,4},{4,5},{5,6},{6,7},{8,9},{9,10},{10,11},{11... | collective-permute-start | bytes 147464 | tf_op jit(solution)/shard_map/ppermute | solution.py:24
  72.4 3.5 %collective-permute-done.11.from_right = bf16[48,512]{1,0:T(8,128)(2,1)S(1)} collective-permute-done((bf16[48,512]{1,0:T(8,128)(2,1)S(1)}, bf16[48,512]{1,0:T(8,128)(2,1)S(1)}, u32[]{:S(2)}, u32[]{:S(2)}) %collective-permute-start.11) | collective-permute-done | bytes 49184 | tf_op jit(solution)/shard_map/ppermute | solution.py:24
  76.2 8.6 %collective-permute-start.12 = (bf16[48,512]{1,0:T(8,128)(2,1)S(1)}, bf16[48,512]{1,0:T(8,128)(2,1)S(1)}, u32[]{:S(2)}, u32[]{:S(2)}) collective-permute-start(bf16[48,512]{1,0:T(8,128)(2,1)S(1)} %get-tuple-element.39), channel_id=1, source_target_pairs={{0,8},{8,16},{16,24},{24,32},{32,40},{40,48},{48,56},{56,64},{64,7... | collective-permute-start | bytes 147464 | tf_op jit(solution)/shard_map/ppermute | solution.py:24
  86.7 3.5 %collective-permute-done.13.from_below = bf16[48,512]{1,0:T(8,128)(2,1)S(1)} collective-permute-done((bf16[48,512]{1,0:T(8,128)(2,1)S(1)}, bf16[48,512]{1,0:T(8,128)(2,1)S(1)}, u32[]{:S(2)}, u32[]{:S(2)}) %collective-permute-start.13) | collective-permute-done | bytes 49184 | tf_op jit(solution)/shard_map/ppermute | solution.py:24
  94.1 5.8 %all-to-all-start.1 = ((bf16[8,48,512]{2,1,0:T(8,128)(2,1)}), bf16[8,48,512]{2,1,0:T(8,128)(2,1)S(1)}, u32[]{:S(2)}, u32[]{:S(2)}) async-start(bf16[8,48,512]{2,1,0:T(8,128)(2,1)} %pad_maximum_fusion.3), calls=%async_computation.1 | async-start | bytes 786432 | tf_op jit(solution)/shard_map/all_to_all | solution.py:379
  103.4 5.5 %all-to-all-done.1 = bf16[8,48,512]{2,1,0:T(8,128)(2,1)S(1)} async-done(((bf16[8,48,512]{2,1,0:T(8,128)(2,1)}), bf16[8,48,512]{2,1,0:T(8,128)(2,1)S(1)}, u32[]{:S(2)}, u32[]{:S(2)}) %all-to-all-start.1) | async-done | bytes 393248 | tf_op jit(solution)/shard_map/all_to_all | solution.py:379
  108.8 3.6 %all-to-all-start = ((bf16[8,192,512]{2,1,0:T(8,128)(2,1)}), bf16[8,192,512]{2,1,0:T(8,128)(2,1)S(1)}, u32[]{:S(2)}, u32[]{:S(2)}) async-start(bf16[8,192,512]{2,1,0:T(8,128)(2,1)} %bitcast.14), calls=%async_computation | async-start | bytes 3145728 | tf_op jit(solution)/shard_map/all_to_all | solution.py:379
  112.6 21.3 %all-to-all-done = bf16[8,192,512]{2,1,0:T(8,128)(2,1)S(1)} async-done(((bf16[8,192,512]{2,1,0:T(8,128)(2,1)}), bf16[8,192,512]{2,1,0:T(8,128)(2,1)S(1)}, u32[]{:S(2)}, u32[]{:S(2)}) %all-to-all-start) | async-done | bytes 1572896 | tf_op jit(solution)/shard_map/all_to_all | solution.py:379
  134.3 4.0 %collective-permute-start.16 = (bf16[128,512]{1,0:T(8,128)(2,1)S(1)}, bf16[128,512]{1,0:T(8,128)(2,1)S(1)}, u32[]{:S(2)}, u32[]{:S(2)}) collective-permute-start(bf16[128,512]{1,0:T(8,128)(2,1)S(1)} %pad_maximum_fusion.5), channel_id=1, source_target_pairs={{0,16},{8,24},{16,0},{24,8},{32,48},{40,56},{48,32},{56,40},{64,80... | collective-permute-start | bytes 393224 | tf_op jit(solution)/shard_map/ppermute | solution.py:28
  141.3 3.9 %collective-permute-start.17 = (bf16[128,512]{1,0:T(8,128)(2,1)S(1)}, bf16[128,512]{1,0:T(8,128)(2,1)S(1)}, u32[]{:S(2)}, u32[]{:S(2)}) collective-permute-start(bf16[128,512]{1,0:T(8,128)(2,1)S(1)} %add_convert_fusion.3), channel_id=1, source_target_pairs={{0,32},{8,40},{16,48},{24,56},{32,0},{40,8},{48,16},{56,24},{64,96... | collective-permute-start | bytes 393224 | tf_op jit(solution)/shard_map/ppermute | solution.py:28
  145.2 6.3 %collective-permute-done.17 = bf16[128,512]{1,0:T(8,128)(2,1)S(1)} collective-permute-done((bf16[128,512]{1,0:T(8,128)(2,1)S(1)}, bf16[128,512]{1,0:T(8,128)(2,1)S(1)}, u32[]{:S(2)}, u32[]{:S(2)}) %collective-permute-start.17) | collective-permute-done | bytes 131104 | tf_op jit(solution)/shard_map/ppermute | solution.py:28
  151.6 10.5 %collective-permute-start.18 = (bf16[128,512]{1,0:T(8,128)(2,1)S(1)}, bf16[128,512]{1,0:T(8,128)(2,1)S(1)}, u32[]{:S(2)}, u32[]{:S(2)}) collective-permute-start(bf16[128,512]{1,0:T(8,128)(2,1)S(1)} %add_convert_fusion.2), channel_id=1, source_target_pairs={{0,64},{8,72},{16,80},{24,88},{32,96},{40,104},{48,112},{56,120},{... | collective-permute-start | bytes 393224 | tf_op jit(solution)/shard_map/ppermute | solution.py:28
  164.6 3.2 %collective-permute-start.19 = (bf16[128,512]{1,0:T(8,128)(2,1)S(1)}, bf16[128,512]{1,0:T(8,128)(2,1)S(1)}, u32[]{:S(2)}, u32[]{:S(2)}) collective-permute-start(bf16[128,512]{1,0:T(8,128)(2,1)S(1)} %add_convert_fusion.1), channel_id=1, source_target_pairs={{0,128},{8,136},{16,144},{24,152},{32,160},{40,168},{48,176},{56,1... | collective-permute-start | bytes 393224 | tf_op jit(solution)/shard_map/ppermute | solution.py:28
  175.7 3.6 %all-to-all-start.2 = ((bf16[8,224,512]{2,1,0:T(8,128)(2,1)}), bf16[8,224,512]{2,1,0:T(8,128)(2,1)S(1)}, u32[]{:S(2)}, u32[]{:S(2)}) async-start(bf16[8,224,512]{2,1,0:T(8,128)(2,1)} %broadcast_in_dim.39), calls=%async_computation.2 | async-start | bytes 3670016 | tf_op jit(solution)/shard_map/all_to_all | solution.py:576
  179.3 24.0 %all-to-all-done.2 = bf16[8,224,512]{2,1,0:T(8,128)(2,1)S(1)} async-done(((bf16[8,224,512]{2,1,0:T(8,128)(2,1)}), bf16[8,224,512]{2,1,0:T(8,128)(2,1)S(1)}, u32[]{:S(2)}, u32[]{:S(2)}) %all-to-all-start.2) | async-done | bytes 1835040 | tf_op jit(solution)/shard_map/all_to_all | solution.py:576
  206.5 3.6 %collective-permute-done.21 = bf16[1808,512]{1,0:T(8,128)(2,1)} collective-permute-done((bf16[1808,512]{1,0:T(8,128)(2,1)}, bf16[1808,512]{1,0:T(8,128)(2,1)}, u32[]{:S(2)}, u32[]{:S(2)}) %collective-permute-start.21) | collective-permute-done | bytes 1851424 | tf_op jit(solution)/shard_map/ppermute | solution.py:28
  (195 shorter events, 69.7 us)
Async XLA Ops:
  2.4 9.6 %collective-permute-start = (bf16[96,256]{1,0:T(8,128)(2,1)S(1)}, bf16[96,256]{1,0:T(8,128)(2,1)S(1)}, u32[]{:S(2)}, u32[]{:S(2)}) collective-permute-start(bf16[96,256]{1,0:T(8,128)(2,1)S(1)} %pad_maximum_fusion.9), channel_id=1, source_target_pairs={{0,8},{8,16},{16,24},{24,32},{32,40},{40,48},{48,56},{56,64},{64,7... | collective-permute-start | bytes 147464 | tf_op jit(solution)/shard_map/ppermute | solution.py:24
  7.3 5.4 %collective-permute-start.1 = (bf16[96,256]{1,0:T(8,128)(2,1)S(1)}, bf16[96,256]{1,0:T(8,128)(2,1)S(1)}, u32[]{:S(2)}, u32[]{:S(2)}) collective-permute-start(bf16[96,256]{1,0:T(8,128)(2,1)S(1)} %pad_maximum_fusion.10), channel_id=1, source_target_pairs={{8,0},{16,8},{24,16},{32,24},{40,32},{48,40},{56,48},{64,56},{72,6... | collective-permute-start | bytes 147464 | tf_op jit(solution)/shard_map/ppermute | solution.py:24
  14.5 4.6 %collective-permute-start.2 = (bf16[112,256]{1,0:T(8,128)(2,1)S(1)}, bf16[112,256]{1,0:T(8,128)(2,1)S(1)}, u32[]{:S(2)}, u32[]{:S(2)}) collective-permute-start(bf16[112,256]{1,0:T(8,128)(2,1)S(1)} %fusion.6), channel_id=1, source_target_pairs={{0,1},{1,2},{2,3},{3,4},{4,5},{5,6},{6,7},{8,9},{9,10},{10,11},{11... | collective-permute-start | bytes 172040 | tf_op jit(solution)/shard_map/ppermute | solution.py:24
  17.8 4.9 %collective-permute-start.3 = (bf16[112,256]{1,0:T(8,128)(2,1)S(1)}, bf16[112,256]{1,0:T(8,128)(2,1)S(1)}, u32[]{:S(2)}, u32[]{:S(2)}) collective-permute-start(bf16[112,256]{1,0:T(8,128)(2,1)S(1)} %fusion.8), channel_id=1, source_target_pairs={{1,0},{2,1},{3,2},{4,3},{5,4},{6,5},{7,6},{9,8},{10,9},{11,10},{12... | collective-permute-start | bytes 172040 | tf_op jit(solution)/shard_map/ppermute | solution.py:24
  25.7 12.2 %collective-permute-start.4 = (bf16[32,512]{1,0:T(8,128)(2,1)S(1)}, bf16[32,512]{1,0:T(8,128)(2,1)S(1)}, u32[]{:S(2)}, u32[]{:S(2)}) collective-permute-start(bf16[32,512]{1,0:T(8,128)(2,1)S(1)} %get-tuple-element.30), channel_id=1, source_target_pairs={{0,8},{8,16},{16,24},{24,32},{32,40},{40,48},{48,56},{56,64},{64,7... | collective-permute-start | bytes 98312 | tf_op jit(solution)/shard_map/ppermute | solution.py:24
  30.4 7.5 %collective-permute-start.5 = (bf16[32,512]{1,0:T(8,128)(2,1)S(1)}, bf16[32,512]{1,0:T(8,128)(2,1)S(1)}, u32[]{:S(2)}, u32[]{:S(2)}) collective-permute-start(bf16[32,512]{1,0:T(8,128)(2,1)S(1)} %get-tuple-element.30), channel_id=1, source_target_pairs={{8,0},{16,8},{24,16},{32,24},{40,32},{48,40},{56,48},{64,56},{72,6... | collective-permute-start | bytes 98312 | tf_op jit(solution)/shard_map/ppermute | solution.py:24
  32.4 5.5 %collective-permute-start.6 = (bf16[16,512]{1,0:T(8,128)(2,1)S(1)}, bf16[16,512]{1,0:T(8,128)(2,1)S(1)}, u32[]{:S(2)}, u32[]{:S(2)}) collective-permute-start(bf16[16,512]{1,0:T(8,128)(2,1)S(1)} %get-tuple-element.91), channel_id=1, source_target_pairs={{0,16},{8,24},{16,32},{24,40},{32,48},{40,56},{48,64},{56,72},{64,... | collective-permute-start | bytes 49160 | tf_op jit(solution)/shard_map/ppermute | solution.py:24
  35.9 4.5 %collective-permute-start.7 = (bf16[16,512]{1,0:T(8,128)(2,1)S(1)}, bf16[16,512]{1,0:T(8,128)(2,1)S(1)}, u32[]{:S(2)}, u32[]{:S(2)}) collective-permute-start(bf16[16,512]{1,0:T(8,128)(2,1)S(1)} %get-tuple-element.90), channel_id=1, source_target_pairs={{16,0},{24,8},{32,16},{40,24},{48,32},{56,40},{64,48},{72,56},{80,... | collective-permute-start | bytes 49160 | tf_op jit(solution)/shard_map/ppermute | solution.py:24
  42.7 7.4 %collective-permute-start.8 = (bf16[96,512]{1,0:T(8,128)(2,1)}, bf16[96,512]{1,0:T(8,128)(2,1)}, u32[]{:S(2)}, u32[]{:S(2)}) collective-permute-start(bf16[96,512]{1,0:T(8,128)(2,1)} %reshape.122), channel_id=1, source_target_pairs={{0,1},{1,2},{2,3},{3,4},{4,5},{5,6},{6,7},{8,9},{9,10},{10,11},{11... | collective-permute-start | bytes 294920 | tf_op jit(solution)/shard_map/ppermute | solution.py:24
  48.8 5.6 %collective-permute-start.9 = (bf16[96,512]{1,0:T(8,128)(2,1)}, bf16[96,512]{1,0:T(8,128)(2,1)S(1)}, u32[]{:S(2)}, u32[]{:S(2)}) collective-permute-start(bf16[96,512]{1,0:T(8,128)(2,1)} %reshape.123), channel_id=1, source_target_pairs={{1,0},{2,1},{3,2},{4,3},{5,4},{6,5},{7,6},{9,8},{10,9},{11,10},{12... | collective-permute-start | bytes 294920 | tf_op jit(solution)/shard_map/ppermute | solution.py:24
  67.0 5.4 %collective-permute-start.10 = (bf16[48,512]{1,0:T(8,128)(2,1)S(1)}, bf16[48,512]{1,0:T(8,128)(2,1)S(1)}, u32[]{:S(2)}, u32[]{:S(2)}) collective-permute-start(bf16[48,512]{1,0:T(8,128)(2,1)S(1)} %get-tuple-element.36), channel_id=1, source_target_pairs={{0,1},{1,2},{2,3},{3,4},{4,5},{5,6},{6,7},{8,9},{9,10},{10,11},{11... | collective-permute-start | bytes 147464 | tf_op jit(solution)/shard_map/ppermute | solution.py:24
  71.1 4.8 %collective-permute-start.11 = (bf16[48,512]{1,0:T(8,128)(2,1)S(1)}, bf16[48,512]{1,0:T(8,128)(2,1)S(1)}, u32[]{:S(2)}, u32[]{:S(2)}) collective-permute-start(bf16[48,512]{1,0:T(8,128)(2,1)S(1)} %get-tuple-element.37), channel_id=1, source_target_pairs={{1,0},{2,1},{3,2},{4,3},{5,4},{6,5},{7,6},{9,8},{10,9},{11,10},{12... | collective-permute-start | bytes 147464 | tf_op jit(solution)/shard_map/ppermute | solution.py:24
  76.2 10.5 %collective-permute-start.12 = (bf16[48,512]{1,0:T(8,128)(2,1)S(1)}, bf16[48,512]{1,0:T(8,128)(2,1)S(1)}, u32[]{:S(2)}, u32[]{:S(2)}) collective-permute-start(bf16[48,512]{1,0:T(8,128)(2,1)S(1)} %get-tuple-element.39), channel_id=1, source_target_pairs={{0,8},{8,16},{16,24},{24,32},{32,40},{40,48},{48,56},{56,64},{64,7... | collective-permute-start | bytes 147464 | tf_op jit(solution)/shard_map/ppermute | solution.py:24
  84.7 5.4 %collective-permute-start.13 = (bf16[48,512]{1,0:T(8,128)(2,1)S(1)}, bf16[48,512]{1,0:T(8,128)(2,1)S(1)}, u32[]{:S(2)}, u32[]{:S(2)}) collective-permute-start(bf16[48,512]{1,0:T(8,128)(2,1)S(1)} %get-tuple-element.40), channel_id=1, source_target_pairs={{8,0},{16,8},{24,16},{32,24},{40,32},{48,40},{56,48},{64,56},{72,6... | collective-permute-start | bytes 147464 | tf_op jit(solution)/shard_map/ppermute | solution.py:24
  94.1 14.7 %all-to-all-start.1 = ((bf16[8,48,512]{2,1,0:T(8,128)(2,1)}), bf16[8,48,512]{2,1,0:T(8,128)(2,1)S(1)}, u32[]{:S(2)}, u32[]{:S(2)}) async-start(bf16[8,48,512]{2,1,0:T(8,128)(2,1)} %pad_maximum_fusion.3), calls=%async_computation.1 | async-start | bytes 786432 | tf_op jit(solution)/shard_map/all_to_all | solution.py:379
  100.0 1.6 collective-permute-start.14
  108.8 25.0 %all-to-all-start = ((bf16[8,192,512]{2,1,0:T(8,128)(2,1)}), bf16[8,192,512]{2,1,0:T(8,128)(2,1)S(1)}, u32[]{:S(2)}, u32[]{:S(2)}) async-start(bf16[8,192,512]{2,1,0:T(8,128)(2,1)} %bitcast.14), calls=%async_computation | async-start | bytes 3145728 | tf_op jit(solution)/shard_map/all_to_all | solution.py:379
  134.3 7.0 %collective-permute-start.16 = (bf16[128,512]{1,0:T(8,128)(2,1)S(1)}, bf16[128,512]{1,0:T(8,128)(2,1)S(1)}, u32[]{:S(2)}, u32[]{:S(2)}) collective-permute-start(bf16[128,512]{1,0:T(8,128)(2,1)S(1)} %pad_maximum_fusion.5), channel_id=1, source_target_pairs={{0,16},{8,24},{16,0},{24,8},{32,48},{40,56},{48,32},{56,40},{64,80... | collective-permute-start | bytes 393224 | tf_op jit(solution)/shard_map/ppermute | solution.py:28
  141.3 10.2 %collective-permute-start.17 = (bf16[128,512]{1,0:T(8,128)(2,1)S(1)}, bf16[128,512]{1,0:T(8,128)(2,1)S(1)}, u32[]{:S(2)}, u32[]{:S(2)}) collective-permute-start(bf16[128,512]{1,0:T(8,128)(2,1)S(1)} %add_convert_fusion.3), channel_id=1, source_target_pairs={{0,32},{8,40},{16,48},{24,56},{32,0},{40,8},{48,16},{56,24},{64,96... | collective-permute-start | bytes 393224 | tf_op jit(solution)/shard_map/ppermute | solution.py:28
  151.6 13.0 %collective-permute-start.18 = (bf16[128,512]{1,0:T(8,128)(2,1)S(1)}, bf16[128,512]{1,0:T(8,128)(2,1)S(1)}, u32[]{:S(2)}, u32[]{:S(2)}) collective-permute-start(bf16[128,512]{1,0:T(8,128)(2,1)S(1)} %add_convert_fusion.2), channel_id=1, source_target_pairs={{0,64},{8,72},{16,80},{24,88},{32,96},{40,104},{48,112},{56,120},{... | collective-permute-start | bytes 393224 | tf_op jit(solution)/shard_map/ppermute | solution.py:28
  164.6 5.6 %collective-permute-start.19 = (bf16[128,512]{1,0:T(8,128)(2,1)S(1)}, bf16[128,512]{1,0:T(8,128)(2,1)S(1)}, u32[]{:S(2)}, u32[]{:S(2)}) collective-permute-start(bf16[128,512]{1,0:T(8,128)(2,1)S(1)} %add_convert_fusion.1), channel_id=1, source_target_pairs={{0,128},{8,136},{16,144},{24,152},{32,160},{40,168},{48,176},{56,1... | collective-permute-start | bytes 393224 | tf_op jit(solution)/shard_map/ppermute | solution.py:28
  170.3 4.0 %collective-permute-start.20 = (bf16[112,512]{1,0:T(8,128)(2,1)S(1)}, bf16[112,512]{1,0:T(8,128)(2,1)S(1)}, u32[]{:S(2)}, u32[]{:S(2)}) collective-permute-start(bf16[112,512]{1,0:T(8,128)(2,1)S(1)} %slice.293), channel_id=1, source_target_pairs={{0,16},{8,24},{16,0},{24,8},{32,48},{40,56},{48,32},{56,40},{64,80... | collective-permute-start | bytes 344072 | tf_op jit(solution)/shard_map/ppermute | solution.py:28
  175.7 27.6 %all-to-all-start.2 = ((bf16[8,224,512]{2,1,0:T(8,128)(2,1)}), bf16[8,224,512]{2,1,0:T(8,128)(2,1)S(1)}, u32[]{:S(2)}, u32[]{:S(2)}) async-start(bf16[8,224,512]{2,1,0:T(8,128)(2,1)} %broadcast_in_dim.39), calls=%async_computation.2 | async-start | bytes 3670016 | tf_op jit(solution)/shard_map/all_to_all | solution.py:576
  204.7 5.4 %collective-permute-start.21 = (bf16[1808,512]{1,0:T(8,128)(2,1)}, bf16[1808,512]{1,0:T(8,128)(2,1)}, u32[]{:S(2)}, u32[]{:S(2)}) collective-permute-start(bf16[1808,512]{1,0:T(8,128)(2,1)} %pad_maximum_fusion), channel_id=1, source_target_pairs={{0,8},{8,0},{16,24},{24,16},{32,40},{40,32},{48,56},{56,48},{64,72... | collective-permute-start | bytes 5554184 | tf_op jit(solution)/shard_map/ppermute | solution.py:28
  (41 other events, 546.7 us)

commit v3 on v2

v3 whole, which is shorter than its diff:
```python
import functools
import math

import jax
import jax.numpy as jnp
import numpy as np
from jax import lax
from jax.experimental import pallas as pl
from jax.experimental.pallas import tpu as pltpu
from jax.sharding import PartitionSpec as P

HEAD = 64
RADIUS = 3
PAIR = 2 * HEAD
TILE = (8, 16)
VMEM = 32 << 20
NEG = -1e30
norm_eps = 1e-06
f32 = jnp.float32
bf16 = jnp.bfloat16


def shifted(x, axis, by):
    count = lax.axis_size(axis)
    pairs = [(i, i + by) for i in range(count) if 0 <= i + by < count]
    return lax.ppermute(x, axis, pairs)


def flip(x, axis, bit):
    return lax.ppermute(x, axis, [(i, i ^ bit) for i in range(lax.axis_size(axis))])


def add_b(a, b):
    return (a.astype(f32) + b.astype(f32)).astype(bf16)


def grid_piece(rows, columns, length=None):
    piece = [(r, c) for r in rows for c in columns]
    return piece + [None] * ((length or len(piece)) - len(piece))


def merge_order(rows, columns):
    return [
        (2 * a + rp, 2 * b + cp)
        for rp in (0, 1)
        for cp in (0, 1)
        for a in range(rows // 2)
        for b in range(columns // 2)
    ]


def fine_keys(rows, columns):
    near, reach = RADIUS + 1, 2 * RADIUS + 1
    tall = range(-reach, rows + reach)
    side = -(-len(tall) * RADIUS // 16) * 16
    rim = merge_order(near, columns)
    return [
        merge_order(rows, columns),
        [(r - near, c) for r, c in rim],
        [(r + rows, c) for r, c in rim],
        grid_piece(range(-reach, -near), range(columns)),
        grid_piece(range(rows + near, rows + reach), range(columns)),
        grid_piece(tall, range(-RADIUS, 0), side),
        grid_piece(tall, range(columns, columns + RADIUS), side),
    ]


def back_keys(rows, columns):
    tall = range(-RADIUS, rows + RADIUS)
    side = -(-len(tall) * RADIUS // 16) * 16
    return [
        merge_order(rows, columns),
        grid_piece(range(-RADIUS, 0), range(columns)),
        grid_piece(range(rows, rows + RADIUS), range(columns)),
        grid_piece(tall, range(-RADIUS, 0), side),
        grid_piece(tall, range(columns, columns + RADIUS), side),
    ]


def coarse_keys(rows, columns):
    reach = 2 * RADIUS
    tall = range(-reach, rows + reach)
    return [
        grid_piece(range(rows), range(columns)),
        grid_piece(range(-2, 0), range(columns)),
        grid_piece(range(rows, rows + 2), range(columns)),
        grid_piece(range(-reach, -2), range(columns)),
        grid_piece(range(rows + 2, rows + reach), range(columns)),
        grid_piece(tall, range(-reach, 0)),
        grid_piece(tall, range(columns, columns + reach)),
    ]


def coarse_queries(rows, columns):
    reach = RADIUS
    tall = range(-reach, rows + reach)
    side = -(-len(tall) * reach // 16) * 16
    return [
        grid_piece(range(rows), range(columns)),
        grid_piece(range(-reach, 0), range(columns)),
        grid_piece(range(rows, rows + reach), range(columns)),
        grid_piece(tall, range(-reach, 0), side),
        grid_piece(tall, range(columns, columns + reach), side),
    ]


def joined(pieces):
    return [place for piece in pieces for place in piece]


def band_bias(queries, keys):
    bias = np.full((len(queries), len(keys)), NEG, np.float32)
    for i, q in enumerate(queries):
        for j, k in enumerate(keys):
            if q is None:
                inside = j == 0
            else:
                inside = k is not None and max(abs(q[0] - k[0]), abs(q[1] - k[1])) <= RADIUS
            if inside:
                bias[i, j] = 0.0
    return bias


def places(keys):
    return Late(jnp.asarray(np.array([[k[i] if k else 0 for k in keys] for i in (0, 1)], np.int32)))


def one_hot(targets, sources):
    place = {s: j for j, s in enumerate(sources) if s is not None}
    matrix = np.zeros((len(targets), len(sources)), np.float32)
    for i, t in enumerate(targets):
        if t is not None and t in place:
            matrix[i, place[t]] = 1.0
    return matrix.astype(jnp.bfloat16)


def dot(a, b):
    return jnp.dot(a, b, preferred_element_type=f32)


def dot_nt(a, b):
    return lax.dot_general(a, b, (((1,), (1,)), ((), ())), preferred_element_type=f32)


def dot_tn(a, b):
    return lax.dot_general(a, b, (((0,), (0,)), ((), ())), preferred_element_type=f32)


def norm_forward(x, gain):
    values = x.astype(f32)
    scale = lax.rsqrt(jnp.mean(values * values, axis=-1, keepdims=True) + norm_eps)
    return values, scale, (values * scale * gain).astype(bf16)


def norm_backward(values, scale, gain, upstream):
    gain_part = jnp.sum(upstream * values * scale, axis=0, keepdims=True)
    weighted = upstream * gain
    inner = jnp.mean(weighted * values, axis=-1, keepdims=True)
    return weighted * scale - values * (scale * scale * scale) * inner, gain_part


def validity(at, where, rows, columns):
    row = at[0:1, :] + where[0] * rows
    col = at[1:2, :] + where[1] * columns
    ok = (row >= 0) & (row < where[2] * rows) & (col >= 0) & (col < where[3] * columns)
    return jnp.where(ok, 0.0, NEG)


def split_rows(x):
    half = x.shape[1] // 2
    return jnp.concatenate([x[:, :half], x[:, half:]], axis=0)


def join_rows(x):
    half = x.shape[0] // 2
    return jnp.concatenate([x[:half], x[half:]], axis=1)


def head_masks():
    lane = lax.broadcasted_iota(jnp.int32, (1, PAIR), 1)
    return [(lane < HEAD).astype(f32), (lane >= HEAD).astype(f32)]


def masked(x, mask):
    return (x.astype(f32) * mask).astype(bf16)


def probabilities(query, keys, bias):
    weights = jnp.exp(dot_nt(query, keys) * (1.0 / math.sqrt(HEAD)) + bias)
    total = jnp.sum(weights, axis=-1, keepdims=True)
    return weights / jnp.where(total > 0.0, total, 1.0)


def score_gradient(prob, dprob):
    total = jnp.sum(prob * dprob, axis=-1, keepdims=True)
    return (prob * (dprob - total) * (1.0 / math.sqrt(HEAD))).astype(bf16)


def lanes(x, place):
    return x[:, place * PAIR : (place + 1) * PAIR]


def rows_pack_kernel(tok, gc, down_out, up_out):
    rim = down_out.shape[0] - 2 * gc.shape[0]
    both = split_rows(gc[...])
    down_out[:rim] = tok[tok.shape[0] - rim :, :]
    up_out[:rim] = tok[:rim, :]
    down_out[rim:] = both
    up_out[rim:] = both


def columns_pack_kernel(tok, gc, up, down, pick, cpick, right_out, left_out):
    rim = up.shape[0] - 2 * gc.shape[0]
    side = pick.shape[0] // 2
    cside = cpick.shape[0] // 2
    field = jnp.concatenate([tok[...], up[:rim], down[:rim]], axis=0)
    sends = dot(pick[...], field).astype(bf16)
    coarse = jnp.concatenate([gc[...], join_rows(up[rim:]), join_rows(down[rim:])], axis=0)
    csends = dot(cpick[...], coarse).astype(bf16)
    right_out[:side] = sends[:side]
    left_out[:side] = sends[side:]
    right_out[side:] = split_rows(csends[:cside])
    left_out[side:] = split_rows(csends[cside:])


def coarse_pack_kernel(near, up, down, pick, right_out, left_out):
    field = jnp.concatenate([near[...], up[...], down[...]], axis=0)
    sends = dot(pick[...], field).astype(bf16)
    side = right_out.shape[0]
    right_out[...] = sends[:side]
    left_out[...] = sends[side:]


def fine_forward_kernel(
    tok, up, down, left, right, perm, perm_rim, gain, w_qkv, w_out, w_merge, band, at, where,
    merged_out, near_out, down_out, up_out, normed_out, proj_out, kv_out, att_out,
):
    width = tok.shape[1]
    count, rim = perm.shape[0], perm_rim.shape[0]
    far = up.shape[0] - 2 * merged_out.shape[0]
    side = (kv_out.shape[0] - count - 2 * far) // 2
    own = dot(perm[...], tok[...]).astype(bf16)
    above = dot(perm_rim[...], up[far - rim : far]).astype(bf16)
    below = dot(perm_rim[...], down[:rim]).astype(bf16)
    inner = jnp.concatenate([own, above, below], axis=0)
    field = jnp.concatenate(
        [inner, up[: far - rim], down[rim:far], left[:side], right[:side]], axis=0
    )
    _, _, normed = norm_forward(field, gain[...])
    normed_out[...] = normed[:count]
    asked = inner.shape[0]
    query = dot(normed[:asked], w_qkv[:, :width]).astype(bf16)
    kv = dot(normed, w_qkv[:, width:]).astype(bf16)
    proj_out[...] = query[:count]
    kv_out[...] = kv
    bias = band[...] + validity(at[...], where, *TILE)
    masks = head_masks()
    parts = []
    for p in range(width // PAIR):
        keys, vals, q = lanes(kv, p), lanes(kv, width // PAIR + p), lanes(query, p)
        total = None
        for mask in masks:
            prob = probabilities(masked(q, mask), keys, bias)
            part = dot(prob.astype(bf16), vals) * mask
            total = part if total is None else total + part
        parts.append(total.astype(bf16))
    attended = jnp.concatenate(parts, axis=1)
    att_out[...] = attended[:count]
    fine = (inner.astype(f32) + dot(attended, w_out[...])).astype(bf16)
    quarter, small = count // 4, rim // 4
    acc = None
    for p in range(4):
        block = fine[p * quarter : (p + 1) * quarter]
        merged_out[:, p * width : (p + 1) * width] = block
        upper = fine[count + p * small : count + (p + 1) * small]
        lower = fine[count + rim + p * small : count + rim + (p + 1) * small]
        block = jnp.concatenate([block, upper, lower], axis=0)
        part = dot(block, w_merge[p * width : (p + 1) * width, :])
        acc = part if acc is None else acc + part
    near = acc.astype(bf16)
    near_out[...] = near
    half = quarter // 2
    down_out[:small] = near[quarter : quarter + small]
    down_out[small:] = near[:half]
    up_out[:half] = near[half:quarter]
    up_out[half:] = near[quarter + small :]


def coarse_kernel(
    near, up, down, left, right, gc, gup, gdown, gleft, gright, merged, pick, gpick,
    gain, w_qkv, w_out, w_merge, band, at, where,
    keep_out, send_out, gain_out, grad_merged_out,
):
    own, width = merged.shape[0], near.shape[1]
    pairs = width // PAIR
    field = jnp.concatenate([near[...], up[...], down[...], left[...], right[...]], axis=0)
    values, scale, normed = norm_forward(field, gain[...])
    kv = dot(normed, w_qkv[:, width:]).astype(bf16)
    picked = dot(pick[...], normed).astype(bf16)
    query = dot(picked, w_qkv[:, :width]).astype(bf16)
    tall, wide = gup.shape[0] - 2 * own, gleft.shape[0] - 2 * (gpick.shape[1] - 3 * own) // 2
    given = [gc[...], join_rows(gup[tall:]), join_rows(gdown[tall:])]
    given += [join_rows(gleft[wide:]), join_rows(gright[wide:])]
    u_b = dot(gpick[...], jnp.concatenate(given, axis=0)).astype(bf16)
    grad_att = dot_nt(u_b, w_out[...]).astype(bf16)
    bias = band[...] + validity(at[...], where, TILE[0] // 2, TILE[1] // 2)
    masks = head_masks()
    att, gq, gk, gv = [], [], [], []
    for p in range(pairs):
        keys, vals = lanes(kv, p), lanes(kv, pairs + p)
        q, g = lanes(query, p), lanes(grad_att, p)
        sums = None
        for mask in masks:
            qm, gm = masked(q, mask), masked(g, mask)
            prob = probabilities(qm, keys, bias)
            prob_b = prob.astype(bf16)
            dscore = score_gradient(prob, dot_nt(gm, vals))
            new = (
                dot(prob_b[:own], vals) * mask,
                dot(dscore[:own], keys) * mask,
                dot_tn(dscore[:, :PAIR], qm)[:own],
                dot_tn(prob_b[:, :PAIR], gm)[:own],
            )
            sums = new if sums is None else tuple(a + b for a, b in zip(sums, new))
        for group, part in zip((att, gq, gk, gv), sums):
            group.append(part.astype(bf16))
    attended = jnp.concatenate(att, axis=1)
    grad_proj = jnp.concatenate(gq + gk + gv, axis=1)
    grad_normed = dot_nt(grad_proj, w_qkv[...])
    grad_in, gain_part = norm_backward(values[:own], scale[:own], gain[...], grad_normed)
    gain_out[...] = gain_part
    c_b = (u_b[:own].astype(f32) + grad_in).astype(bf16)
    grad_merged_out[...] = dot_nt(c_b, w_merge[...])
    first = where[0] % 2 == 0
    place = 0
    for x in (merged[...], normed[:own], attended):
        half = x.shape[1] // 2
        low, high = x[:, :half].astype(f32), x[:, half:].astype(f32)
        keep_out[:, place : place + half] = jnp.where(first, low, high).astype(bf16)
        send_out[:, place : place + half] = jnp.where(first, high, low).astype(bf16)
        place += half
    for g in (c_b, grad_proj, u_b[:own]):
        send_out[:, place : place + g.shape[1]] = g
        place += g.shape[1]


def coarse_weights_kernel(factor, keep, sent, got, out):
    half = keep.shape[1]
    cols = out.shape[2]
    x = jnp.concatenate([keep[...], got[:, :half]], axis=0)
    g = jnp.concatenate([sent[:, half:], got[:, half:]], axis=0)
    wide = half // 2
    narrow = wide // 2
    normed, attended = x[:, wide : wide + narrow], x[:, wide + narrow :]
    parts = [(x[:, :wide], 0)] + [(normed, b) for b in (1, 2, 3)] + [(attended, 4)]
    place = 0
    for a, b in parts:
        part = (dot_tn(a, g[:, b * cols : (b + 1) * cols]) * factor).astype(bf16)
        rows = part.shape[0] // out.shape[0]
        for j in range(out.shape[0]):
            out[j, place : place + rows] = part[j * rows : (j + 1) * rows]
        place += rows


def fine_backward_kernel(
    grad_fine, grad_merged, perm, query_in, kv_in, pick, w_out, band, at, where,
    up_out, gq_out, mid_out, left_out, right_out,
):
    width = grad_fine.shape[1]
    pairs = width // PAIR
    total = jnp.concatenate([grad_merged[:, p * width : (p + 1) * width] for p in range(4)], axis=0)
    up = dot(perm[...], grad_fine[...]) + total
    up_out[...] = up
    grad_att = dot_nt(up.astype(bf16), w_out[...]).astype(bf16)
    query = query_in[...]
    kv = dot(pick[...], kv_in[...]).astype(bf16)
    bias = band[...] + validity(at[...], where, *TILE)
    masks = head_masks()
    middle, side = mid_out.shape[0], left_out.shape[0]
    for p in range(pairs):
        keys, vals = lanes(kv, p), lanes(kv, pairs + p)
        q, g = lanes(query, p), lanes(grad_att, p)
        sums = None
        for mask in masks:
            qm, gm = masked(q, mask), masked(g, mask)
            prob = probabilities(qm, keys, bias)
            dscore = score_gradient(prob, dot_nt(gm, vals))
            new = (
                dot(dscore, keys) * mask,
                dot_tn(dscore, qm),
                dot_tn(prob.astype(bf16), gm),
            )
            sums = new if sums is None else tuple(a + b for a, b in zip(sums, new))
        gq_out[:, p * PAIR : (p + 1) * PAIR] = sums[0].astype(bf16)
        for part, at in ((sums[1], p), (sums[2], pairs + p)):
            where = slice(at * PAIR, (at + 1) * PAIR)
            mid_out[:, where] = part[:middle]
            left_out[:, where] = part[middle : middle + side].astype(bf16)
            right_out[:, where] = part[middle + side :].astype(bf16)


def fine_fold_kernel(mid, from_left, from_right, place_left, place_right, own_out, top_out, bottom_out):
    folded = mid[...] + dot(place_left[...], from_left[...]) + dot(place_right[...], from_right[...])
    own, rim = own_out.shape[0], top_out.shape[0]
    own_out[...] = folded[:own]
    top_out[...] = folded[own : own + rim].astype(bf16)
    bottom_out[...] = folded[own + rim :].astype(bf16)


def fine_last_kernel(
    own, from_above, from_below, place_above, place_below, gq, up, tok, perm, normed, att, gain, w_qkv, where,
    grad_out, gain_out, keep_out, send_out,
):
    width = tok.shape[1]
    kv = own[...] + dot(place_above[...], from_above[...]) + dot(place_below[...], from_below[...])
    grad_proj = jnp.concatenate([gq[...], kv.astype(bf16)], axis=1)
    values, scale, _ = norm_forward(dot(perm[...], tok[...]), gain[...])
    grad_in, gain_part = norm_backward(values, scale, gain[...], dot_nt(grad_proj, w_qkv[...]))
    gain_out[...] = gain_part
    grad_out[...] = dot_tn(perm[...], (up[...] + grad_in).astype(bf16)).astype(bf16)
    first = where[0] % 2 == 0
    half = width // 2
    place = 0
    for x in (normed[...], att[...]):
        low, high = x[:, :half].astype(f32), x[:, half:].astype(f32)
        keep_out[:, place : place + half] = jnp.where(first, low, high).astype(bf16)
        send_out[:, place : place + half] = jnp.where(first, high, low).astype(bf16)
        place += half
    send_out[:, place : place + 3 * width] = grad_proj
    send_out[:, place + 3 * width :] = up[...].astype(bf16)


def fine_weights_kernel(factor, keep, sent, got, gain, cgain, out):
    wide = keep.shape[1]
    half = wide // 2
    x = jnp.concatenate([keep[...], got[:, :wide]], axis=0)
    g = jnp.concatenate([sent[:, wide:], got[:, wide:]], axis=0)
    qkv = (dot_tn(x[:, :half], g[:, : 3 * wide]) * factor).astype(bf16)
    last = (dot_tn(x[:, half:], g[:, 3 * wide :]) * factor).astype(bf16)
    rows = half // out.shape[0]
    zeros = jnp.zeros((14, 2 * wide), f32)
    padded = jnp.concatenate([gain[...], jnp.zeros((1, wide), f32)], axis=1)
    gains = jnp.concatenate([cgain[...], padded, zeros], axis=0)
    gains = (gains * factor).astype(bf16)
    for j in range(out.shape[0]):
        at = slice(j * rows, (j + 1) * rows)
        out[j, :rows] = qkv[at, : 2 * wide]
        out[j, rows : 2 * rows, :wide] = qkv[at, 2 * wide :]
        out[j, rows : 2 * rows, wide:] = last[at]
        out[j, 2 * rows :] = gains


def unpack_kernel(where, mine, other, merge, qkv1, out1, qkv0, out0, *scratch):
    first = where[0] % 2
    cols, width = mine.shape[0], mine.shape[2]
    half = width // 2
    sems = scratch[-1]
    outs = (merge, qkv1, out1, qkv0, out0)
    m, q1, o1, q0, o0 = scratch[:-1]
    at = 0
    copies = []

    def move(rows, lanes, dst, dst_lanes):
        for src, core in ((mine, first), (other, 1 - first)):
            for j in range(cols):
                dst[core * cols + j, :, dst_lanes] = src[j, rows, lanes]

    def finish(n):
        copies.append(pltpu.make_async_copy(scratch[n], outs[n], sems.at[n]))
        copies[-1].start()

    every = slice(0, width)
    for n in (0, 1, 2):
        rows = outs[n].shape[1]
        for b in range(outs[n].shape[2] // width):
            move(slice(at, at + rows), every, scratch[n], slice(b * width, (b + 1) * width))
            at += rows
        finish(n)
    rows = qkv0.shape[1]
    move(slice(at, at + rows), every, q0, every)
    at += rows
    move(slice(at, at + rows), slice(0, half), q0, slice(width, width + half))
    finish(3)
    move(slice(at, at + rows), slice(half, width), o0, slice(0, half))
    finish(4)
    for copy in copies:
        copy.wait()


class Late:
    def __init__(self, value):
        self.value = value


class Arriving:
    def __init__(self, ref, copy):
        self.ref, self.copy, self.shape = ref, copy, ref.shape

    def __getitem__(self, index):
        if self.copy is not None:
            self.copy.wait()
            self.copy = None
        return self.ref[index]


def call(kernel, outs, flops=1 << 28):
    vmem = pl.BlockSpec(memory_space=pltpu.VMEM)
    smem = pl.BlockSpec(memory_space=pltpu.SMEM)
    anywhere = pl.BlockSpec(memory_space=pl.ANY)

    def run(*args):
        late = [i for i, a in enumerate(args) if isinstance(a, Late)]
        given = [
            pltpu.with_memory_space_constraint(a.value, pltpu.HBM) if isinstance(a, Late) else a
            for a in args
        ]

        def body(*refs):
            ins, results = list(refs[: len(args)]), refs[len(args) : len(args) + len(outs)]
            rest = refs[len(args) + len(outs) :]
            arriving = []
            for n, i in enumerate(late):
                copy = pltpu.make_async_copy(ins[i], rest[n], rest[-1].at[n])
                copy.start()
                ins[i] = Arriving(rest[n], copy)
                arriving.append(ins[i])
            kernel(*ins, *results)
            for operand in arriving:
                if operand.copy is not None:
                    operand.copy.wait()

        scratch = [pltpu.VMEM(given[i].shape, given[i].dtype) for i in late]
        if late:
            scratch.append(pltpu.SemaphoreType.DMA((len(late),)))
        return pl.pallas_call(
            body,
            out_shape=[jax.ShapeDtypeStruct(shape, dtype) for shape, dtype in outs],
            in_specs=[
                anywhere if i in late else smem if a.ndim == 1 else vmem
                for i, a in enumerate(given)
            ],
            out_specs=[vmem] * len(outs),
            scratch_shapes=scratch,
            compiler_params=pltpu.CompilerParams(vmem_limit_bytes=VMEM),
            cost_estimate=pl.CostEstimate(flops=flops, bytes_accessed=4 << 20, transcendentals=0),
        )(*given)

    return run


def scatter_over_columns(x):
    count = lax.axis_size("col")
    pieces = lax.all_to_all(x, "col", 0, 0)
    return jnp.sum(pieces.reshape(count, -1, x.shape[-1]).astype(f32), axis=0).astype(bf16)


def reduce_rows(x, small):
    half = x.shape[0] // 2
    mine = (lax.axis_index("row") // 2) % 2
    keep = lax.dynamic_slice_in_dim(x, mine * half, half, axis=0)
    send = lax.dynamic_slice_in_dim(x, (1 - mine) * half, half, axis=0)
    got = flip(jnp.concatenate([send, small], axis=0), "row", 2)
    x = add_b(jnp.concatenate([keep, small], axis=0), got)
    bit = 4
    while bit < lax.axis_size("row"):
        x = add_b(x, flip(x, "row", bit))
        bit *= 2
    x, small = x[:half], x[half:]
    other = flip(x, "row", 2)
    return jnp.where(mine == 0, jnp.concatenate([x, other]), jnp.concatenate([other, x])), small


def per_device(
    tokens,
    gain_fine,
    qkv_fine,
    out_fine,
    w_merge,
    gain_coarse,
    qkv_coarse,
    out_coarse,
    grad_fine,
    grad_coarse,
):
    rows, columns, width = tokens.shape
    crows, ccolumns, cwidth = grad_coarse.shape
    count, ccount = rows * columns, crows * ccolumns
    cols = lax.axis_size("col")
    where = jnp.stack(
        [lax.axis_index("row"), lax.axis_index("col"), lax.axis_size("row"), cols]
    ).astype(jnp.int32)
    factor = 1.0 / math.sqrt(rows * lax.axis_size("row") * columns * cols)
    tok = Late(tokens.reshape(count, width))
    gc = Late(grad_coarse.reshape(ccount, cwidth))
    gain0, gain1 = Late(gain_fine[None, :]), Late(gain_coarse[None, :])
    qkv_fine, out_fine, w_merge = Late(qkv_fine), Late(out_fine), Late(w_merge)
    qkv_coarse, out_coarse = Late(qkv_coarse), Late(out_coarse)

    def moved(piece, dr, dc):
        return [None if p is None else (p[0] + dr, p[1] + dc) for p in piece]

    def chosen(targets, sources):
        return Late(jnp.asarray(one_hot(targets, sources)))

    keys0, keys1 = fine_keys(rows, columns), coarse_keys(crows, ccolumns)
    queries1 = coarse_queries(crows, ccolumns)
    natural = grid_piece(range(rows), range(columns))
    cnatural = queries1[0]
    rim = (2 * RADIUS + 1) * columns
    side, cside = len(keys0[5]), len(queries1[3])
    send_down, send_up = call(
        rows_pack_kernel, [((rim + 2 * ccount, width), bf16)] * 2, flops=1 << 20
    )(tok, gc)
    up = shifted(send_down, "row", 1)
    down = shifted(send_up, "row", -1)
    held = natural + moved(natural[-rim:], -rows, 0) + moved(natural[:rim], rows, 0)
    cheld = cnatural + moved(cnatural, -crows, 0) + moved(cnatural, crows, 0)
    send_right, send_left = call(
        columns_pack_kernel, [((side + 2 * cside, width), bf16)] * 2, flops=1 << 20
    )(
        tok,
        gc,
        up,
        down,
        chosen(moved(keys0[5], 0, columns) + moved(keys0[6], 0, -columns), held),
        chosen(moved(queries1[3], 0, ccolumns) + moved(queries1[4], 0, -ccolumns), cheld),
    )
    left = shifted(send_right, "col", 1)
    right = shifted(send_left, "col", -1)

    flat0 = joined(keys0)
    own0 = keys0[0]
    asked0 = joined(keys0[:3])
    perm = chosen(own0, natural)
    near = len(keys0[1])
    merged, near1, down1, up1, normed0, query0, kv0, att0 = call(
        fine_forward_kernel,
        [
            ((ccount, 4 * width), bf16),
            ((ccount + near // 2, cwidth), bf16),
            ((ccount, cwidth), bf16),
            ((ccount, cwidth), bf16),
            ((count, width), bf16),
            ((count, width), bf16),
            ((len(flat0), 2 * width), bf16),
            ((count, width), bf16),
        ],
    )(
        tok,
        up,
        down,
        left,
        right,
        perm,
        chosen(merge_order(RADIUS + 1, columns), natural[:near]),
        gain0,
        qkv_fine,
        out_fine,
        w_merge,
        Late(jnp.asarray(band_bias(asked0, flat0))),
        places(flat0),
        where,
    )

    above1 = shifted(down1, "row", 1)
    below1 = shifted(up1, "row", -1)
    tall1 = joined(keys1[:5])
    wide1 = len(keys1[5])
    send_right, send_left = call(
        coarse_pack_kernel, [((wide1, cwidth), bf16)] * 2, flops=1 << 20
    )(
        near1,
        above1,
        below1,
        chosen(moved(keys1[5], 0, ccolumns) + moved(keys1[6], 0, -ccolumns), tall1),
    )
    left1 = shifted(send_right, "col", 1)
    right1 = shifted(send_left, "col", -1)

    flat1, ask1 = joined(keys1), joined(queries1)
    kept = (4 * width + 2 * cwidth) // 2
    keep1, send1, gain_part1, grad_merged = call(
        coarse_kernel,
        [
            ((ccount, kept), bf16),
            ((ccount, kept + 5 * cwidth), bf16),
            ((1, cwidth), f32),
            ((ccount, 4 * width), f32),
        ],
    )(
        near1,
        above1,
        below1,
        left1,
        right1,
        gc,
        up,
        down,
        left,
        right,
        merged,
        chosen(ask1, flat1),
        chosen(ask1, cheld + queries1[3] + queries1[4]),
        gain1,
        qkv_coarse,
        out_coarse,
        w_merge,
        Late(jnp.asarray(band_bias(ask1, flat1))),
        places(flat1),
        where,
    )
    n1 = (2 * width + 4 * (cwidth // 2)) // cols
    (packed1,) = call(
        functools.partial(coarse_weights_kernel, factor), [((cols, n1, cwidth), bf16)]
    )(keep1, send1, flip(send1, "row", 1))

    backs = back_keys(rows, columns)
    flatb = joined(backs)
    rims = len(backs[1])
    bside = len(backs[3])
    middle = count + 2 * rims
    up0, gq0, mid, left_rim, right_rim = call(
        fine_backward_kernel,
        [
            ((count, width), f32),
            ((count, width), bf16),
            ((middle, 2 * width), f32),
            ((bside, 2 * width), bf16),
            ((bside, 2 * width), bf16),
        ],
    )(
        Late(grad_fine.reshape(count, width)),
        grad_merged,
        perm,
        query0,
        kv0,
        chosen(flatb, flat0),
        out_fine,
        Late(jnp.asarray(band_bias(own0, flatb))),
        places(flatb),
        where,
    )
    left_rim, right_rim, packed1 = lax.optimization_barrier((left_rim, right_rim, packed1))
    sums1 = scatter_over_columns(packed1)
    from_right = shifted(left_rim, "col", -1)
    from_left = shifted(right_rim, "col", 1)
    mids = joined(backs[:3])
    own, top_rim, bottom_rim = call(
        fine_fold_kernel,
        [((count, 2 * width), f32), ((rims, 2 * width), bf16), ((rims, 2 * width), bf16)],
        flops=1 << 20,
    )(
        mid,
        from_left,
        from_right,
        chosen(mids, moved(backs[4], 0, -columns)),
        chosen(mids, moved(backs[3], 0, columns)),
    )
    from_below = shifted(top_rim, "row", -1)
    from_above = shifted(bottom_rim, "row", 1)
    from_above, from_below, sums1 = lax.optimization_barrier((from_above, from_below, sums1))
    grad_tokens, gain_part0, keep0, send0 = call(
        fine_last_kernel,
        [
            ((count, width), bf16),
            ((1, width), f32),
            ((count, width), bf16),
            ((count, 5 * width), bf16),
        ],
    )(
        own,
        from_above,
        from_below,
        chosen(own0, moved(backs[2], -rows, 0)),
        chosen(own0, moved(backs[1], rows, 0)),
        gq0,
        up0,
        tok,
        perm,
        normed0,
        att0,
        gain0,
        qkv_fine,
        where,
    )
    n0 = width // cols
    (packed0,) = call(
        functools.partial(fine_weights_kernel, factor), [((cols, n0 + 16, cwidth), bf16)]
    )(keep0, send0, flip(send0, "row", 1), gain_part0, gain_part1)
    sums0 = scatter_over_columns(packed0)

    x, small = reduce_rows(jnp.concatenate([sums1, sums0[:n0]], axis=0), sums0[n0:])
    gains = small.astype(f32) + flip(small, "row", 1).astype(f32)
    x = lax.all_to_all(jnp.broadcast_to(x, (cols,) + x.shape), "col", 0, 0)
    other = flip(x, "row", 1)
    shapes = [
        (2 * cols, 2 * width // cols, cwidth),
        (2 * cols, cwidth // 2 // cols, 3 * cwidth),
        (2 * cols, cwidth // 2 // cols, cwidth),
        (2 * cols, width // 2 // cols, 3 * width),
        (2 * cols, width // 2 // cols, width),
    ]
    vmem = pl.BlockSpec(memory_space=pltpu.VMEM)
    grads = pl.pallas_call(
        unpack_kernel,
        out_shape=[jax.ShapeDtypeStruct(s, bf16) for s in shapes],
        in_specs=[pl.BlockSpec(memory_space=pltpu.SMEM), vmem, vmem],
        out_specs=[pl.BlockSpec(memory_space=pl.ANY)] * len(shapes),
        scratch_shapes=[pltpu.VMEM(s, bf16) for s in shapes]
        + [pltpu.SemaphoreType.DMA((len(shapes),))],
        compiler_params=pltpu.CompilerParams(vmem_limit_bytes=16 << 20),
    )(where, x, other)
    grad_merge, grad_qkv1, grad_out1, grad_qkv0, grad_out0 = (
        g.reshape(-1, g.shape[2]) for g in grads
    )
    return (
        grad_tokens.reshape(rows, columns, width),
        gains[1, :width],
        grad_qkv0,
        grad_out0,
        grad_merge,
        gains[0],
        grad_qkv1,
        grad_out1,
    )


def solution(mesh):
    in_specs = (
        P("row", "col", None),
        P(),
        P(),
        P(),
        P(),
        P(),
        P(),
        P(),
        P("row", "col", None),
        P("row", "col", None),
    )
    out_specs = (P("row", "col", None), P(), P(), P(), P(), P(), P(), P())
    return jax.shard_map(
        per_device, mesh=mesh, in_specs=in_specs, out_specs=out_specs, check_vma=False
    )
```

time: 221 us -> 194 us (0.88)
  waiting for transfers between devices: 91.1 us -> 64 us
  blocking collectives: 0 us -> 21.1 us
  local copies, waits for them, and re-layouts: 19.3 us -> 1.31 us
  Pallas kernels: 12.8 us -> 29.2 us
  other arithmetic: 12.2 us -> 0.75 us
  starting transfers between devices: 81.7 us -> 74.3 us
    all_to_all x1 -> x0, waiting for transfers between devices: 24 us -> none  [per_device(): lax.all_to_all(jnp.broadcast_to(x, (cols,) + x.shape), 'col', 0, 0)]
    all_to_all x0 -> x1, blocking collectives: none -> 21.1 us  [per_device(): x = lax.all_to_all(jnp.broadcast_to(x, (cols,) + x.shape), 'col', 0, 0)]
    all_to_all x2, waiting for transfers between devices: 26.7 us -> 8.86 us  [scatter_over_columns(): pieces = lax.all_to_all(x, 'col', 0, 0)]
    ppermute x14 -> x12, waiting for transfers between devices: 17.1 us -> 33.6 us  [shifted(): return lax.ppermute(x, axis, pairs)]
    pallas_call x7 -> x11, Pallas kernels: 12.8 us -> 29.2 us  [the longest x10 26.7 us: run(): pl.pallas_call(body, out_shape=[jax.ShapeDtypeStruct(shape, dtype) for sh...]
    ppermute x14 -> x12, starting transfers between devices: 43.6 us -> 32.5 us  [shifted(): return lax.ppermute(x, axis, pairs)]
    concatenate x13 -> x0, other arithmetic: 8.29 us -> none  [the longest x3 2.54 us: whole(): return jnp.concatenate(halves(start, stop, place, length), axis=0)]
    unnamed x89 -> x0, local copies, waits for them, and re-layouts: 7.86 us -> none
  transfers between devices with their start and end apart: 25 -> 23, of which waited for: 17 -> 16; matrix products, arithmetic and copies ran while one was open for 3% -> 1% of each run, Pallas kernels for 1% -> 3%
where the time goes in v3:
time: 194 us; the launch traced here: 192 us
  starting transfers between devices  74.3 us (38%)
  waiting for transfers between devices  64 us (33%)
  Pallas kernels  29.2 us (15%)
  blocking collectives  21.1 us (11%)
    ppermute x12, waiting for transfers between devices, shifted(): return lax.ppermute(x, axis, pairs)  33.6 us
    ppermute x12, starting transfers between devices, shifted(): return lax.ppermute(x, axis, pairs)  32.5 us
    ppermute x9, starting transfers between devices, flip(): lax.ppermute(x, axis, [(i, i ^ bit) for i in range(lax.axis_size(axis))])  29.9 us
    pallas_call x10, Pallas kernels, run(): pl.pallas_call(body, out_shape=[jax.ShapeDtypeStruct(shape, dtype) for sh...  26.7 us
    ppermute x9, waiting for transfers between devices, flip(): lax.ppermute(x, axis, [(i, i ^ bit) for i in range(lax.axis_size(axis))])  21.5 us
    all_to_all x1, blocking collectives, per_device(): x = lax.all_to_all(jnp.broadcast_to(x, (cols,) + x.shape), 'col', 0, 0)  21.1 us
    all_to_all x2, starting transfers between devices, scatter_over_columns(): pieces = lax.all_to_all(x, 'col', 0, 0)  11.9 us
    all_to_all x2, waiting for transfers between devices, scatter_over_columns(): pieces = lax.all_to_all(x, 'col', 0, 0)  8.86 us
  transfers between devices with their start and end apart: 23, of which 16 were waited for; matrix products, arithmetic and copies ran while one was open for 1% of the time, Pallas kernels for 3%

profile of v3, /device:TPU:1, one launch (start us, length us, event | category | flops | bytes accessed | tf_op | source)
XLA Modules:
  0.0 191.8 jit_solution(12705229866741791486)
XLA Ops:
  1.5 4.9 %collective-permute-start = (bf16[176,256]{1,0:T(8,128)(2,1)S(1)}, bf16[176,256]{1,0:T(8,128)(2,1)S(1)}, u32[]{:S(2)}, u32[]{:S(2)}) collective-permute-start(bf16[176,256]{1,0:T(8,128)(2,1)S(1)} %get-tuple-element.49), channel_id=1, source_target_pairs={{0,8},{8,16},{16,24},{24,32},{32,40},{40,48},{48,56},{56,64},{64,7... | collective-permute-start | bytes 270344 | tf_op jit(solution)/shard_map/ppermute | solution.py:26
  8.4 3.9 %collective-permute-done.1.refs_3_.refs_2_.refs_7_ = bf16[176,256]{1,0:T(8,128)(2,1)S(1)} collective-permute-done((bf16[176,256]{1,0:T(8,128)(2,1)S(1)}, bf16[176,256]{1,0:T(8,128)(2,1)S(1)}, u32[]{:S(2)}, u32[]{:S(2)}) %collective-permute-start.1) | collective-permute-done | bytes 90144 | tf_op jit(solution)/shard_map/ppermute | solution.py:26
  18.2 3.7 %collective-permute-done.3.refs_4_.refs_9_ = bf16[144,256]{1,0:T(8,128)(2,1)S(1)} collective-permute-done((bf16[144,256]{1,0:T(8,128)(2,1)S(1)}, bf16[144,256]{1,0:T(8,128)(2,1)S(1)}, u32[]{:S(2)}, u32[]{:S(2)}) %collective-permute-start.3) | collective-permute-done | bytes 73760 | tf_op jit(solution)/shard_map/ppermute | solution.py:26
  21.9 4.3 %shard_map.325 = (bf16[32,1024]{1,0:T(8,128)(2,1)S(1)}, bf16[64,512]{1,0:T(8,128)(2,1)S(1)}, bf16[32,512]{1,0:T(8,128)(2,1)S(1)}, bf16[32,512]{1,0:T(8,128)(2,1)...) custom-call(bf16[128,256]{1,0:T(8,128)(2,1)} %bitcast.17, ...), custom_call_target="tpu_custom_call" | custom-call | flops 268435456 | bytes 4194304 | tf_op jit(solution)/shard_map/pallas_call | solution.py:535
  26.2 3.3 %collective-permute-start.4 = (bf16[32,512]{1,0:T(8,128)(2,1)S(1)}, bf16[32,512]{1,0:T(8,128)(2,1)S(1)}, u32[]{:S(2)}, u32[]{:S(2)}) collective-permute-start(bf16[32,512]{1,0:T(8,128)(2,1)S(1)} %get-tuple-element.54), channel_id=1, source_target_pairs={{0,8},{8,16},{16,24},{24,32},{32,40},{40,48},{48,56},{56,64},{64,7... | collective-permute-start | bytes 98312 | tf_op jit(solution)/shard_map/ppermute | solution.py:26
  31.4 3.3 %collective-permute-done.5.refs_2_ = bf16[32,512]{1,0:T(8,128)(2,1)S(1)} collective-permute-done((bf16[32,512]{1,0:T(8,128)(2,1)S(1)}, bf16[32,512]{1,0:T(8,128)(2,1)S(1)}, u32[]{:S(2)}, u32[]{:S(2)}) %collective-permute-start.5) | collective-permute-done | bytes 32800 | tf_op jit(solution)/shard_map/ppermute | solution.py:26
  40.5 3.7 %collective-permute-done.7.refs_4_ = bf16[96,512]{1,0:T(8,128)(2,1)S(1)} collective-permute-done((bf16[96,512]{1,0:T(8,128)(2,1)S(1)}, bf16[96,512]{1,0:T(8,128)(2,1)S(1)}, u32[]{:S(2)}, u32[]{:S(2)}) %collective-permute-start.7) | collective-permute-done | bytes 98336 | tf_op jit(solution)/shard_map/ppermute | solution.py:26
  44.2 8.2 %shard_map.327 = (bf16[32,1024]{1,0:T(8,128)(2,1)S(1)}, bf16[32,3584]{1,0:T(8,128)(2,1)S(1)}, f32[1,512]{1,0:T(1,128)S(1)}, f32[32,1024]{1,0:T(8,128)S(1)}) custom-call(bf16[64,512]{1,0:T(8,128)(2,1)S(1)} %get-tuple-element.53.refs_0_, bf16[32,512]{1,0:T(8,128)(2,1)S(1)} %collective-permute-done.4.refs_1_, ...), custom_call_target="tpu_custom_call" | custom-call | flops 268435456 | bytes 4194304 | tf_op jit(solution)/shard_map/pallas_call | solution.py:535
  52.5 4.1 %shard_map.328 = (f32[128,256]{1,0:T(8,128)S(1)}, bf16[128,256]{1,0:T(8,128)(2,1)S(1)}, f32[224,512]{1,0:T(8,128)S(1)}, bf16[48,512]{1,0:T(8,128)(2,1)S(1)}, bf16[48,512]{1,0:T(8,128)(2,1)S(1)}) custom-call(bf16[128,256]{1,0:T(8,128)(2,1)} %bitcast.22, f32[32,1024]{1,0:T(8,128)S(1)} %get-tuple-element.59.refs_1_, ...), custom_call_target="tpu_custom_call" | custom-call | flops 268435456 | bytes 4194304 | tf_op jit(solution)/shard_map/pallas_call | solution.py:535
  58.4 6.8 %all-to-all-start = ((bf16[8,192,512]{2,1,0:T(8,128)(2,1)}), bf16[8,192,512]{2,1,0:T(8,128)(2,1)S(1)}, u32[]{:S(2)}, u32[]{:S(2)}) async-start(bf16[8,192,512]{2,1,0:T(8,128)(2,1)} %shard_map.329), calls=%async_computation | async-start | bytes 3145728 | tf_op jit(solution)/shard_map/all_to_all | solution.py:553
  65.2 3.4 %collective-permute-start.9 = (bf16[48,512]{1,0:T(8,128)(2,1)S(1)}, bf16[48,512]{1,0:T(8,128)(2,1)S(1)}, u32[]{:S(2)}, u32[]{:S(2)}) collective-permute-start(bf16[48,512]{1,0:T(8,128)(2,1)S(1)} %get-tuple-element.67), channel_id=1, source_target_pairs={{0,1},{1,2},{2,3},{3,4},{4,5},{5,6},{6,7},{8,9},{9,10},{10,11},{11... | collective-permute-start | bytes 147464 | tf_op jit(solution)/shard_map/ppermute | solution.py:26
  69.8 14.0 %collective-permute-done.9.refs_1_ = bf16[48,512]{1,0:T(8,128)(2,1)S(1)} collective-permute-done((bf16[48,512]{1,0:T(8,128)(2,1)S(1)}, bf16[48,512]{1,0:T(8,128)(2,1)S(1)}, u32[]{:S(2)}, u32[]{:S(2)}) %collective-permute-start.9) | collective-permute-done | bytes 49184 | tf_op jit(solution)/shard_map/ppermute | solution.py:26
  86.4 5.1 %collective-permute-start.11 = (bf16[48,512]{1,0:T(8,128)(2,1)S(1)}, bf16[48,512]{1,0:T(8,128)(2,1)S(1)}, u32[]{:S(2)}, u32[]{:S(2)}) collective-permute-start(bf16[48,512]{1,0:T(8,128)(2,1)S(1)} %get-tuple-element.70), channel_id=1, source_target_pairs={{0,8},{8,16},{16,24},{24,32},{32,40},{40,48},{48,56},{56,64},{64,7... | collective-permute-start | bytes 147464 | tf_op jit(solution)/shard_map/ppermute | solution.py:26
  93.7 3.2 %collective-permute-done.12.refs_2_ = bf16[48,512]{1,0:T(8,128)(2,1)S(1)} collective-permute-done((bf16[48,512]{1,0:T(8,128)(2,1)S(1)}, bf16[48,512]{1,0:T(8,128)(2,1)S(1)}, u32[]{:S(2)}, u32[]{:S(2)}) %collective-permute-start.12) | collective-permute-done | bytes 49184 | tf_op jit(solution)/shard_map/ppermute | solution.py:26
  102.6 5.1 %all-to-all-start.1 = ((bf16[8,48,512]{2,1,0:T(8,128)(2,1)}), bf16[8,48,512]{2,1,0:T(8,128)(2,1)S(1)}, u32[]{:S(2)}, u32[]{:S(2)}) async-start(bf16[8,48,512]{2,1,0:T(8,128)(2,1)} %shard_map.332), calls=%async_computation.1 | async-start | bytes 786432 | tf_op jit(solution)/shard_map/all_to_all | solution.py:553
  107.7 8.9 %all-to-all-done.1 = bf16[8,48,512]{2,1,0:T(8,128)(2,1)S(1)} async-done(((bf16[8,48,512]{2,1,0:T(8,128)(2,1)}), bf16[8,48,512]{2,1,0:T(8,128)(2,1)S(1)}, u32[]{:S(2)}, u32[]{:S(2)}) %all-to-all-start.1) | async-done | bytes 393248 | tf_op jit(solution)/shard_map/all_to_all | solution.py:553
  116.9 3.3 %collective-permute-start.14 = (bf16[128,512]{1,0:T(8,128)(2,1)S(1)}, bf16[128,512]{1,0:T(8,128)(2,1)S(1)}, u32[]{:S(2)}, u32[]{:S(2)}) collective-permute-start(bf16[128,512]{1,0:T(8,128)(2,1)S(1)} %pad_maximum_fusion), channel_id=1, source_target_pairs={{0,16},{8,24},{16,0},{24,8},{32,48},{40,56},{48,32},{56,40},{64,80... | collective-permute-start | bytes 393224 | tf_op jit(solution)/shard_map/ppermute | solution.py:30
  123.3 6.6 %collective-permute-start.15 = (bf16[128,512]{1,0:T(8,128)(2,1)S(1)}, bf16[128,512]{1,0:T(8,128)(2,1)S(1)}, u32[]{:S(2)}, u32[]{:S(2)}) collective-permute-start(bf16[128,512]{1,0:T(8,128)(2,1)S(1)} %add_convert_fusion.3), channel_id=1, source_target_pairs={{0,32},{8,40},{16,48},{24,56},{32,0},{40,8},{48,16},{56,24},{64,96... | collective-permute-start | bytes 393224 | tf_op jit(solution)/shard_map/ppermute | solution.py:30
  129.8 5.8 %collective-permute-done.15 = bf16[128,512]{1,0:T(8,128)(2,1)S(1)} collective-permute-done((bf16[128,512]{1,0:T(8,128)(2,1)S(1)}, bf16[128,512]{1,0:T(8,128)(2,1)S(1)}, u32[]{:S(2)}, u32[]{:S(2)}) %collective-permute-start.15) | collective-permute-done | bytes 131104 | tf_op jit(solution)/shard_map/ppermute | solution.py:30
  135.7 8.7 %collective-permute-start.16 = (bf16[128,512]{1,0:T(8,128)(2,1)S(1)}, bf16[128,512]{1,0:T(8,128)(2,1)S(1)}, u32[]{:S(2)}, u32[]{:S(2)}) collective-permute-start(bf16[128,512]{1,0:T(8,128)(2,1)S(1)} %add_convert_fusion.2), channel_id=1, source_target_pairs={{0,64},{8,72},{16,80},{24,88},{32,96},{40,104},{48,112},{56,120},{... | collective-permute-start | bytes 393224 | tf_op jit(solution)/shard_map/ppermute | solution.py:30
  146.8 3.6 %collective-permute-start.17 = (bf16[128,512]{1,0:T(8,128)(2,1)S(1)}, bf16[128,512]{1,0:T(8,128)(2,1)S(1)}, u32[]{:S(2)}, u32[]{:S(2)}) collective-permute-start(bf16[128,512]{1,0:T(8,128)(2,1)S(1)} %add_convert_fusion.1), channel_id=1, source_target_pairs={{0,128},{8,136},{16,144},{24,152},{32,160},{40,168},{48,176},{56,1... | collective-permute-start | bytes 393224 | tf_op jit(solution)/shard_map/ppermute | solution.py:30
  157.0 21.1 %all_to_all.15.mine = bf16[8,224,512]{2,1,0:T(8,128)(2,1)S(1)} all-to-all(bf16[8,224,512]{2,1,0:T(8,128)(2,1)S(1)} %broadcast_in_dim.11), channel_id=1, replica_groups=mesh['row'=32,'col'=8] {'col'}, dimensions={0} | all-to-all | bytes 3670016 | tf_op jit(solution)/shard_map/all_to_all | solution.py:794
  178.2 6.4 %collective-permute-start.20 = (bf16[8,224,512]{2,1,0:T(8,128)(2,1)S(1)}, bf16[8,224,512]{2,1,0:T(8,128)(2,1)S(1)}, u32[]{:S(2)}, u32[]{:S(2)}) collective-permute-start(bf16[8,224,512]{2,1,0:T(8,128)(2,1)S(1)} %all_to_all.15.mine), channel_id=1, source_target_pairs={{0,8},{8,0},{16,24},{24,16},{32,40},{40,32},{48,56},{56,48},{64,72... | collective-permute-start | bytes 5505032 | tf_op jit(solution)/shard_map/ppermute | solution.py:30
  184.6 3.4 %collective-permute-done.18 = bf16[16,512]{1,0:T(8,128)(2,1)S(1)} collective-permute-done((bf16[16,512]{1,0:T(8,128)(2,1)S(1)}, bf16[16,512]{1,0:T(8,128)(2,1)S(1)}, u32[]{:S(2)}, u32[]{:S(2)}) %collective-permute-start.18) | collective-permute-done | bytes 16416 | tf_op jit(solution)/shard_map/ppermute | solution.py:30
  (52 shorter events, 45.9 us)
Async XLA Ops:
  1.5 6.9 %collective-permute-start = (bf16[176,256]{1,0:T(8,128)(2,1)S(1)}, bf16[176,256]{1,0:T(8,128)(2,1)S(1)}, u32[]{:S(2)}, u32[]{:S(2)}) collective-permute-start(bf16[176,256]{1,0:T(8,128)(2,1)S(1)} %get-tuple-element.49), channel_id=1, source_target_pairs={{0,8},{8,16},{16,24},{24,32},{32,40},{40,48},{48,56},{56,64},{64,7... | collective-permute-start | bytes 270344 | tf_op jit(solution)/shard_map/ppermute | solution.py:26
  6.5 5.8 %collective-permute-start.1 = (bf16[176,256]{1,0:T(8,128)(2,1)S(1)}, bf16[176,256]{1,0:T(8,128)(2,1)S(1)}, u32[]{:S(2)}, u32[]{:S(2)}) collective-permute-start(bf16[176,256]{1,0:T(8,128)(2,1)S(1)} %get-tuple-element.50), channel_id=1, source_target_pairs={{8,0},{16,8},{24,16},{32,24},{40,32},{48,40},{56,48},{64,56},{72,6... | collective-permute-start | bytes 270344 | tf_op jit(solution)/shard_map/ppermute | solution.py:26
  13.7 4.5 %collective-permute-start.2 = (bf16[144,256]{1,0:T(8,128)(2,1)S(1)}, bf16[144,256]{1,0:T(8,128)(2,1)S(1)}, u32[]{:S(2)}, u32[]{:S(2)}) collective-permute-start(bf16[144,256]{1,0:T(8,128)(2,1)S(1)} %get-tuple-element.51), channel_id=1, source_target_pairs={{0,1},{1,2},{2,3},{3,4},{4,5},{5,6},{6,7},{8,9},{9,10},{10,11},{11... | collective-permute-start | bytes 221192 | tf_op jit(solution)/shard_map/ppermute | solution.py:26
  16.8 5.1 %collective-permute-start.3 = (bf16[144,256]{1,0:T(8,128)(2,1)S(1)}, bf16[144,256]{1,0:T(8,128)(2,1)S(1)}, u32[]{:S(2)}, u32[]{:S(2)}) collective-permute-start(bf16[144,256]{1,0:T(8,128)(2,1)S(1)} %get-tuple-element.52), channel_id=1, source_target_pairs={{1,0},{2,1},{3,2},{4,3},{5,4},{6,5},{7,6},{9,8},{10,9},{11,10},{12... | collective-permute-start | bytes 221192 | tf_op jit(solution)/shard_map/ppermute | solution.py:26
  26.2 5.2 %collective-permute-start.4 = (bf16[32,512]{1,0:T(8,128)(2,1)S(1)}, bf16[32,512]{1,0:T(8,128)(2,1)S(1)}, u32[]{:S(2)}, u32[]{:S(2)}) collective-permute-start(bf16[32,512]{1,0:T(8,128)(2,1)S(1)} %get-tuple-element.54), channel_id=1, source_target_pairs={{0,8},{8,16},{16,24},{24,32},{32,40},{40,48},{48,56},{56,64},{64,7... | collective-permute-start | bytes 98312 | tf_op jit(solution)/shard_map/ppermute | solution.py:26
  29.5 5.2 %collective-permute-start.5 = (bf16[32,512]{1,0:T(8,128)(2,1)S(1)}, bf16[32,512]{1,0:T(8,128)(2,1)S(1)}, u32[]{:S(2)}, u32[]{:S(2)}) collective-permute-start(bf16[32,512]{1,0:T(8,128)(2,1)S(1)} %get-tuple-element.55), channel_id=1, source_target_pairs={{8,0},{16,8},{24,16},{32,24},{40,32},{48,40},{56,48},{64,56},{72,6... | collective-permute-start | bytes 98312 | tf_op jit(solution)/shard_map/ppermute | solution.py:26
  35.7 4.7 %collective-permute-start.6 = (bf16[96,512]{1,0:T(8,128)(2,1)S(1)}, bf16[96,512]{1,0:T(8,128)(2,1)S(1)}, u32[]{:S(2)}, u32[]{:S(2)}) collective-permute-start(bf16[96,512]{1,0:T(8,128)(2,1)S(1)} %get-tuple-element.56), channel_id=1, source_target_pairs={{0,1},{1,2},{2,3},{3,4},{4,5},{5,6},{6,7},{8,9},{9,10},{10,11},{11... | collective-permute-start | bytes 294920 | tf_op jit(solution)/shard_map/ppermute | solution.py:26
  38.9 5.4 %collective-permute-start.7 = (bf16[96,512]{1,0:T(8,128)(2,1)S(1)}, bf16[96,512]{1,0:T(8,128)(2,1)S(1)}, u32[]{:S(2)}, u32[]{:S(2)}) collective-permute-start(bf16[96,512]{1,0:T(8,128)(2,1)S(1)} %get-tuple-element.57), channel_id=1, source_target_pairs={{1,0},{2,1},{3,2},{4,3},{5,4},{6,5},{7,6},{9,8},{10,9},{11,10},{12... | collective-permute-start | bytes 294920 | tf_op jit(solution)/shard_map/ppermute | solution.py:26
  52.4 4.2 %collective-permute-start.8 = (bf16[32,3584]{1,0:T(8,128)(2,1)S(1)}, bf16[32,3584]{1,0:T(8,128)(2,1)S(1)}, u32[]{:S(2)}, u32[]{:S(2)}) collective-permute-start(bf16[32,3584]{1,0:T(8,128)(2,1)S(1)} %get-tuple-element.66.refs_1_), channel_id=1, source_target_pairs={{0,8},{8,0},{16,24},{24,16},{32,40},{40,32},{48,56},{56,48},{64,72... | collective-permute-start | bytes 688136 | tf_op jit(solution)/shard_map/ppermute | solution.py:30
  58.4 35.0 %all-to-all-start = ((bf16[8,192,512]{2,1,0:T(8,128)(2,1)}), bf16[8,192,512]{2,1,0:T(8,128)(2,1)S(1)}, u32[]{:S(2)}, u32[]{:S(2)}) async-start(bf16[8,192,512]{2,1,0:T(8,128)(2,1)} %shard_map.329), calls=%async_computation | async-start | bytes 3145728 | tf_op jit(solution)/shard_map/all_to_all | solution.py:553
  65.2 18.7 %collective-permute-start.9 = (bf16[48,512]{1,0:T(8,128)(2,1)S(1)}, bf16[48,512]{1,0:T(8,128)(2,1)S(1)}, u32[]{:S(2)}, u32[]{:S(2)}) collective-permute-start(bf16[48,512]{1,0:T(8,128)(2,1)S(1)} %get-tuple-element.67), channel_id=1, source_target_pairs={{0,1},{1,2},{2,3},{3,4},{4,5},{5,6},{6,7},{8,9},{9,10},{10,11},{11... | collective-permute-start | bytes 147464 | tf_op jit(solution)/shard_map/ppermute | solution.py:26
  68.5 16.7 %collective-permute-start.10 = (bf16[48,512]{1,0:T(8,128)(2,1)S(1)}, bf16[48,512]{1,0:T(8,128)(2,1)S(1)}, u32[]{:S(2)}, u32[]{:S(2)}) collective-permute-start(bf16[48,512]{1,0:T(8,128)(2,1)S(1)} %get-tuple-element.68), channel_id=1, source_target_pairs={{1,0},{2,1},{3,2},{4,3},{5,4},{6,5},{7,6},{9,8},{10,9},{11,10},{12... | collective-permute-start | bytes 147464 | tf_op jit(solution)/shard_map/ppermute | solution.py:26
  86.4 7.3 %collective-permute-start.11 = (bf16[48,512]{1,0:T(8,128)(2,1)S(1)}, bf16[48,512]{1,0:T(8,128)(2,1)S(1)}, u32[]{:S(2)}, u32[]{:S(2)}) collective-permute-start(bf16[48,512]{1,0:T(8,128)(2,1)S(1)} %get-tuple-element.70), channel_id=1, source_target_pairs={{0,8},{8,16},{16,24},{24,32},{32,40},{40,48},{48,56},{56,64},{64,7... | collective-permute-start | bytes 147464 | tf_op jit(solution)/shard_map/ppermute | solution.py:26
  91.5 5.4 %collective-permute-start.12 = (bf16[48,512]{1,0:T(8,128)(2,1)S(1)}, bf16[48,512]{1,0:T(8,128)(2,1)S(1)}, u32[]{:S(2)}, u32[]{:S(2)}) collective-permute-start(bf16[48,512]{1,0:T(8,128)(2,1)S(1)} %get-tuple-element.71), channel_id=1, source_target_pairs={{8,0},{16,8},{24,16},{32,24},{40,32},{48,40},{56,48},{64,56},{72,6... | collective-permute-start | bytes 147464 | tf_op jit(solution)/shard_map/ppermute | solution.py:26
  99.9 1.7 collective-permute-start.13
  102.6 14.0 %all-to-all-start.1 = ((bf16[8,48,512]{2,1,0:T(8,128)(2,1)}), bf16[8,48,512]{2,1,0:T(8,128)(2,1)S(1)}, u32[]{:S(2)}, u32[]{:S(2)}) async-start(bf16[8,48,512]{2,1,0:T(8,128)(2,1)} %shard_map.332), calls=%async_computation.1 | async-start | bytes 786432 | tf_op jit(solution)/shard_map/all_to_all | solution.py:553
  116.9 6.4 %collective-permute-start.14 = (bf16[128,512]{1,0:T(8,128)(2,1)S(1)}, bf16[128,512]{1,0:T(8,128)(2,1)S(1)}, u32[]{:S(2)}, u32[]{:S(2)}) collective-permute-start(bf16[128,512]{1,0:T(8,128)(2,1)S(1)} %pad_maximum_fusion), channel_id=1, source_target_pairs={{0,16},{8,24},{16,0},{24,8},{32,48},{40,56},{48,32},{56,40},{64,80... | collective-permute-start | bytes 393224 | tf_op jit(solution)/shard_map/ppermute | solution.py:30
  123.3 12.4 %collective-permute-start.15 = (bf16[128,512]{1,0:T(8,128)(2,1)S(1)}, bf16[128,512]{1,0:T(8,128)(2,1)S(1)}, u32[]{:S(2)}, u32[]{:S(2)}) collective-permute-start(bf16[128,512]{1,0:T(8,128)(2,1)S(1)} %add_convert_fusion.3), channel_id=1, source_target_pairs={{0,32},{8,40},{16,48},{24,56},{32,0},{40,8},{48,16},{56,24},{64,96... | collective-permute-start | bytes 393224 | tf_op jit(solution)/shard_map/ppermute | solution.py:30
  135.7 11.1 %collective-permute-start.16 = (bf16[128,512]{1,0:T(8,128)(2,1)S(1)}, bf16[128,512]{1,0:T(8,128)(2,1)S(1)}, u32[]{:S(2)}, u32[]{:S(2)}) collective-permute-start(bf16[128,512]{1,0:T(8,128)(2,1)S(1)} %add_convert_fusion.2), channel_id=1, source_target_pairs={{0,64},{8,72},{16,80},{24,88},{32,96},{40,104},{48,112},{56,120},{... | collective-permute-start | bytes 393224 | tf_op jit(solution)/shard_map/ppermute | solution.py:30
  146.8 5.9 %collective-permute-start.17 = (bf16[128,512]{1,0:T(8,128)(2,1)S(1)}, bf16[128,512]{1,0:T(8,128)(2,1)S(1)}, u32[]{:S(2)}, u32[]{:S(2)}) collective-permute-start(bf16[128,512]{1,0:T(8,128)(2,1)S(1)} %add_convert_fusion.1), channel_id=1, source_target_pairs={{0,128},{8,136},{16,144},{24,152},{32,160},{40,168},{48,176},{56,1... | collective-permute-start | bytes 393224 | tf_op jit(solution)/shard_map/ppermute | solution.py:30
  152.8 4.0 %collective-permute-start.19 = (bf16[112,512]{1,0:T(8,128)(2,1)S(1)}, bf16[112,512]{1,0:T(8,128)(2,1)S(1)}, u32[]{:S(2)}, u32[]{:S(2)}) collective-permute-start(bf16[112,512]{1,0:T(8,128)(2,1)S(1)} %slice.28), channel_id=1, source_target_pairs={{0,16},{8,24},{16,0},{24,8},{32,48},{40,56},{48,32},{56,40},{64,80... | collective-permute-start | bytes 344072 | tf_op jit(solution)/shard_map/ppermute | solution.py:30
  178.2 11.0 %collective-permute-start.20 = (bf16[8,224,512]{2,1,0:T(8,128)(2,1)S(1)}, bf16[8,224,512]{2,1,0:T(8,128)(2,1)S(1)}, u32[]{:S(2)}, u32[]{:S(2)}) collective-permute-start(bf16[8,224,512]{2,1,0:T(8,128)(2,1)S(1)} %all_to_all.15.mine), channel_id=1, source_target_pairs={{0,8},{8,0},{16,24},{24,16},{32,40},{40,32},{48,56},{56,48},{64,72... | collective-permute-start | bytes 5505032 | tf_op jit(solution)/shard_map/ppermute | solution.py:30
  184.6 3.4 %collective-permute-start.18 = (bf16[16,512]{1,0:T(8,128)(2,1)S(1)}, bf16[16,512]{1,0:T(8,128)(2,1)S(1)}, u32[]{:S(2)}, u32[]{:S(2)}) collective-permute-start(bf16[16,512]{1,0:T(8,128)(2,1)S(1)} %slice.26), channel_id=1, source_target_pairs={{0,8},{8,0},{16,24},{24,16},{32,40},{40,32},{48,56},{56,48},{64,72... | collective-permute-start | bytes 49160 | tf_op jit(solution)/shard_map/ppermute | solution.py:30

commit v4 on v3

--- a/solution.py
+++ b/solution.py
@@ -233,7 +233,7 @@
 
 def fine_forward_kernel(
     tok, up, down, left, right, perm, perm_rim, gain, w_qkv, w_out, w_merge, band, at, where,
-    merged_out, near_out, down_out, up_out, normed_out, proj_out, kv_out, att_out,
+    merged_out, near_out, down_out, up_out, field_out, proj_out, kv_out, att_out,
 ):
     width = tok.shape[1]
     count, rim = perm.shape[0], perm_rim.shape[0]
@@ -247,7 +247,7 @@
         [inner, up[: far - rim], down[rim:far], left[:side], right[:side]], axis=0
     )
     _, _, normed = norm_forward(field, gain[...])
-    normed_out[...] = normed[:count]
+    field_out[...] = field
     asked = inner.shape[0]
     query = dot(normed[:asked], w_qkv[:, :width]).astype(bf16)
     kv = dot(normed, w_qkv[:, width:]).astype(bf16)
@@ -286,9 +286,18 @@
     up_out[half:] = near[quarter + small :]
 
 
+def coarse_upstream_kernel(gc, gup, gdown, gleft, gright, gpick, w_out, up_out, att_out):
+    own = gc.shape[0]
+    tall, wide = gup.shape[0] - 2 * own, gleft.shape[0] - 2 * (gpick.shape[1] - 3 * own) // 2
+    given = [gc[...], join_rows(gup[tall:]), join_rows(gdown[tall:])]
+    given += [join_rows(gleft[wide:]), join_rows(gright[wide:])]
+    u_b = dot(gpick[...], jnp.concatenate(given, axis=0)).astype(bf16)
+    up_out[...] = u_b[:own]
+    att_out[...] = dot_nt(u_b, w_out[...]).astype(bf16)
+
+
 def coarse_kernel(
-    near, up, down, left, right, gc, gup, gdown, gleft, gright, merged, pick, gpick,
-    gain, w_qkv, w_out, w_merge, band, at, where,
+    near, up, down, left, right, upstream, grad_out, merged, pick, gain, w_qkv, w_merge, band, at, where,
     keep_out, send_out, gain_out, grad_merged_out,
 ):
     own, width = merged.shape[0], near.shape[1]
@@ -298,11 +307,7 @@
     kv = dot(normed, w_qkv[:, width:]).astype(bf16)
     picked = dot(pick[...], normed).astype(bf16)
     query = dot(picked, w_qkv[:, :width]).astype(bf16)
-    tall, wide = gup.shape[0] - 2 * own, gleft.shape[0] - 2 * (gpick.shape[1] - 3 * own) // 2
-    given = [gc[...], join_rows(gup[tall:]), join_rows(gdown[tall:])]
-    given += [join_rows(gleft[wide:]), join_rows(gright[wide:])]
-    u_b = dot(gpick[...], jnp.concatenate(given, axis=0)).astype(bf16)
-    grad_att = dot_nt(u_b, w_out[...]).astype(bf16)
+    u_b, grad_att = upstream[...], grad_out[...]
     bias = band[...] + validity(at[...], where, TILE[0] // 2, TILE[1] // 2)
     masks = head_masks()
     att, gq, gk, gv = [], [], [], []
@@ -329,7 +334,7 @@
     grad_normed = dot_nt(grad_proj, w_qkv[...])
     grad_in, gain_part = norm_backward(values[:own], scale[:own], gain[...], grad_normed)
     gain_out[...] = gain_part
-    c_b = (u_b[:own].astype(f32) + grad_in).astype(bf16)
+    c_b = (u_b.astype(f32) + grad_in).astype(bf16)
     grad_merged_out[...] = dot_nt(c_b, w_merge[...])
     first = where[0] % 2 == 0
     place = 0
@@ -339,12 +344,12 @@
         keep_out[:, place : place + half] = jnp.where(first, low, high).astype(bf16)
         send_out[:, place : place + half] = jnp.where(first, high, low).astype(bf16)
         place += half
-    for g in (c_b, grad_proj, u_b[:own]):
+    for g in (c_b, grad_proj, u_b):
         send_out[:, place : place + g.shape[1]] = g
         place += g.shape[1]
 
 
-def coarse_weights_kernel(factor, keep, sent, got, out):
+def weights_kernel(factor, keep, sent, got, fine_keep, fine_got, gain, cgain, out):
     half = keep.shape[1]
     cols = out.shape[2]
     x = jnp.concatenate([keep[...], got[:, :half]], axis=0)
@@ -360,23 +365,38 @@
         for j in range(out.shape[0]):
             out[j, place : place + rows] = part[j * rows : (j + 1) * rows]
         place += rows
+    fine = add_b(fine_keep[...], fine_got[...])
+    half = fine.shape[0] // 2
+    rows = half // out.shape[0]
+    padded = jnp.concatenate([gain[...], jnp.zeros((1, cols - gain.shape[1]), f32)], axis=1)
+    gains = jnp.concatenate([cgain[...], padded, jnp.zeros((14, cols), f32)], axis=0)
+    gains = (gains * factor).astype(bf16)
+    for j in range(out.shape[0]):
+        out[j, place : place + rows] = fine[j * rows : (j + 1) * rows]
+        out[j, place + rows : place + 2 * rows] = fine[half + j * rows : half + (j + 1) * rows]
+        out[j, place + 2 * rows :] = gains
 
 
 def fine_backward_kernel(
-    grad_fine, grad_merged, perm, query_in, kv_in, pick, w_out, band, at, where,
-    up_out, gq_out, mid_out, left_out, right_out,
+    factor,
+    grad_fine, grad_merged, perm, query_in, kv_in, field, att, pick, w_out, w_qkv, gain, band,
+    at, where,
+    up_out, gq_out, mid_out, left_out, right_out, gain_out, keep_out, send_out,
 ):
     width = grad_fine.shape[1]
     pairs = width // PAIR
     total = jnp.concatenate([grad_merged[:, p * width : (p + 1) * width] for p in range(4)], axis=0)
     up = dot(perm[...], grad_fine[...]) + total
     up_out[...] = up
-    grad_att = dot_nt(up.astype(bf16), w_out[...]).astype(bf16)
+    up_b = up.astype(bf16)
+    grad_att = dot_nt(up_b, w_out[...]).astype(bf16)
     query = query_in[...]
     kv = dot(pick[...], kv_in[...]).astype(bf16)
+    values, scale, normed = norm_forward(dot(pick[...], field[...]), gain[...])
     bias = band[...] + validity(at[...], where, *TILE)
     masks = head_masks()
     middle, side = mid_out.shape[0], left_out.shape[0]
+    gq, gk, gv = [], [], []
     for p in range(pairs):
         keys, vals = lanes(kv, p), lanes(kv, pairs + p)
         q, g = lanes(query, p), lanes(grad_att, p)
@@ -391,12 +411,35 @@
                 dot_tn(prob.astype(bf16), gm),
             )
             sums = new if sums is None else tuple(a + b for a, b in zip(sums, new))
-        gq_out[:, p * PAIR : (p + 1) * PAIR] = sums[0].astype(bf16)
-        for part, at in ((sums[1], p), (sums[2], pairs + p)):
-            where = slice(at * PAIR, (at + 1) * PAIR)
-            mid_out[:, where] = part[:middle]
-            left_out[:, where] = part[middle : middle + side].astype(bf16)
-            right_out[:, where] = part[middle + side :].astype(bf16)
+        gq.append(sums[0].astype(bf16))
+        gk.append(sums[1])
+        gv.append(sums[2])
+    grad_query = jnp.concatenate(gq, axis=1)
+    grad_kv = jnp.concatenate(gk + gv, axis=1)
+    grad_b = grad_kv.astype(bf16)
+    gq_out[...] = grad_query
+    mid_out[...] = grad_kv[:middle]
+    left_out[...] = grad_b[middle : middle + side]
+    right_out[...] = grad_b[middle + side :]
+    own = query.shape[0]
+    grad_normed = dot_nt(grad_b, w_qkv[:, width:])
+    own_normed = dot_nt(grad_query, w_qkv[:, :width])
+    ratio = values * scale
+    gain_out[...] = jnp.sum(grad_normed * ratio, axis=0, keepdims=True) + jnp.sum(
+        own_normed * ratio[:own], axis=0, keepdims=True
+    )
+    wq = dot_tn(normed[:own], grad_query) * factor
+    wkv = dot_tn(normed, grad_b) * factor
+    wo = dot_tn(att[...], up_b) * factor
+    half = width // 2
+    first = where[0] % 2 == 0
+    blocks = []
+    for rows in (slice(0, half), slice(half, width)):
+        high = jnp.concatenate([wq[rows], wkv[rows, :width]], axis=1)
+        low = jnp.concatenate([wkv[rows, width:], wo[rows]], axis=1)
+        blocks.append(jnp.concatenate([high, low], axis=0))
+    keep_out[...] = jnp.where(first, blocks[0], blocks[1]).astype(bf16)
+    send_out[...] = jnp.where(first, blocks[1], blocks[0]).astype(bf16)
 
 
 def fine_fold_kernel(mid, from_left, from_right, place_left, place_right, own_out, top_out, bottom_out):
@@ -408,46 +451,13 @@
 
 
 def fine_last_kernel(
-    own, from_above, from_below, place_above, place_below, gq, up, tok, perm, normed, att, gain, w_qkv, where,
-    grad_out, gain_out, keep_out, send_out,
+    own, from_above, from_below, place_above, place_below, gq, up, tok, perm, gain, w_qkv, grad_out
 ):
-    width = tok.shape[1]
     kv = own[...] + dot(place_above[...], from_above[...]) + dot(place_below[...], from_below[...])
     grad_proj = jnp.concatenate([gq[...], kv.astype(bf16)], axis=1)
     values, scale, _ = norm_forward(dot(perm[...], tok[...]), gain[...])
-    grad_in, gain_part = norm_backward(values, scale, gain[...], dot_nt(grad_proj, w_qkv[...]))
-    gain_out[...] = gain_part
+    grad_in, _ = norm_backward(values, scale, gain[...], dot_nt(grad_proj, w_qkv[...]))
     grad_out[...] = dot_tn(perm[...], (up[...] + grad_in).astype(bf16)).astype(bf16)
-    first = where[0] % 2 == 0
-    half = width // 2
-    place = 0
-    for x in (normed[...], att[...]):
-        low, high = x[:, :half].astype(f32), x[:, half:].astype(f32)
-        keep_out[:, place : place + half] = jnp.where(first, low, high).astype(bf16)
-        send_out[:, place : place + half] = jnp.where(first, high, low).astype(bf16)
-        place += half
-    send_out[:, place : place + 3 * width] = grad_proj
-    send_out[:, place + 3 * width :] = up[...].astype(bf16)
-
-
-def fine_weights_kernel(factor, keep, sent, got, gain, cgain, out):
-    wide = keep.shape[1]
-    half = wide // 2
-    x = jnp.concatenate([keep[...], got[:, :wide]], axis=0)
-    g = jnp.concatenate([sent[:, wide:], got[:, wide:]], axis=0)
-    qkv = (dot_tn(x[:, :half], g[:, : 3 * wide]) * factor).astype(bf16)
-    last = (dot_tn(x[:, half:], g[:, 3 * wide :]) * factor).astype(bf16)
-    rows = half // out.shape[0]
-    zeros = jnp.zeros((14, 2 * wide), f32)
-    padded = jnp.concatenate([gain[...], jnp.zeros((1, wide), f32)], axis=1)
-    gains = jnp.concatenate([cgain[...], padded, zeros], axis=0)
-    gains = (gains * factor).astype(bf16)
-    for j in range(out.shape[0]):
-        at = slice(j * rows, (j + 1) * rows)
-        out[j, :rows] = qkv[at, : 2 * wide]
-        out[j, rows : 2 * rows, :wide] = qkv[at, 2 * wide :]
-        out[j, rows : 2 * rows, wide:] = last[at]
-        out[j, 2 * rows :] = gains
 
 
 def unpack_kernel(where, mine, other, merge, qkv1, out1, qkv0, out0, *scratch):
@@ -554,20 +564,20 @@
     return jnp.sum(pieces.reshape(count, -1, x.shape[-1]).astype(f32), axis=0).astype(bf16)
 
 
-def reduce_rows(x, small):
-    half = x.shape[0] // 2
-    mine = (lax.axis_index("row") // 2) % 2
-    keep = lax.dynamic_slice_in_dim(x, mine * half, half, axis=0)
-    send = lax.dynamic_slice_in_dim(x, (1 - mine) * half, half, axis=0)
-    got = flip(jnp.concatenate([send, small], axis=0), "row", 2)
-    x = add_b(jnp.concatenate([keep, small], axis=0), got)
-    bit = 4
-    while bit < lax.axis_size("row"):
-        x = add_b(x, flip(x, "row", bit))
-        bit *= 2
-    x, small = x[:half], x[half:]
-    other = flip(x, "row", 2)
-    return jnp.where(mine == 0, jnp.concatenate([x, other]), jnp.concatenate([other, x])), small
+def trade_rows(pieces):
+    count = lax.axis_size("row") // 2
+    groups = [[2 * i + core for i in range(count)] for core in (0, 1)]
+    return lax.all_to_all(pieces, "row", 0, 0, axis_index_groups=groups)
+
+
+def scatter_over_rows(x):
+    pieces = trade_rows(x.reshape(lax.axis_size("row") // 2, -1, x.shape[1]))
+    return jnp.sum(pieces.astype(f32), axis=0).astype(bf16)
+
+
+def gather_over_rows(x):
+    count = lax.axis_size("row") // 2
+    return trade_rows(jnp.broadcast_to(x, (count,) + x.shape)).reshape(-1, x.shape[1])
 
 
 def per_device(
@@ -633,14 +643,14 @@
     asked0 = joined(keys0[:3])
     perm = chosen(own0, natural)
     near = len(keys0[1])
-    merged, near1, down1, up1, normed0, query0, kv0, att0 = call(
+    merged, near1, down1, up1, field0, query0, kv0, att0 = call(
         fine_forward_kernel,
         [
             ((ccount, 4 * width), bf16),
             ((ccount + near // 2, cwidth), bf16),
             ((ccount, cwidth), bf16),
             ((ccount, cwidth), bf16),
-            ((count, width), bf16),
+            ((len(flat0), width), bf16),
             ((count, width), bf16),
             ((len(flat0), 2 * width), bf16),
             ((count, width), bf16),
@@ -678,6 +688,18 @@
     right1 = shifted(send_left, "col", -1)
 
     flat1, ask1 = joined(keys1), joined(queries1)
+    upstream1, grad_att1 = call(
+        coarse_upstream_kernel,
+        [((ccount, cwidth), bf16), ((len(ask1), cwidth), bf16)],
+    )(
+        gc,
+        up,
+        down,
+        left,
+        right,
+        chosen(ask1, cheld + queries1[3] + queries1[4]),
+        out_coarse,
+    )
     kept = (4 * width + 2 * cwidth) // 2
     keep1, send1, gain_part1, grad_merged = call(
         coarse_kernel,
@@ -693,40 +715,35 @@
         below1,
         left1,
         right1,
-        gc,
-        up,
-        down,
-        left,
-        right,
+        upstream1,
+        grad_att1,
         merged,
         chosen(ask1, flat1),
-        chosen(ask1, cheld + queries1[3] + queries1[4]),
         gain1,
         qkv_coarse,
-        out_coarse,
         w_merge,
         Late(jnp.asarray(band_bias(ask1, flat1))),
         places(flat1),
         where,
     )
-    n1 = (2 * width + 4 * (cwidth // 2)) // cols
-    (packed1,) = call(
-        functools.partial(coarse_weights_kernel, factor), [((cols, n1, cwidth), bf16)]
-    )(keep1, send1, flip(send1, "row", 1))
+    got1 = flip(send1, "row", 1)
 
     backs = back_keys(rows, columns)
     flatb = joined(backs)
     rims = len(backs[1])
     bside = len(backs[3])
     middle = count + 2 * rims
-    up0, gq0, mid, left_rim, right_rim = call(
-        fine_backward_kernel,
+    up0, gq0, mid, left_rim, right_rim, gain_part0, keep0, send0 = call(
+        functools.partial(fine_backward_kernel, factor),
         [
             ((count, width), f32),
             ((count, width), bf16),
             ((middle, 2 * width), f32),
             ((bside, 2 * width), bf16),
             ((bside, 2 * width), bf16),
+            ((1, width), f32),
+            ((width, 2 * width), bf16),
+            ((width, 2 * width), bf16),
         ],
     )(
         Late(grad_fine.reshape(count, width)),
@@ -734,16 +751,26 @@
         perm,
         query0,
         kv0,
+        field0,
+        att0,
         chosen(flatb, flat0),
         out_fine,
+        qkv_fine,
+        gain0,
         Late(jnp.asarray(band_bias(own0, flatb))),
         places(flatb),
         where,
     )
-    left_rim, right_rim, packed1 = lax.optimization_barrier((left_rim, right_rim, packed1))
-    sums1 = scatter_over_columns(packed1)
+    n1 = (2 * width + 4 * (cwidth // 2)) // cols
+    n0 = width // cols
+    (packed,) = call(
+        functools.partial(weights_kernel, factor), [((cols, n1 + n0 + 16, cwidth), bf16)]
+    )(keep1, send1, got1, keep0, flip(send0, "row", 1), gain_part0, gain_part1)
+    sums = scatter_over_columns(packed)
     from_right = shifted(left_rim, "col", -1)
     from_left = shifted(right_rim, "col", 1)
+    sums, from_left, from_right = lax.optimization_barrier((sums, from_left, from_right))
+    sums = scatter_over_rows(sums)
     mids = joined(backs[:3])
     own, top_rim, bottom_rim = call(
         fine_fold_kernel,
@@ -756,16 +783,14 @@
         chosen(mids, moved(backs[4], 0, -columns)),
         chosen(mids, moved(backs[3], 0, columns)),
     )
+    x = gather_over_rows(sums)
+    x, top_rim, bottom_rim = lax.optimization_barrier((x, top_rim, bottom_rim))
     from_below = shifted(top_rim, "row", -1)
     from_above = shifted(bottom_rim, "row", 1)
-    from_above, from_below, sums1 = lax.optimization_barrier((from_above, from_below, sums1))
-    grad_tokens, gain_part0, keep0, send0 = call(
+    (grad_tokens,) = call(
         fine_last_kernel,
         [
             ((count, width), bf16),
-            ((1, width), f32),
-            ((count, width), bf16),
-            ((count, 5 * width), bf16),
         ],
     )(
         own,
@@ -777,21 +802,13 @@
         up0,
         tok,
         perm,
-        normed0,
-        att0,
         gain0,
         qkv_fine,
-        where,
-    )
-    n0 = width // cols
-    (packed0,) = call(
-        functools.partial(fine_weights_kernel, factor), [((cols, n0 + 16, cwidth), bf16)]
-    )(keep0, send0, flip(send0, "row", 1), gain_part0, gain_part1)
-    sums0 = scatter_over_columns(packed0)
-
-    x, small = reduce_rows(jnp.concatenate([sums1, sums0[:n0]], axis=0), sums0[n0:])
+    )
+    x, small = x[:-16], x[-16:]
     gains = small.astype(f32) + flip(small, "row", 1).astype(f32)
     x = lax.all_to_all(jnp.broadcast_to(x, (cols,) + x.shape), "col", 0, 0)
+    x, grad_tokens = lax.optimization_barrier((x, grad_tokens))
     other = flip(x, "row", 1)
     shapes = [
         (2 * cols, 2 * width // cols, cwidth),

time: 194 us -> 173 us (0.89)
  starting transfers between devices: 74.3 us -> 54.1 us
  waiting for transfers between devices: 64 us -> 60.3 us
  local copies, waits for them, and re-layouts: 1.31 us -> 3.49 us
    ppermute x9 -> x4, starting transfers between devices: 29.9 us -> 1.45 us  [flip(): lax.ppermute(x, axis, [(i, i ^ bit) for i in range(lax.axis_size(axis))])]
    ppermute x9 -> x4, waiting for transfers between devices: 21.5 us -> 4.79 us  [flip(): lax.ppermute(x, axis, [(i, i ^ bit) for i in range(lax.axis_size(axis))])]
    all_to_all x0 -> x2, waiting for transfers between devices: none -> 16.4 us  [the longest x1 8.29 us: trade_rows(): return lax.all_to_all(pieces, 'row', 0, 0, axis_index_groups=groups)]
    ppermute x12, waiting for transfers between devices: 33.6 us -> 18 us  [shifted(): return lax.ppermute(x, axis, pairs)]
    all_to_all x2 -> x1, waiting for transfers between devices: 8.86 us -> 21.2 us  [scatter_over_columns(): pieces = lax.all_to_all(x, 'col', 0, 0)]
    all_to_all x0 -> x2, starting transfers between devices: none -> 10.5 us  [the longest x1 5.29 us: trade_rows(): return lax.all_to_all(pieces, 'row', 0, 0, axis_index_groups=groups)]
    all_to_all x2 -> x1, starting transfers between devices: 11.9 us -> 6.77 us  [scatter_over_columns(): pieces = lax.all_to_all(x, 'col', 0, 0)]
    ppermute x12, starting transfers between devices: 32.5 us -> 35.4 us  [shifted(): return lax.ppermute(x, axis, pairs)]
  transfers between devices with their start and end apart: 23 -> 19, of which waited for: 16 -> 11; matrix products, arithmetic and copies ran while one was open for 1% -> 2% of each run, Pallas kernels for 3% -> 3%
where the time goes in v4:
time: 173 us; the launch traced here: 172 us
  waiting for transfers between devices  60.3 us (35%)
  starting transfers between devices  54.1 us (31%)
  Pallas kernels  29.5 us (17%)
  blocking collectives  21.7 us (13%)
  local copies, waits for them, and re-layouts  3.49 us (2%)
  other arithmetic  2.03 us (1%)
    ppermute x12, starting transfers between devices, shifted(): return lax.ppermute(x, axis, pairs)  35.4 us
    pallas_call x10, Pallas kernels, run(): pl.pallas_call(body, out_shape=[jax.ShapeDtypeStruct(shape, dtype) for sh...  27 us
    all_to_all x1, blocking collectives, trade_rows(): return lax.all_to_all(pieces, 'row', 0, 0, axis_index_groups=groups)  21.7 us
    all_to_all x1, waiting for transfers between devices, scatter_over_columns(): pieces = lax.all_to_all(x, 'col', 0, 0)  21.2 us
    ppermute x12, waiting for transfers between devices, shifted(): return lax.ppermute(x, axis, pairs)  18 us
    all_to_all x1, waiting for transfers between devices, trade_rows(): return lax.all_to_all(pieces, 'row', 0, 0, axis_index_groups=groups)  8.29 us
    all_to_all x1, waiting for transfers between devices, per_device(): x = lax.all_to_all(jnp.broadcast_to(x, (cols,) + x.shape), 'col', 0, 0)  8.07 us
    all_to_all x1, starting transfers between devices, scatter_over_columns(): pieces = lax.all_to_all(x, 'col', 0, 0)  6.77 us
  transfers between devices with their start and end apart: 19, of which 11 were waited for; matrix products, arithmetic and copies ran while one was open for 2% of the time, Pallas kernels for 3%

profile of v4, /device:TPU:1, one launch (start us, length us, event | category | flops | bytes accessed | tf_op | source)
XLA Modules:
  0.0 172.2 jit_solution(17612027137578301862)
XLA Ops:
  1.5 4.9 %collective-permute-start = (bf16[176,256]{1,0:T(8,128)(2,1)S(1)}, bf16[176,256]{1,0:T(8,128)(2,1)S(1)}, u32[]{:S(2)}, u32[]{:S(2)}) collective-permute-start(bf16[176,256]{1,0:T(8,128)(2,1)S(1)} %get-tuple-element.52), channel_id=1, source_target_pairs={{0,8},{8,16},{16,24},{24,32},{32,40},{40,48},{48,56},{56,64},{64,7... | collective-permute-start | bytes 270344 | tf_op jit(solution)/shard_map/ppermute | solution.py:26
  8.4 3.9 %collective-permute-done.1.refs_3_.refs_2_ = bf16[176,256]{1,0:T(8,128)(2,1)S(1)} collective-permute-done((bf16[176,256]{1,0:T(8,128)(2,1)S(1)}, bf16[176,256]{1,0:T(8,128)(2,1)S(1)}, u32[]{:S(2)}, u32[]{:S(2)}) %collective-permute-start.1) | collective-permute-done | bytes 90144 | tf_op jit(solution)/shard_map/ppermute | solution.py:26
  13.7 3.1 %collective-permute-start.2 = (bf16[144,256]{1,0:T(8,128)(2,1)S(1)}, bf16[144,256]{1,0:T(8,128)(2,1)S(1)}, u32[]{:S(2)}, u32[]{:S(2)}) collective-permute-start(bf16[144,256]{1,0:T(8,128)(2,1)S(1)} %get-tuple-element.54), channel_id=1, source_target_pairs={{0,1},{1,2},{2,3},{3,4},{4,5},{5,6},{6,7},{8,9},{9,10},{10,11},{11... | collective-permute-start | bytes 221192 | tf_op jit(solution)/shard_map/ppermute | solution.py:26
  18.2 3.7 %collective-permute-done.3.refs_4_ = bf16[144,256]{1,0:T(8,128)(2,1)S(1)} collective-permute-done((bf16[144,256]{1,0:T(8,128)(2,1)S(1)}, bf16[144,256]{1,0:T(8,128)(2,1)S(1)}, u32[]{:S(2)}, u32[]{:S(2)}) %collective-permute-start.3) | collective-permute-done | bytes 73760 | tf_op jit(solution)/shard_map/ppermute | solution.py:26
  21.9 4.3 %shard_map.325 = (bf16[32,1024]{1,0:T(8,128)(2,1)S(1)}, bf16[64,512]{1,0:T(8,128)(2,1)S(1)}, bf16[32,512]{1,0:T(8,128)(2,1)S(1)}, bf16[32,512]{1,0:T(8,128)(2,1)...) custom-call(bf16[128,256]{1,0:T(8,128)(2,1)} %bitcast.17, ...), custom_call_target="tpu_custom_call" | custom-call | flops 268435456 | bytes 4194304 | tf_op jit(solution)/shard_map/pallas_call | solution.py:545
  26.2 3.3 %collective-permute-start.4 = (bf16[32,512]{1,0:T(8,128)(2,1)S(1)}, bf16[32,512]{1,0:T(8,128)(2,1)S(1)}, u32[]{:S(2)}, u32[]{:S(2)}) collective-permute-start(bf16[32,512]{1,0:T(8,128)(2,1)S(1)} %get-tuple-element.57), channel_id=1, source_target_pairs={{0,8},{8,16},{16,24},{24,32},{32,40},{40,48},{48,56},{56,64},{64,7... | collective-permute-start | bytes 98312 | tf_op jit(solution)/shard_map/ppermute | solution.py:26
  31.4 3.3 %collective-permute-done.5.refs_2_ = bf16[32,512]{1,0:T(8,128)(2,1)S(1)} collective-permute-done((bf16[32,512]{1,0:T(8,128)(2,1)S(1)}, bf16[32,512]{1,0:T(8,128)(2,1)S(1)}, u32[]{:S(2)}, u32[]{:S(2)}) %collective-permute-start.5) | collective-permute-done | bytes 32800 | tf_op jit(solution)/shard_map/ppermute | solution.py:26
  35.7 3.1 %collective-permute-start.6 = (bf16[96,512]{1,0:T(8,128)(2,1)S(1)}, bf16[96,512]{1,0:T(8,128)(2,1)S(1)}, u32[]{:S(2)}, u32[]{:S(2)}) collective-permute-start(bf16[96,512]{1,0:T(8,128)(2,1)S(1)} %get-tuple-element.59), channel_id=1, source_target_pairs={{0,1},{1,2},{2,3},{3,4},{4,5},{5,6},{6,7},{8,9},{9,10},{10,11},{11... | collective-permute-start | bytes 294920 | tf_op jit(solution)/shard_map/ppermute | solution.py:26
  41.6 2.6 %collective-permute-done.7.refs_4_ = bf16[96,512]{1,0:T(8,128)(2,1)S(1)} collective-permute-done((bf16[96,512]{1,0:T(8,128)(2,1)S(1)}, bf16[96,512]{1,0:T(8,128)(2,1)S(1)}, u32[]{:S(2)}, u32[]{:S(2)}) %collective-permute-start.7) | collective-permute-done | bytes 98336 | tf_op jit(solution)/shard_map/ppermute | solution.py:26
  44.2 7.6 %shard_map.328 = (bf16[32,1024]{1,0:T(8,128)(2,1)S(1)}, bf16[32,3584]{1,0:T(8,128)(2,1)S(1)}, f32[1,512]{1,0:T(1,128)S(1)}, f32[32,1024]{1,0:T(8,128)S(1)}) custom-call(bf16[64,512]{1,0:T(8,128)(2,1)S(1)} %get-tuple-element.56.refs_0_, bf16[32,512]{1,0:T(8,128)(2,1)S(1)} %collective-permute-done.4.refs_1_, ...), custom_call_target="tpu_custom_call" | custom-call | flops 268435456 | bytes 4194304 | tf_op jit(solution)/shard_map/pallas_call | solution.py:545
  51.9 4.9 %shard_map.329 = (f32[128,256]{1,0:T(8,128)S(1)}, bf16[128,256]{1,0:T(8,128)(2,1)S(1)}, f32[224,512]{1,0:T(8,128)S(1)}, bf16[48,512]{1,0:T(8,128)(2,1)S(1)}, bf1...) custom-call(bf16[128,256]{1,0:T(8,128)(2,1)} %bitcast.22, ...), custom_call_target="tpu_custom_call" | custom-call | flops 268435456 | bytes 4194304 | tf_op jit(solution)/shard_map/pallas_call | solution.py:545
  60.7 6.8 %all-to-all-start = ((bf16[8,240,512]{2,1,0:T(8,128)(2,1)}), bf16[8,240,512]{2,1,0:T(8,128)(2,1)}, u32[]{:S(2)}, u32[]{:S(2)}) async-start(bf16[8,240,512]{2,1,0:T(8,128)(2,1)} %shard_map.330), calls=%async_computation | async-start | bytes 3932160 | tf_op jit(solution)/shard_map/all_to_all | solution.py:563
  67.4 3.4 %collective-permute-start.10 = (bf16[48,512]{1,0:T(8,128)(2,1)S(1)}, bf16[48,512]{1,0:T(8,128)(2,1)S(1)}, u32[]{:S(2)}, u32[]{:S(2)}) collective-permute-start(bf16[48,512]{1,0:T(8,128)(2,1)S(1)} %get-tuple-element.75), channel_id=1, source_target_pairs={{0,1},{1,2},{2,3},{3,4},{4,5},{5,6},{6,7},{8,9},{9,10},{10,11},{11... | collective-permute-start | bytes 147464 | tf_op jit(solution)/shard_map/ppermute | solution.py:26
  72.1 21.2 %all-to-all-done = bf16[8,240,512]{2,1,0:T(8,128)(2,1)} async-done(((bf16[8,240,512]{2,1,0:T(8,128)(2,1)}), bf16[8,240,512]{2,1,0:T(8,128)(2,1)}, u32[]{:S(2)}, u32[]{:S(2)}) %all-to-all-start) | async-done | bytes 1966112 | tf_op jit(solution)/shard_map/all_to_all | solution.py:563
  96.0 21.7 %all_to_all.20 = bf16[16,15,512]{2,1,0:T(8,128)(2,1)S(1)} all-to-all(bf16[16,15,512]{2,1,0:T(8,128)(2,1)S(1)} %reshape.52), channel_id=1, replica_groups={{0,16,32,48,64,80,96,112,128,144,160,176,192,208,224,240},{8,24,40,56,7..., dimensions={0} | all-to-all | bytes 491520 | tf_op jit(solution)/shard_map/all_to_all | solution.py:570
  118.4 5.3 %all-to-all-start.2 = ((bf16[16,15,512]{2,1,0:T(8,128)(2,1)}), bf16[16,15,512]{2,1,0:T(8,128)(2,1)S(1)}, u32[]{:S(2)}, u32[]{:S(2)}) async-start(bf16[16,15,512]{2,1,0:T(8,128)(2,1)} %broadcast_in_dim.14), calls=%async_computation.2 | async-start | bytes 524288 | tf_op jit(solution)/shard_map/all_to_all | solution.py:570
  124.9 8.3 %all-to-all-done.2 = bf16[16,15,512]{2,1,0:T(8,128)(2,1)S(1)} async-done(((bf16[16,15,512]{2,1,0:T(8,128)(2,1)}), bf16[16,15,512]{2,1,0:T(8,128)(2,1)S(1)}, u32[]{:S(2)}, u32[]{:S(2)}) %all-to-all-start.2) | async-done | bytes 245792 | tf_op jit(solution)/shard_map/all_to_all | solution.py:570
  134.7 5.2 %all-to-all-start.3 = ((bf16[8,224,512]{2,1,0:T(8,128)(2,1)}), bf16[8,224,512]{2,1,0:T(8,128)(2,1)S(1)}, u32[]{:S(2)}, u32[]{:S(2)}) async-start(bf16[8,224,512]{2,1,0:T(8,128)(2,1)} %broadcast_in_dim.15), calls=%async_computation.3 | async-start | bytes 3670016 | tf_op jit(solution)/shard_map/all_to_all | solution.py:810
  139.9 8.0 %collective-permute-start.12 = (bf16[48,512]{1,0:T(8,128)(2,1)S(1)}, bf16[48,512]{1,0:T(8,128)(2,1)S(1)}, u32[]{:S(2)}, u32[]{:S(2)}) collective-permute-start(bf16[48,512]{1,0:T(8,128)(2,1)S(1)} %get-tuple-element.85), channel_id=1, source_target_pairs={{0,8},{8,16},{16,24},{24,32},{32,40},{40,48},{48,56},{56,64},{64,7... | collective-permute-start | bytes 147464 | tf_op jit(solution)/shard_map/ppermute | solution.py:26
  149.8 3.8 %collective-permute-done.13.refs_2_ = bf16[48,512]{1,0:T(8,128)(2,1)S(1)} collective-permute-done((bf16[48,512]{1,0:T(8,128)(2,1)S(1)}, bf16[48,512]{1,0:T(8,128)(2,1)S(1)}, u32[]{:S(2)}, u32[]{:S(2)}) %collective-permute-start.13) | collective-permute-done | bytes 49184 | tf_op jit(solution)/shard_map/ppermute | solution.py:26
  153.6 2.5 %shard_map.332 = bf16[128,256]{1,0:T(8,128)(2,1)} custom-call(f32[128,512]{1,0:T(8,128)S(1)} %get-tuple-element.84.refs_0_, bf16[48,512]{1,0:T(8,128)(2,1)S(1)} %collective-permute-done.12.refs_1_, bf16[48,512]{1,0:T(8,128)(2,1)S(1)} %collective-permute-done.13.refs_2_, bf16[128,48]{1,0:T(8,128)(2,1)} %constant.69.clone.refs_3_, ...), custom_call_target="tpu_custom_call" | custom-call | flops 268435456 | bytes 4194304 | tf_op jit(solution)/shard_map/pallas_call | solution.py:545
  156.1 8.1 %all-to-all-done.3.mine = bf16[8,224,512]{2,1,0:T(8,128)(2,1)S(1)} async-done(((bf16[8,224,512]{2,1,0:T(8,128)(2,1)}), bf16[8,224,512]{2,1,0:T(8,128)(2,1)S(1)}, u32[]{:S(2)}, u32[]{:S(2)}) %all-to-all-start.3) | async-done | bytes 1835040 | tf_op jit(solution)/shard_map/all_to_all | solution.py:810
  165.0 3.4 %collective-permute-done.14 = bf16[16,512]{1,0:T(8,128)(2,1)S(1)} collective-permute-done((bf16[16,512]{1,0:T(8,128)(2,1)S(1)}, bf16[16,512]{1,0:T(8,128)(2,1)S(1)}, u32[]{:S(2)}, u32[]{:S(2)}) %collective-permute-start.14) | collective-permute-done | bytes 16416 | tf_op jit(solution)/shard_map/ppermute | solution.py:30
  169.6 2.5 %shard_map.333 = (bf16[16,64,512]{2,1,0:T(8,128)(2,1)}, bf16[16,32,1536]{2,1,0:T(8,128)(2,1)}, bf16[16,32,512]{2,1,0:T(8,128)(2,1)}, bf16[16,16,768]{2,1,0:T(8,128)(2,1)}, bf16[16,16,256]{2,1,0:T(8,128)(2,1)}) custom-call(s32[4]{0:T(128)S(1)} %pad_add_fusion.refs_13_.refs_14_.where, bf16[8,224,512]{2,1,0:T(8,128)(2,1)S(1)} %all-to-all-done.3.mine, ...), custom_call_target="tpu_custom_call" | custom-call | tf_op jit(solution)/shard_map/pallas_call | solution.py:821
  (38 shorter events, 26.4 us)
Async XLA Ops:
  1.5 6.9 %collective-permute-start = (bf16[176,256]{1,0:T(8,128)(2,1)S(1)}, bf16[176,256]{1,0:T(8,128)(2,1)S(1)}, u32[]{:S(2)}, u32[]{:S(2)}) collective-permute-start(bf16[176,256]{1,0:T(8,128)(2,1)S(1)} %get-tuple-element.52), channel_id=1, source_target_pairs={{0,8},{8,16},{16,24},{24,32},{32,40},{40,48},{48,56},{56,64},{64,7... | collective-permute-start | bytes 270344 | tf_op jit(solution)/shard_map/ppermute | solution.py:26
  6.5 5.8 %collective-permute-start.1 = (bf16[176,256]{1,0:T(8,128)(2,1)S(1)}, bf16[176,256]{1,0:T(8,128)(2,1)S(1)}, u32[]{:S(2)}, u32[]{:S(2)}) collective-permute-start(bf16[176,256]{1,0:T(8,128)(2,1)S(1)} %get-tuple-element.53), channel_id=1, source_target_pairs={{8,0},{16,8},{24,16},{32,24},{40,32},{48,40},{56,48},{64,56},{72,6... | collective-permute-start | bytes 270344 | tf_op jit(solution)/shard_map/ppermute | solution.py:26
  13.7 4.5 %collective-permute-start.2 = (bf16[144,256]{1,0:T(8,128)(2,1)S(1)}, bf16[144,256]{1,0:T(8,128)(2,1)S(1)}, u32[]{:S(2)}, u32[]{:S(2)}) collective-permute-start(bf16[144,256]{1,0:T(8,128)(2,1)S(1)} %get-tuple-element.54), channel_id=1, source_target_pairs={{0,1},{1,2},{2,3},{3,4},{4,5},{5,6},{6,7},{8,9},{9,10},{10,11},{11... | collective-permute-start | bytes 221192 | tf_op jit(solution)/shard_map/ppermute | solution.py:26
  16.8 5.1 %collective-permute-start.3 = (bf16[144,256]{1,0:T(8,128)(2,1)S(1)}, bf16[144,256]{1,0:T(8,128)(2,1)S(1)}, u32[]{:S(2)}, u32[]{:S(2)}) collective-permute-start(bf16[144,256]{1,0:T(8,128)(2,1)S(1)} %get-tuple-element.55), channel_id=1, source_target_pairs={{1,0},{2,1},{3,2},{4,3},{5,4},{6,5},{7,6},{9,8},{10,9},{11,10},{12... | collective-permute-start | bytes 221192 | tf_op jit(solution)/shard_map/ppermute | solution.py:26
  26.2 5.2 %collective-permute-start.4 = (bf16[32,512]{1,0:T(8,128)(2,1)S(1)}, bf16[32,512]{1,0:T(8,128)(2,1)S(1)}, u32[]{:S(2)}, u32[]{:S(2)}) collective-permute-start(bf16[32,512]{1,0:T(8,128)(2,1)S(1)} %get-tuple-element.57), channel_id=1, source_target_pairs={{0,8},{8,16},{16,24},{24,32},{32,40},{40,48},{48,56},{56,64},{64,7... | collective-permute-start | bytes 98312 | tf_op jit(solution)/shard_map/ppermute | solution.py:26
  29.5 5.2 %collective-permute-start.5 = (bf16[32,512]{1,0:T(8,128)(2,1)S(1)}, bf16[32,512]{1,0:T(8,128)(2,1)S(1)}, u32[]{:S(2)}, u32[]{:S(2)}) collective-permute-start(bf16[32,512]{1,0:T(8,128)(2,1)S(1)} %get-tuple-element.58), channel_id=1, source_target_pairs={{8,0},{16,8},{24,16},{32,24},{40,32},{48,40},{56,48},{64,56},{72,6... | collective-permute-start | bytes 98312 | tf_op jit(solution)/shard_map/ppermute | solution.py:26
  35.7 5.9 %collective-permute-start.6 = (bf16[96,512]{1,0:T(8,128)(2,1)S(1)}, bf16[96,512]{1,0:T(8,128)(2,1)S(1)}, u32[]{:S(2)}, u32[]{:S(2)}) collective-permute-start(bf16[96,512]{1,0:T(8,128)(2,1)S(1)} %get-tuple-element.59), channel_id=1, source_target_pairs={{0,1},{1,2},{2,3},{3,4},{4,5},{5,6},{6,7},{8,9},{9,10},{10,11},{11... | collective-permute-start | bytes 294920 | tf_op jit(solution)/shard_map/ppermute | solution.py:26
  38.9 5.4 %collective-permute-start.7 = (bf16[96,512]{1,0:T(8,128)(2,1)S(1)}, bf16[96,512]{1,0:T(8,128)(2,1)S(1)}, u32[]{:S(2)}, u32[]{:S(2)}) collective-permute-start(bf16[96,512]{1,0:T(8,128)(2,1)S(1)} %get-tuple-element.60), channel_id=1, source_target_pairs={{1,0},{2,1},{3,2},{4,3},{5,4},{6,5},{7,6},{9,8},{10,9},{11,10},{12... | collective-permute-start | bytes 294920 | tf_op jit(solution)/shard_map/ppermute | solution.py:26
  56.8 2.0 %collective-permute-start.9 = (bf16[256,512]{1,0:T(8,128)(2,1)S(1)}, bf16[256,512]{1,0:T(8,128)(2,1)S(1)}, u32[]{:S(2)}, u32[]{:S(2)}) collective-permute-start(bf16[256,512]{1,0:T(8,128)(2,1)S(1)} %get-tuple-element.72), channel_id=1, source_target_pairs={{0,8},{8,0},{16,24},{24,16},{32,40},{40,32},{48,56},{56,48},{64,72... | collective-permute-start | bytes 786440 | tf_op jit(solution)/shard_map/ppermute | solution.py:30
  56.9 1.9 %collective-permute-start.8 = (bf16[32,3584]{1,0:T(8,128)(2,1)S(1)}, bf16[32,3584]{1,0:T(8,128)(2,1)S(1)}, u32[]{:S(2)}, u32[]{:S(2)}) collective-permute-start(bf16[32,3584]{1,0:T(8,128)(2,1)S(1)} %get-tuple-element.65.refs_1_), channel_id=1, source_target_pairs={{0,8},{8,0},{16,24},{24,16},{32,40},{40,32},{48,56},{56,48},{64,72... | collective-permute-start | bytes 688136 | tf_op jit(solution)/shard_map/ppermute | solution.py:30
  60.7 32.6 %all-to-all-start = ((bf16[8,240,512]{2,1,0:T(8,128)(2,1)}), bf16[8,240,512]{2,1,0:T(8,128)(2,1)}, u32[]{:S(2)}, u32[]{:S(2)}) async-start(bf16[8,240,512]{2,1,0:T(8,128)(2,1)} %shard_map.330), calls=%async_computation | async-start | bytes 3932160 | tf_op jit(solution)/shard_map/all_to_all | solution.py:563
  67.4 27.7 %collective-permute-start.10 = (bf16[48,512]{1,0:T(8,128)(2,1)S(1)}, bf16[48,512]{1,0:T(8,128)(2,1)S(1)}, u32[]{:S(2)}, u32[]{:S(2)}) collective-permute-start(bf16[48,512]{1,0:T(8,128)(2,1)S(1)} %get-tuple-element.75), channel_id=1, source_target_pairs={{0,1},{1,2},{2,3},{3,4},{4,5},{5,6},{6,7},{8,9},{9,10},{10,11},{11... | collective-permute-start | bytes 147464 | tf_op jit(solution)/shard_map/ppermute | solution.py:26
  70.8 25.1 %collective-permute-start.11 = (bf16[48,512]{1,0:T(8,128)(2,1)S(1)}, bf16[48,512]{1,0:T(8,128)(2,1)S(1)}, u32[]{:S(2)}, u32[]{:S(2)}) collective-permute-start(bf16[48,512]{1,0:T(8,128)(2,1)S(1)} %get-tuple-element.76), channel_id=1, source_target_pairs={{1,0},{2,1},{3,2},{4,3},{5,4},{6,5},{7,6},{9,8},{10,9},{11,10},{12... | collective-permute-start | bytes 147464 | tf_op jit(solution)/shard_map/ppermute | solution.py:26
  118.4 14.7 %all-to-all-start.2 = ((bf16[16,15,512]{2,1,0:T(8,128)(2,1)}), bf16[16,15,512]{2,1,0:T(8,128)(2,1)S(1)}, u32[]{:S(2)}, u32[]{:S(2)}) async-start(bf16[16,15,512]{2,1,0:T(8,128)(2,1)} %broadcast_in_dim.14), calls=%async_computation.2 | async-start | bytes 524288 | tf_op jit(solution)/shard_map/all_to_all | solution.py:570
  134.7 29.4 %all-to-all-start.3 = ((bf16[8,224,512]{2,1,0:T(8,128)(2,1)}), bf16[8,224,512]{2,1,0:T(8,128)(2,1)S(1)}, u32[]{:S(2)}, u32[]{:S(2)}) async-start(bf16[8,224,512]{2,1,0:T(8,128)(2,1)} %broadcast_in_dim.15), calls=%async_computation.3 | async-start | bytes 3670016 | tf_op jit(solution)/shard_map/all_to_all | solution.py:810
  139.9 9.9 %collective-permute-start.12 = (bf16[48,512]{1,0:T(8,128)(2,1)S(1)}, bf16[48,512]{1,0:T(8,128)(2,1)S(1)}, u32[]{:S(2)}, u32[]{:S(2)}) collective-permute-start(bf16[48,512]{1,0:T(8,128)(2,1)S(1)} %get-tuple-element.85), channel_id=1, source_target_pairs={{0,8},{8,16},{16,24},{24,32},{32,40},{40,48},{48,56},{56,64},{64,7... | collective-permute-start | bytes 147464 | tf_op jit(solution)/shard_map/ppermute | solution.py:26
  147.9 5.7 %collective-permute-start.13 = (bf16[48,512]{1,0:T(8,128)(2,1)S(1)}, bf16[48,512]{1,0:T(8,128)(2,1)S(1)}, u32[]{:S(2)}, u32[]{:S(2)}) collective-permute-start(bf16[48,512]{1,0:T(8,128)(2,1)S(1)} %get-tuple-element.86), channel_id=1, source_target_pairs={{8,0},{16,8},{24,16},{32,24},{40,32},{48,40},{56,48},{64,56},{72,6... | collective-permute-start | bytes 147464 | tf_op jit(solution)/shard_map/ppermute | solution.py:26
  164.1 5.4 %collective-permute-start.15 = (bf16[8,224,512]{2,1,0:T(8,128)(2,1)S(1)}, bf16[8,224,512]{2,1,0:T(8,128)(2,1)S(1)}, u32[]{:S(2)}, u32[]{:S(2)}) collective-permute-start(bf16[8,224,512]{2,1,0:T(8,128)(2,1)S(1)} %all-to-all-done.3.mine), channel_id=1, source_target_pairs={{0,8},{8,0},{16,24},{24,16},{32,40},{40,32},{48,56},{56,48},{64,72... | collective-permute-start | bytes 5505032 | tf_op jit(solution)/shard_map/ppermute | solution.py:30
  165.0 3.4 %collective-permute-start.14 = (bf16[16,512]{1,0:T(8,128)(2,1)S(1)}, bf16[16,512]{1,0:T(8,128)(2,1)S(1)}, u32[]{:S(2)}, u32[]{:S(2)}) collective-permute-start(bf16[16,512]{1,0:T(8,128)(2,1)S(1)} %slice.13), channel_id=1, source_target_pairs={{0,8},{8,0},{16,24},{24,16},{32,40},{40,32},{48,56},{56,48},{64,72... | collective-permute-start | bytes 49160 | tf_op jit(solution)/shard_map/ppermute | solution.py:30

commit v5 on v4

--- a/solution.py
+++ b/solution.py
@@ -13,7 +13,7 @@
 RADIUS = 3
 PAIR = 2 * HEAD
 TILE = (8, 16)
-VMEM = 32 << 20
+VMEM = 20 << 20
 NEG = -1e30
 norm_eps = 1e-06
 f32 = jnp.float32
@@ -377,10 +377,25 @@
         out[j, place + 2 * rows :] = gains
 
 
+def fine_again_kernel(
+    query_in, kv_in, field, pick, gain, band, at, where, kv_out, normed_out, ratio_out, *probs
+):
+    kv = dot(pick[...], kv_in[...]).astype(bf16)
+    values, scale, normed = norm_forward(dot(pick[...], field[...]), gain[...])
+    kv_out[...] = kv
+    normed_out[...] = normed
+    ratio_out[...] = values * scale
+    bias = band[...] + validity(at[...], where, *TILE)
+    masks = head_masks()
+    for h, out in enumerate(probs):
+        q = masked(lanes(query_in, h // 2), masks[h % 2])
+        out[...] = probabilities(q, lanes(kv, h // 2), bias)
+
+
 def fine_backward_kernel(
     factor,
-    grad_fine, grad_merged, perm, query_in, kv_in, field, att, pick, w_out, w_qkv, gain, band,
-    at, where,
+    grad_fine, grad_merged, perm, query_in, kv, normed_in, ratio_in, att, p0, p1, p2, p3,
+    w_out, w_qkv, gain, where,
     up_out, gq_out, mid_out, left_out, right_out, gain_out, keep_out, send_out,
 ):
     width = grad_fine.shape[1]
@@ -391,9 +406,7 @@
     up_b = up.astype(bf16)
     grad_att = dot_nt(up_b, w_out[...]).astype(bf16)
     query = query_in[...]
-    kv = dot(pick[...], kv_in[...]).astype(bf16)
-    values, scale, normed = norm_forward(dot(pick[...], field[...]), gain[...])
-    bias = band[...] + validity(at[...], where, *TILE)
+    normed, ratio = normed_in[...], ratio_in[...]
     masks = head_masks()
     middle, side = mid_out.shape[0], left_out.shape[0]
     gq, gk, gv = [], [], []
@@ -401,9 +414,9 @@
         keys, vals = lanes(kv, p), lanes(kv, pairs + p)
         q, g = lanes(query, p), lanes(grad_att, p)
         sums = None
-        for mask in masks:
+        for h, mask in enumerate(masks):
             qm, gm = masked(q, mask), masked(g, mask)
-            prob = probabilities(qm, keys, bias)
+            prob = (p0, p1, p2, p3)[2 * p + h][...]
             dscore = score_gradient(prob, dot_nt(gm, vals))
             new = (
                 dot(dscore, keys) * mask,
@@ -424,7 +437,6 @@
     own = query.shape[0]
     grad_normed = dot_nt(grad_b, w_qkv[:, width:])
     own_normed = dot_nt(grad_query, w_qkv[:, :width])
-    ratio = values * scale
     gain_out[...] = jnp.sum(grad_normed * ratio, axis=0, keepdims=True) + jnp.sum(
         own_normed * ratio[:own], axis=0, keepdims=True
     )
@@ -556,6 +568,31 @@
         )(*given)
 
     return run
+
+
+def preload(values, after):
+    held = [v.value for v in values]
+    *held, _ = lax.optimization_barrier((*held, after))
+    count = len(held)
+
+    def body(*refs):
+        copies = [
+            pltpu.make_async_copy(refs[i], refs[count + i], refs[-1].at[i]) for i in range(count)
+        ]
+        for copy in copies:
+            copy.start()
+        for copy in copies:
+            copy.wait()
+
+    return pl.pallas_call(
+        body,
+        out_shape=[jax.ShapeDtypeStruct(v.shape, v.dtype) for v in held],
+        in_specs=[pl.BlockSpec(memory_space=pl.ANY)] * count,
+        out_specs=[pl.BlockSpec(memory_space=pltpu.VMEM)] * count,
+        scratch_shapes=[pltpu.SemaphoreType.DMA((count,))],
+        compiler_params=pltpu.CompilerParams(vmem_limit_bytes=VMEM),
+        cost_estimate=pl.CostEstimate(flops=1 << 20, bytes_accessed=4 << 20, transcendentals=0),
+    )(*[pltpu.with_memory_space_constraint(v, pltpu.HBM) for v in held])
 
 
 def scatter_over_columns(x):
@@ -625,24 +662,41 @@
     down = shifted(send_up, "row", -1)
     held = natural + moved(natural[-rim:], -rows, 0) + moved(natural[:rim], rows, 0)
     cheld = cnatural + moved(cnatural, -crows, 0) + moved(cnatural, crows, 0)
+    flat0 = joined(keys0)
+    own0 = keys0[0]
+    asked0 = joined(keys0[:3])
+    near = len(keys0[1])
+    perm = chosen(own0, natural)
+    tok_v, gc_v, picks, cpicks, *ready0 = preload(
+        [
+            tok,
+            gc,
+            chosen(moved(keys0[5], 0, columns) + moved(keys0[6], 0, -columns), held),
+            chosen(moved(queries1[3], 0, ccolumns) + moved(queries1[4], 0, -ccolumns), cheld),
+            perm,
+            chosen(merge_order(RADIUS + 1, columns), natural[:near]),
+            gain0,
+            qkv_fine,
+            out_fine,
+            w_merge,
+            Late(jnp.asarray(band_bias(asked0, flat0))),
+            places(flat0),
+        ],
+        send_up,
+    )
     send_right, send_left = call(
         columns_pack_kernel, [((side + 2 * cside, width), bf16)] * 2, flops=1 << 20
     )(
-        tok,
-        gc,
+        tok_v,
+        gc_v,
         up,
         down,
-        chosen(moved(keys0[5], 0, columns) + moved(keys0[6], 0, -columns), held),
-        chosen(moved(queries1[3], 0, ccolumns) + moved(queries1[4], 0, -ccolumns), cheld),
+        picks,
+        cpicks,
     )
     left = shifted(send_right, "col", 1)
     right = shifted(send_left, "col", -1)
 
-    flat0 = joined(keys0)
-    own0 = keys0[0]
-    asked0 = joined(keys0[:3])
-    perm = chosen(own0, natural)
-    near = len(keys0[1])
     merged, near1, down1, up1, field0, query0, kv0, att0 = call(
         fine_forward_kernel,
         [
@@ -656,19 +710,12 @@
             ((count, width), bf16),
         ],
     )(
-        tok,
+        tok_v,
         up,
         down,
         left,
         right,
-        perm,
-        chosen(merge_order(RADIUS + 1, columns), natural[:near]),
-        gain0,
-        qkv_fine,
-        out_fine,
-        w_merge,
-        Late(jnp.asarray(band_bias(asked0, flat0))),
-        places(flat0),
+        *ready0,
         where,
     )
 
@@ -676,18 +723,51 @@
     below1 = shifted(up1, "row", -1)
     tall1 = joined(keys1[:5])
     wide1 = len(keys1[5])
+    flat1, ask1 = joined(keys1), joined(queries1)
+    picks1, pick1, gain_v, qkv_v, merge_v, band1, at1 = preload(
+        [
+            chosen(moved(keys1[5], 0, ccolumns) + moved(keys1[6], 0, -ccolumns), tall1),
+            chosen(ask1, flat1),
+            gain1,
+            qkv_coarse,
+            w_merge,
+            Late(jnp.asarray(band_bias(ask1, flat1))),
+            places(flat1),
+        ],
+        near1,
+    )
     send_right, send_left = call(
         coarse_pack_kernel, [((wide1, cwidth), bf16)] * 2, flops=1 << 20
     )(
         near1,
         above1,
         below1,
-        chosen(moved(keys1[5], 0, ccolumns) + moved(keys1[6], 0, -ccolumns), tall1),
+        picks1,
     )
     left1 = shifted(send_right, "col", 1)
     right1 = shifted(send_left, "col", -1)
 
     flat1, ask1 = joined(keys1), joined(queries1)
+    backs = back_keys(rows, columns)
+    flatb = joined(backs)
+    kvb, normedb, ratiob, *probs = call(
+        fine_again_kernel,
+        [
+            ((len(flatb), 2 * width), bf16),
+            ((len(flatb), width), bf16),
+            ((len(flatb), width), f32),
+        ]
+        + [((count, len(flatb)), f32)] * (width // HEAD),
+    )(
+        query0,
+        kv0,
+        field0,
+        chosen(flatb, flat0),
+        gain0,
+        Late(jnp.asarray(band_bias(own0, flatb))),
+        places(flatb),
+        where,
+    )
     upstream1, grad_att1 = call(
         coarse_upstream_kernel,
         [((ccount, cwidth), bf16), ((len(ask1), cwidth), bf16)],
@@ -718,18 +798,16 @@
         upstream1,
         grad_att1,
         merged,
-        chosen(ask1, flat1),
-        gain1,
-        qkv_coarse,
-        w_merge,
-        Late(jnp.asarray(band_bias(ask1, flat1))),
-        places(flat1),
+        pick1,
+        gain_v,
+        qkv_v,
+        merge_v,
+        band1,
+        at1,
         where,
     )
     got1 = flip(send1, "row", 1)
 
-    backs = back_keys(rows, columns)
-    flatb = joined(backs)
     rims = len(backs[1])
     bside = len(backs[3])
     middle = count + 2 * rims
@@ -750,15 +828,14 @@
         grad_merged,
         perm,
         query0,
-        kv0,
-        field0,
+        kvb,
+        normedb,
+        ratiob,
         att0,
-        chosen(flatb, flat0),
+        *probs,
         out_fine,
         qkv_fine,
         gain0,
-        Late(jnp.asarray(band_bias(own0, flatb))),
-        places(flatb),
         where,
     )
     n1 = (2 * width + 4 * (cwidth // 2)) // cols
@@ -806,9 +883,10 @@
         qkv_fine,
     )
     x, small = x[:-16], x[-16:]
+    x = lax.all_to_all(jnp.broadcast_to(x, (cols,) + x.shape), "col", 0, 0)
     gains = small.astype(f32) + flip(small, "row", 1).astype(f32)
-    x = lax.all_to_all(jnp.broadcast_to(x, (cols,) + x.shape), "col", 0, 0)
-    x, grad_tokens = lax.optimization_barrier((x, grad_tokens))
+    gain_sums = (gains[1, :width], gains[0])
+    x, grad_tokens, gain_sums = lax.optimization_barrier((x, grad_tokens, gain_sums))
     other = flip(x, "row", 1)
     shapes = [
         (2 * cols, 2 * width // cols, cwidth),
@@ -832,11 +910,11 @@
     )
     return (
         grad_tokens.reshape(rows, columns, width),
-        gains[1, :width],
+        gain_sums[0],
         grad_qkv0,
         grad_out0,
         grad_merge,
-        gains[0],
+        gain_sums[1],
         grad_qkv1,
         grad_out1,
     )

time: 173 us -> 166 us (0.960)
  waiting for transfers between devices: 60.3 us -> 52.7 us
    ppermute x12, waiting for transfers between devices: 18 us -> 10.5 us  [shifted(): return lax.ppermute(x, axis, pairs)]
    ppermute x4, starting transfers between devices: 1.45 us -> 6.14 us  [flip(): lax.ppermute(x, axis, [(i, i ^ bit) for i in range(lax.axis_size(axis))])]
    ppermute x12, starting transfers between devices: 35.4 us -> 30.8 us  [shifted(): return lax.ppermute(x, axis, pairs)]
    pallas_call x10 -> x11, Pallas kernels: 27 us -> 23.3 us  [run(): pl.pallas_call(body, out_shape=[jax.ShapeDtypeStruct(shape, dtype) for sh...]
    pallas_call x0 -> x2, Pallas kernels: none -> 3.71 us  [preload(): pl.pallas_call(body, out_shape=[jax.ShapeDtypeStruct(v.shape, v.dtype) fo...]
  transfers between devices with their start and end apart: 19 -> 19, of which waited for: 11 -> 10; matrix products, arithmetic and copies ran while one was open for 2% -> 2% of each run, Pallas kernels for 3% -> 7%
where the time goes in v5:
time: 166 us; the launch traced here: 165 us
  starting transfers between devices  54.5 us (33%)
  waiting for transfers between devices  52.7 us (32%)
  Pallas kernels  29.5 us (18%)
  blocking collectives  21.7 us (13%)
  local copies, waits for them, and re-layouts  3.48 us (2%)
  other arithmetic  2.03 us (1%)
    ppermute x12, starting transfers between devices, shifted(): return lax.ppermute(x, axis, pairs)  30.8 us
    pallas_call x11, Pallas kernels, run(): pl.pallas_call(body, out_shape=[jax.ShapeDtypeStruct(shape, dtype) for sh...  23.3 us
    all_to_all x1, blocking collectives, trade_rows(): return lax.all_to_all(pieces, 'row', 0, 0, axis_index_groups=groups)  21.7 us
    all_to_all x1, waiting for transfers between devices, scatter_over_columns(): pieces = lax.all_to_all(x, 'col', 0, 0)  21.2 us
    ppermute x12, waiting for transfers between devices, shifted(): return lax.ppermute(x, axis, pairs)  10.5 us
    all_to_all x1, waiting for transfers between devices, trade_rows(): return lax.all_to_all(pieces, 'row', 0, 0, axis_index_groups=groups)  8.32 us
    all_to_all x1, waiting for transfers between devices, per_device(): x = lax.all_to_all(jnp.broadcast_to(x, (cols,) + x.shape), 'col', 0, 0)  7.94 us
    all_to_all x1, starting transfers between devices, scatter_over_columns(): pieces = lax.all_to_all(x, 'col', 0, 0)  6.75 us
  transfers between devices with their start and end apart: 19, of which 10 were waited for; matrix products, arithmetic and copies ran while one was open for 2% of the time, Pallas kernels for 7%

profile of v5, /device:TPU:1, one launch (start us, length us, event | category | flops | bytes accessed | tf_op | source)
XLA Modules:
  0.0 164.7 jit_solution(17825971716165670206)
XLA Ops:
  1.5 4.9 %collective-permute-start = (bf16[176,256]{1,0:T(8,128)(2,1)S(1)}, bf16[176,256]{1,0:T(8,128)(2,1)S(1)}, u32[]{:S(2)}, u32[]{:S(2)}) collective-permute-start(bf16[176,256]{1,0:T(8,128)(2,1)S(1)} %get-tuple-element.113), channel_id=1, source_target_pairs={{0,8},{8,16},{16,24},{24,32},{32,40},{40,48},{48,56},{56,64},{64,7... | collective-permute-start | bytes 270344 | tf_op jit(solution)/shard_map/ppermute | solution.py:26
  10.2 2.1 %collective-permute-done.1.refs_3_.refs_2_ = bf16[176,256]{1,0:T(8,128)(2,1)S(1)} collective-permute-done((bf16[176,256]{1,0:T(8,128)(2,1)S(1)}, bf16[176,256]{1,0:T(8,128)(2,1)S(1)}, u32[]{:S(2)}, u32[]{:S(2)}) %collective-permute-start.1) | collective-permute-done | bytes 90144 | tf_op jit(solution)/shard_map/ppermute | solution.py:26
  12.5 3.1 %collective-permute-start.2 = (bf16[144,256]{1,0:T(8,128)(2,1)S(1)}, bf16[144,256]{1,0:T(8,128)(2,1)S(1)}, u32[]{:S(2)}, u32[]{:S(2)}) collective-permute-start(bf16[144,256]{1,0:T(8,128)(2,1)S(1)} %get-tuple-element.117), channel_id=1, source_target_pairs={{0,1},{1,2},{2,3},{3,4},{4,5},{5,6},{6,7},{8,9},{9,10},{10,11},{11... | collective-permute-start | bytes 221192 | tf_op jit(solution)/shard_map/ppermute | solution.py:26
  17.0 3.7 %collective-permute-done.3.refs_4_ = bf16[144,256]{1,0:T(8,128)(2,1)S(1)} collective-permute-done((bf16[144,256]{1,0:T(8,128)(2,1)S(1)}, bf16[144,256]{1,0:T(8,128)(2,1)S(1)}, u32[]{:S(2)}, u32[]{:S(2)}) %collective-permute-start.3) | collective-permute-done | bytes 73760 | tf_op jit(solution)/shard_map/ppermute | solution.py:26
  20.7 2.8 %shard_map.326 = (bf16[32,1024]{1,0:T(8,128)(2,1)S(1)}, bf16[64,512]{1,0:T(8,128)(2,1)S(1)}, bf16[32,512]{1,0:T(8,128)(2,1)S(1)}, bf16[32,512]{1,0:T(8,128)(2,1)...) custom-call(bf16[128,256]{1,0:T(8,128)(2,1)S(1)} %get-tuple-element., ...), custom_call_target="tpu_custom_call" | custom-call | flops 268435456 | bytes 4194304 | tf_op jit(solution)/shard_map/pallas_call | solution.py:557
  23.5 3.3 %collective-permute-start.4 = (bf16[32,512]{1,0:T(8,128)(2,1)S(1)}, bf16[32,512]{1,0:T(8,128)(2,1)S(1)}, u32[]{:S(2)}, u32[]{:S(2)}) collective-permute-start(bf16[32,512]{1,0:T(8,128)(2,1)S(1)} %get-tuple-element.128), channel_id=1, source_target_pairs={{0,8},{8,16},{16,24},{24,32},{32,40},{40,48},{48,56},{56,64},{64,7... | collective-permute-start | bytes 98312 | tf_op jit(solution)/shard_map/ppermute | solution.py:26
  32.2 3.1 %collective-permute-start.6 = (bf16[96,512]{1,0:T(8,128)(2,1)S(1)}, bf16[96,512]{1,0:T(8,128)(2,1)S(1)}, u32[]{:S(2)}, u32[]{:S(2)}) collective-permute-start(bf16[96,512]{1,0:T(8,128)(2,1)S(1)} %get-tuple-element.138), channel_id=1, source_target_pairs={{0,1},{1,2},{2,3},{3,4},{4,5},{5,6},{6,7},{8,9},{9,10},{10,11},{11... | collective-permute-start | bytes 294920 | tf_op jit(solution)/shard_map/ppermute | solution.py:26
  36.7 2.7 %shard_map.331 = (bf16[320,512]{1,0:T(8,128)(2,1)S(1)}, bf16[320,256]{1,0:T(8,128)(2,1)S(1)}, f32[320,256]{1,0:T(8,128)S(1)}, f32[128,320]{1,0:T(8,128)S(1)}, f3...) custom-call(bf16[128,256]{1,0:T(8,128)(2,1)S(1)} %get-tuple-element.152.refs_0_.refs_3_, ...), custom_call_target="tpu_custom_call" | custom-call | flops 268435456 | bytes 4194304 | tf_op jit(solution)/shard_map/pallas_call | solution.py:557
  40.8 5.9 %shard_map.330 = (bf16[32,1024]{1,0:T(8,128)(2,1)S(1)}, bf16[32,3584]{1,0:T(8,128)(2,1)S(1)}, f32[1,512]{1,0:T(1,128)S(1)}, f32[32,1024]{1,0:T(8,128)S(1)}) custom-call(bf16[64,512]{1,0:T(8,128)(2,1)S(1)} %get-tuple-element.127.refs_0_, bf16[32,512]{1,0:T(8,128)(2,1)S(1)} %collective-permute-done.4.refs_1_, ...), custom_call_target="tpu_custom_call" | custom-call | flops 268435456 | bytes 4194304 | tf_op jit(solution)/shard_map/pallas_call | solution.py:557
  46.7 3.8 %shard_map.332 = (f32[128,256]{1,0:T(8,128)S(1)}, bf16[128,256]{1,0:T(8,128)(2,1)S(1)}, f32[224,512]{1,0:T(8,128)S(1)}, bf16[48,512]{1,0:T(8,128)(2,1)S(1)}, bf1...) custom-call(bf16[128,256]{1,0:T(8,128)(2,1)} %bitcast.21, ...), custom_call_target="tpu_custom_call" | custom-call | flops 268435456 | bytes 4194304 | tf_op jit(solution)/shard_map/pallas_call | solution.py:557
  54.3 6.7 %all-to-all-start = ((bf16[8,240,512]{2,1,0:T(8,128)(2,1)}), bf16[8,240,512]{2,1,0:T(8,128)(2,1)}, u32[]{:S(2)}, u32[]{:S(2)}) async-start(bf16[8,240,512]{2,1,0:T(8,128)(2,1)} %shard_map.333), calls=%async_computation | async-start | bytes 3932160 | tf_op jit(solution)/shard_map/all_to_all | solution.py:600
  61.1 3.4 %collective-permute-start.10 = (bf16[48,512]{1,0:T(8,128)(2,1)S(1)}, bf16[48,512]{1,0:T(8,128)(2,1)S(1)}, u32[]{:S(2)}, u32[]{:S(2)}) collective-permute-start(bf16[48,512]{1,0:T(8,128)(2,1)S(1)} %get-tuple-element.167), channel_id=1, source_target_pairs={{0,1},{1,2},{2,3},{3,4},{4,5},{5,6},{6,7},{8,9},{9,10},{10,11},{11... | collective-permute-start | bytes 147464 | tf_op jit(solution)/shard_map/ppermute | solution.py:26
  65.8 21.2 %all-to-all-done = bf16[8,240,512]{2,1,0:T(8,128)(2,1)} async-done(((bf16[8,240,512]{2,1,0:T(8,128)(2,1)}), bf16[8,240,512]{2,1,0:T(8,128)(2,1)}, u32[]{:S(2)}, u32[]{:S(2)}) %all-to-all-start) | async-done | bytes 1966112 | tf_op jit(solution)/shard_map/all_to_all | solution.py:600
  89.6 21.7 %all_to_all.20 = bf16[16,15,512]{2,1,0:T(8,128)(2,1)S(1)} all-to-all(bf16[16,15,512]{2,1,0:T(8,128)(2,1)S(1)} %reshape.52), channel_id=1, replica_groups={{0,16,32,48,64,80,96,112,128,144,160,176,192,208,224,240},{8,24,40,56,7..., dimensions={0} | all-to-all | bytes 491520 | tf_op jit(solution)/shard_map/all_to_all | solution.py:607
  112.0 5.3 %all-to-all-start.2 = ((bf16[16,15,512]{2,1,0:T(8,128)(2,1)}), bf16[16,15,512]{2,1,0:T(8,128)(2,1)S(1)}, u32[]{:S(2)}, u32[]{:S(2)}) async-start(bf16[16,15,512]{2,1,0:T(8,128)(2,1)} %broadcast_in_dim.14), calls=%async_computation.2 | async-start | bytes 524288 | tf_op jit(solution)/shard_map/all_to_all | solution.py:607
  118.4 8.3 %all-to-all-done.2 = bf16[16,15,512]{2,1,0:T(8,128)(2,1)S(1)} async-done(((bf16[16,15,512]{2,1,0:T(8,128)(2,1)}), bf16[16,15,512]{2,1,0:T(8,128)(2,1)S(1)}, u32[]{:S(2)}, u32[]{:S(2)}) %all-to-all-start.2) | async-done | bytes 245792 | tf_op jit(solution)/shard_map/all_to_all | solution.py:607
  128.3 5.4 %all-to-all-start.3 = ((bf16[8,224,512]{2,1,0:T(8,128)(2,1)}), bf16[8,224,512]{2,1,0:T(8,128)(2,1)S(1)}, u32[]{:S(2)}, u32[]{:S(2)}) async-start(bf16[8,224,512]{2,1,0:T(8,128)(2,1)} %broadcast_in_dim.15), calls=%async_computation.3 | async-start | bytes 3670016 | tf_op jit(solution)/shard_map/all_to_all | solution.py:886
  133.7 4.7 %collective-permute-start.14 = (bf16[16,512]{1,0:T(8,128)(2,1)S(1)}, bf16[16,512]{1,0:T(8,128)(2,1)S(1)}, u32[]{:S(2)}, u32[]{:S(2)}) collective-permute-start(bf16[16,512]{1,0:T(8,128)(2,1)S(1)} %slice.13), channel_id=1, source_target_pairs={{0,8},{8,0},{16,24},{24,16},{32,40},{40,32},{48,56},{56,48},{64,72... | collective-permute-start | bytes 49160 | tf_op jit(solution)/shard_map/ppermute | solution.py:30
  138.4 3.4 %collective-permute-start.12 = (bf16[48,512]{1,0:T(8,128)(2,1)S(1)}, bf16[48,512]{1,0:T(8,128)(2,1)S(1)}, u32[]{:S(2)}, u32[]{:S(2)}) collective-permute-start(bf16[48,512]{1,0:T(8,128)(2,1)S(1)} %get-tuple-element.177), channel_id=1, source_target_pairs={{0,8},{8,16},{16,24},{24,32},{32,40},{40,48},{48,56},{56,64},{64,7... | collective-permute-start | bytes 147464 | tf_op jit(solution)/shard_map/ppermute | solution.py:26
  145.0 2.6 %collective-permute-done.13.refs_2_ = bf16[48,512]{1,0:T(8,128)(2,1)S(1)} collective-permute-done((bf16[48,512]{1,0:T(8,128)(2,1)S(1)}, bf16[48,512]{1,0:T(8,128)(2,1)S(1)}, u32[]{:S(2)}, u32[]{:S(2)}) %collective-permute-start.13) | collective-permute-done | bytes 49184 | tf_op jit(solution)/shard_map/ppermute | solution.py:26
  147.6 2.5 %shard_map.335 = bf16[128,256]{1,0:T(8,128)(2,1)} custom-call(f32[128,512]{1,0:T(8,128)S(1)} %get-tuple-element.176.refs_0_, bf16[48,512]{1,0:T(8,128)(2,1)S(1)} %collective-permute-done.12.refs_1_, bf16[48,512]{1,0:T(8,128)(2,1)S(1)} %collective-permute-done.13.refs_2_, bf16[128,48]{1,0:T(8,128)(2,1)} %constant.69.clone.refs_3_, ...), custom_call_target="tpu_custom_call" | custom-call | flops 268435456 | bytes 4194304 | tf_op jit(solution)/shard_map/pallas_call | solution.py:557
  150.0 7.9 %all-to-all-done.3.mine = bf16[8,224,512]{2,1,0:T(8,128)(2,1)S(1)} async-done(((bf16[8,224,512]{2,1,0:T(8,128)(2,1)}), bf16[8,224,512]{2,1,0:T(8,128)(2,1)S(1)}, u32[]{:S(2)}, u32[]{:S(2)}) %all-to-all-start.3) | async-done | bytes 1835040 | tf_op jit(solution)/shard_map/all_to_all | solution.py:886
  158.8 3.4 %collective-permute-done.15.other = bf16[8,224,512]{2,1,0:T(8,128)(2,1)S(1)} collective-permute-done((bf16[8,224,512]{2,1,0:T(8,128)(2,1)S(1)}, bf16[8,224,512]{2,1,0:T(8,128)(2,1)S(1)}, u32[]{:S(2)}, u32[]{:S(2)}) %collective-permute-start.15) | collective-permute-done | bytes 1835040 | tf_op jit(solution)/shard_map/ppermute | solution.py:30
  162.2 2.5 %shard_map.336 = (bf16[16,64,512]{2,1,0:T(8,128)(2,1)}, bf16[16,32,1536]{2,1,0:T(8,128)(2,1)}, bf16[16,32,512]{2,1,0:T(8,128)(2,1)}, bf16[16,16,768]{2,1,0:T(8,128)(2,1)}, bf16[16,16,256]{2,1,0:T(8,128)(2,1)}) custom-call(s32[4]{0:T(128)S(1)} %pad_add_fusion.refs_13_.refs_14_.refs_7_.refs_15_.where, bf16[8,224,512]{2,1,0:T(8,128)(2,1)S(1)} %all-to-all-done.3.mine, ...), custom_call_target="tpu_custom_call" | custom-call | tf_op jit(solution)/shard_map/pallas_call | solution.py:899
  (41 shorter events, 29.5 us)
Async XLA Ops:
  1.5 8.7 %collective-permute-start = (bf16[176,256]{1,0:T(8,128)(2,1)S(1)}, bf16[176,256]{1,0:T(8,128)(2,1)S(1)}, u32[]{:S(2)}, u32[]{:S(2)}) collective-permute-start(bf16[176,256]{1,0:T(8,128)(2,1)S(1)} %get-tuple-element.113), channel_id=1, source_target_pairs={{0,8},{8,16},{16,24},{24,32},{32,40},{40,48},{48,56},{56,64},{64,7... | collective-permute-start | bytes 270344 | tf_op jit(solution)/shard_map/ppermute | solution.py:26
  6.5 5.8 %collective-permute-start.1 = (bf16[176,256]{1,0:T(8,128)(2,1)S(1)}, bf16[176,256]{1,0:T(8,128)(2,1)S(1)}, u32[]{:S(2)}, u32[]{:S(2)}) collective-permute-start(bf16[176,256]{1,0:T(8,128)(2,1)S(1)} %get-tuple-element.99), channel_id=1, source_target_pairs={{8,0},{16,8},{24,16},{32,24},{40,32},{48,40},{56,48},{64,56},{72,6... | collective-permute-start | bytes 270344 | tf_op jit(solution)/shard_map/ppermute | solution.py:26
  12.5 4.5 %collective-permute-start.2 = (bf16[144,256]{1,0:T(8,128)(2,1)S(1)}, bf16[144,256]{1,0:T(8,128)(2,1)S(1)}, u32[]{:S(2)}, u32[]{:S(2)}) collective-permute-start(bf16[144,256]{1,0:T(8,128)(2,1)S(1)} %get-tuple-element.117), channel_id=1, source_target_pairs={{0,1},{1,2},{2,3},{3,4},{4,5},{5,6},{6,7},{8,9},{9,10},{10,11},{11... | collective-permute-start | bytes 221192 | tf_op jit(solution)/shard_map/ppermute | solution.py:26
  15.6 5.1 %collective-permute-start.3 = (bf16[144,256]{1,0:T(8,128)(2,1)S(1)}, bf16[144,256]{1,0:T(8,128)(2,1)S(1)}, u32[]{:S(2)}, u32[]{:S(2)}) collective-permute-start(bf16[144,256]{1,0:T(8,128)(2,1)S(1)} %get-tuple-element.118), channel_id=1, source_target_pairs={{1,0},{2,1},{3,2},{4,3},{5,4},{6,5},{7,6},{9,8},{10,9},{11,10},{12... | collective-permute-start | bytes 221192 | tf_op jit(solution)/shard_map/ppermute | solution.py:26
  23.5 7.1 %collective-permute-start.4 = (bf16[32,512]{1,0:T(8,128)(2,1)S(1)}, bf16[32,512]{1,0:T(8,128)(2,1)S(1)}, u32[]{:S(2)}, u32[]{:S(2)}) collective-permute-start(bf16[32,512]{1,0:T(8,128)(2,1)S(1)} %get-tuple-element.128), channel_id=1, source_target_pairs={{0,8},{8,16},{16,24},{24,32},{32,40},{40,48},{48,56},{56,64},{64,7... | collective-permute-start | bytes 98312 | tf_op jit(solution)/shard_map/ppermute | solution.py:26
  26.8 5.2 %collective-permute-start.5 = (bf16[32,512]{1,0:T(8,128)(2,1)S(1)}, bf16[32,512]{1,0:T(8,128)(2,1)S(1)}, u32[]{:S(2)}, u32[]{:S(2)}) collective-permute-start(bf16[32,512]{1,0:T(8,128)(2,1)S(1)} %get-tuple-element.129), channel_id=1, source_target_pairs={{8,0},{16,8},{24,16},{32,24},{40,32},{48,40},{56,48},{64,56},{72,6... | collective-permute-start | bytes 98312 | tf_op jit(solution)/shard_map/ppermute | solution.py:26
  32.2 8.6 %collective-permute-start.6 = (bf16[96,512]{1,0:T(8,128)(2,1)S(1)}, bf16[96,512]{1,0:T(8,128)(2,1)S(1)}, u32[]{:S(2)}, u32[]{:S(2)}) collective-permute-start(bf16[96,512]{1,0:T(8,128)(2,1)S(1)} %get-tuple-element.138), channel_id=1, source_target_pairs={{0,1},{1,2},{2,3},{3,4},{4,5},{5,6},{6,7},{8,9},{9,10},{10,11},{11... | collective-permute-start | bytes 294920 | tf_op jit(solution)/shard_map/ppermute | solution.py:26
  35.4 5.4 %collective-permute-start.7 = (bf16[96,512]{1,0:T(8,128)(2,1)S(1)}, bf16[96,512]{1,0:T(8,128)(2,1)S(1)}, u32[]{:S(2)}, u32[]{:S(2)}) collective-permute-start(bf16[96,512]{1,0:T(8,128)(2,1)S(1)} %get-tuple-element.139), channel_id=1, source_target_pairs={{1,0},{2,1},{3,2},{4,3},{5,4},{6,5},{7,6},{9,8},{10,9},{11,10},{12... | collective-permute-start | bytes 294920 | tf_op jit(solution)/shard_map/ppermute | solution.py:26
  50.5 2.0 %collective-permute-start.9 = (bf16[256,512]{1,0:T(8,128)(2,1)S(1)}, bf16[256,512]{1,0:T(8,128)(2,1)S(1)}, u32[]{:S(2)}, u32[]{:S(2)}) collective-permute-start(bf16[256,512]{1,0:T(8,128)(2,1)S(1)} %get-tuple-element.164), channel_id=1, source_target_pairs={{0,8},{8,0},{16,24},{24,16},{32,40},{40,32},{48,56},{56,48},{64,72... | collective-permute-start | bytes 786440 | tf_op jit(solution)/shard_map/ppermute | solution.py:30
  50.6 1.9 %collective-permute-start.8 = (bf16[32,3584]{1,0:T(8,128)(2,1)S(1)}, bf16[32,3584]{1,0:T(8,128)(2,1)S(1)}, u32[]{:S(2)}, u32[]{:S(2)}) collective-permute-start(bf16[32,3584]{1,0:T(8,128)(2,1)S(1)} %get-tuple-element.150.refs_1_), channel_id=1, source_target_pairs={{0,8},{8,0},{16,24},{24,16},{32,40},{40,32},{48,56},{56,48},{64,72... | collective-permute-start | bytes 688136 | tf_op jit(solution)/shard_map/ppermute | solution.py:30
  54.3 32.6 %all-to-all-start = ((bf16[8,240,512]{2,1,0:T(8,128)(2,1)}), bf16[8,240,512]{2,1,0:T(8,128)(2,1)}, u32[]{:S(2)}, u32[]{:S(2)}) async-start(bf16[8,240,512]{2,1,0:T(8,128)(2,1)} %shard_map.333), calls=%async_computation | async-start | bytes 3932160 | tf_op jit(solution)/shard_map/all_to_all | solution.py:600
  61.1 27.7 %collective-permute-start.10 = (bf16[48,512]{1,0:T(8,128)(2,1)S(1)}, bf16[48,512]{1,0:T(8,128)(2,1)S(1)}, u32[]{:S(2)}, u32[]{:S(2)}) collective-permute-start(bf16[48,512]{1,0:T(8,128)(2,1)S(1)} %get-tuple-element.167), channel_id=1, source_target_pairs={{0,1},{1,2},{2,3},{3,4},{4,5},{5,6},{6,7},{8,9},{9,10},{10,11},{11... | collective-permute-start | bytes 147464 | tf_op jit(solution)/shard_map/ppermute | solution.py:26
  64.5 25.0 %collective-permute-start.11 = (bf16[48,512]{1,0:T(8,128)(2,1)S(1)}, bf16[48,512]{1,0:T(8,128)(2,1)S(1)}, u32[]{:S(2)}, u32[]{:S(2)}) collective-permute-start(bf16[48,512]{1,0:T(8,128)(2,1)S(1)} %get-tuple-element.168), channel_id=1, source_target_pairs={{1,0},{2,1},{3,2},{4,3},{5,4},{6,5},{7,6},{9,8},{10,9},{11,10},{12... | collective-permute-start | bytes 147464 | tf_op jit(solution)/shard_map/ppermute | solution.py:26
  112.0 14.7 %all-to-all-start.2 = ((bf16[16,15,512]{2,1,0:T(8,128)(2,1)}), bf16[16,15,512]{2,1,0:T(8,128)(2,1)S(1)}, u32[]{:S(2)}, u32[]{:S(2)}) async-start(bf16[16,15,512]{2,1,0:T(8,128)(2,1)} %broadcast_in_dim.14), calls=%async_computation.2 | async-start | bytes 524288 | tf_op jit(solution)/shard_map/all_to_all | solution.py:607
  128.3 29.7 %all-to-all-start.3 = ((bf16[8,224,512]{2,1,0:T(8,128)(2,1)}), bf16[8,224,512]{2,1,0:T(8,128)(2,1)S(1)}, u32[]{:S(2)}, u32[]{:S(2)}) async-start(bf16[8,224,512]{2,1,0:T(8,128)(2,1)} %broadcast_in_dim.15), calls=%async_computation.3 | async-start | bytes 3670016 | tf_op jit(solution)/shard_map/all_to_all | solution.py:886
  133.7 10.0 %collective-permute-start.14 = (bf16[16,512]{1,0:T(8,128)(2,1)S(1)}, bf16[16,512]{1,0:T(8,128)(2,1)S(1)}, u32[]{:S(2)}, u32[]{:S(2)}) collective-permute-start(bf16[16,512]{1,0:T(8,128)(2,1)S(1)} %slice.13), channel_id=1, source_target_pairs={{0,8},{8,0},{16,24},{24,16},{32,40},{40,32},{48,56},{56,48},{64,72... | collective-permute-start | bytes 49160 | tf_op jit(solution)/shard_map/ppermute | solution.py:30
  138.4 6.5 %collective-permute-start.12 = (bf16[48,512]{1,0:T(8,128)(2,1)S(1)}, bf16[48,512]{1,0:T(8,128)(2,1)S(1)}, u32[]{:S(2)}, u32[]{:S(2)}) collective-permute-start(bf16[48,512]{1,0:T(8,128)(2,1)S(1)} %get-tuple-element.177), channel_id=1, source_target_pairs={{0,8},{8,16},{16,24},{24,32},{32,40},{40,48},{48,56},{56,64},{64,7... | collective-permute-start | bytes 147464 | tf_op jit(solution)/shard_map/ppermute | solution.py:26
  141.9 5.7 %collective-permute-start.13 = (bf16[48,512]{1,0:T(8,128)(2,1)S(1)}, bf16[48,512]{1,0:T(8,128)(2,1)S(1)}, u32[]{:S(2)}, u32[]{:S(2)}) collective-permute-start(bf16[48,512]{1,0:T(8,128)(2,1)S(1)} %get-tuple-element.178), channel_id=1, source_target_pairs={{8,0},{16,8},{24,16},{32,24},{40,32},{48,40},{56,48},{64,56},{72,6... | collective-permute-start | bytes 147464 | tf_op jit(solution)/shard_map/ppermute | solution.py:26
  158.0 4.3 %collective-permute-start.15 = (bf16[8,224,512]{2,1,0:T(8,128)(2,1)S(1)}, bf16[8,224,512]{2,1,0:T(8,128)(2,1)S(1)}, u32[]{:S(2)}, u32[]{:S(2)}) collective-permute-start(bf16[8,224,512]{2,1,0:T(8,128)(2,1)S(1)} %all-to-all-done.3.mine), channel_id=1, source_target_pairs={{0,8},{8,0},{16,24},{24,16},{32,40},{40,32},{48,56},{56,48},{64,72... | collective-permute-start | bytes 5505032 | tf_op jit(solution)/shard_map/ppermute | solution.py:30

commit v6 on v5

--- a/solution.py
+++ b/solution.py
@@ -724,7 +724,7 @@
     tall1 = joined(keys1[:5])
     wide1 = len(keys1[5])
     flat1, ask1 = joined(keys1), joined(queries1)
-    picks1, pick1, gain_v, qkv_v, merge_v, band1, at1 = preload(
+    picks1, pick1, gain_v, qkv_v, merge_v, band1, at1, *ready3 = preload(
         [
             chosen(moved(keys1[5], 0, ccolumns) + moved(keys1[6], 0, -ccolumns), tall1),
             chosen(ask1, flat1),
@@ -733,6 +733,10 @@
             w_merge,
             Late(jnp.asarray(band_bias(ask1, flat1))),
             places(flat1),
+            Late(grad_fine.reshape(count, width)),
+            perm,
+            out_fine,
+            qkv_fine,
         ],
         near1,
     )
@@ -824,17 +828,17 @@
             ((width, 2 * width), bf16),
         ],
     )(
-        Late(grad_fine.reshape(count, width)),
+        ready3[0],
         grad_merged,
-        perm,
+        ready3[1],
         query0,
         kvb,
         normedb,
         ratiob,
         att0,
         *probs,
-        out_fine,
-        qkv_fine,
+        ready3[2],
+        ready3[3],
         gain0,
         where,
     )

time: 166 us -> 165 us (level)
  no operation moved by 1% of the time
where the time goes in v6:
time: 165 us; the launch traced here: 164 us
  starting transfers between devices  54.5 us (33%)
  waiting for transfers between devices  52.4 us (32%)
  Pallas kernels  29 us (18%)
  blocking collectives  21.7 us (13%)
  local copies, waits for them, and re-layouts  3.48 us (2%)
  other arithmetic  2.03 us (1%)
    ppermute x12, starting transfers between devices, shifted(): return lax.ppermute(x, axis, pairs)  30.9 us
    pallas_call x11, Pallas kernels, run(): pl.pallas_call(body, out_shape=[jax.ShapeDtypeStruct(shape, dtype) for sh...  22.6 us
    all_to_all x1, blocking collectives, trade_rows(): return lax.all_to_all(pieces, 'row', 0, 0, axis_index_groups=groups)  21.7 us
    all_to_all x1, waiting for transfers between devices, scatter_over_columns(): pieces = lax.all_to_all(x, 'col', 0, 0)  21.2 us
    ppermute x12, waiting for transfers between devices, shifted(): return lax.ppermute(x, axis, pairs)  10.3 us
    all_to_all x1, waiting for transfers between devices, trade_rows(): return lax.all_to_all(pieces, 'row', 0, 0, axis_index_groups=groups)  8.3 us
    all_to_all x1, waiting for transfers between devices, per_device(): x = lax.all_to_all(jnp.broadcast_to(x, (cols,) + x.shape), 'col', 0, 0)  7.96 us
    all_to_all x1, starting transfers between devices, scatter_over_columns(): pieces = lax.all_to_all(x, 'col', 0, 0)  6.73 us
  transfers between devices with their start and end apart: 19, of which 10 were waited for; matrix products, arithmetic and copies ran while one was open for 2% of the time, Pallas kernels for 7%

profile of v6, /device:TPU:1, one launch (start us, length us, event | category | flops | bytes accessed | tf_op | source)
XLA Modules:
  0.0 164.0 jit_solution(7000054680187551181)
XLA Ops:
  1.5 4.9 %collective-permute-start = (bf16[176,256]{1,0:T(8,128)(2,1)S(1)}, bf16[176,256]{1,0:T(8,128)(2,1)S(1)}, u32[]{:S(2)}, u32[]{:S(2)}) collective-permute-start(bf16[176,256]{1,0:T(8,128)(2,1)S(1)} %get-tuple-element.121), channel_id=1, source_target_pairs={{0,8},{8,16},{16,24},{24,32},{32,40},{40,48},{48,56},{56,64},{64,7... | collective-permute-start | bytes 270344 | tf_op jit(solution)/shard_map/ppermute | solution.py:26
  12.5 3.1 %collective-permute-start.2 = (bf16[144,256]{1,0:T(8,128)(2,1)S(1)}, bf16[144,256]{1,0:T(8,128)(2,1)S(1)}, u32[]{:S(2)}, u32[]{:S(2)}) collective-permute-start(bf16[144,256]{1,0:T(8,128)(2,1)S(1)} %get-tuple-element.125), channel_id=1, source_target_pairs={{0,1},{1,2},{2,3},{3,4},{4,5},{5,6},{6,7},{8,9},{9,10},{10,11},{11... | collective-permute-start | bytes 221192 | tf_op jit(solution)/shard_map/ppermute | solution.py:26
  17.0 3.7 %collective-permute-done.3.refs_4_ = bf16[144,256]{1,0:T(8,128)(2,1)S(1)} collective-permute-done((bf16[144,256]{1,0:T(8,128)(2,1)S(1)}, bf16[144,256]{1,0:T(8,128)(2,1)S(1)}, u32[]{:S(2)}, u32[]{:S(2)}) %collective-permute-start.3) | collective-permute-done | bytes 73760 | tf_op jit(solution)/shard_map/ppermute | solution.py:26
  20.7 2.8 %shard_map.326 = (bf16[32,1024]{1,0:T(8,128)(2,1)S(1)}, bf16[64,512]{1,0:T(8,128)(2,1)S(1)}, bf16[32,512]{1,0:T(8,128)(2,1)S(1)}, bf16[32,512]{1,0:T(8,128)(2,1)...) custom-call(bf16[128,256]{1,0:T(8,128)(2,1)S(1)} %get-tuple-element., ...), custom_call_target="tpu_custom_call" | custom-call | flops 268435456 | bytes 4194304 | tf_op jit(solution)/shard_map/pallas_call | solution.py:557
  23.5 3.3 %collective-permute-start.4 = (bf16[32,512]{1,0:T(8,128)(2,1)S(1)}, bf16[32,512]{1,0:T(8,128)(2,1)S(1)}, u32[]{:S(2)}, u32[]{:S(2)}) collective-permute-start(bf16[32,512]{1,0:T(8,128)(2,1)S(1)} %get-tuple-element.136), channel_id=1, source_target_pairs={{0,8},{8,16},{16,24},{24,32},{32,40},{40,48},{48,56},{56,64},{64,7... | collective-permute-start | bytes 98312 | tf_op jit(solution)/shard_map/ppermute | solution.py:26
  28.7 2.1 %shard_map.327 = (bf16[192,128]{1,0:T(8,128)(2,1)S(1)}, bf16[144,320]{1,0:T(8,128)(2,1)S(1)}, f32[1,512]{1,0:T(1,128)S(1)}, bf16[512,1536]{1,0:T(8,128)(2,1)S(1)...) custom-call(bf16[192,128]{1,0:T(8,128)(2,1)} %constant.59.clone.refs, ...), custom_call_target="tpu_custom_call" | custom-call | flops 1048576 | bytes 4194304 | tf_op jit(solution)/shard_map/pallas_call | solution.py:587
  32.2 3.1 %collective-permute-start.6 = (bf16[96,512]{1,0:T(8,128)(2,1)S(1)}, bf16[96,512]{1,0:T(8,128)(2,1)S(1)}, u32[]{:S(2)}, u32[]{:S(2)}) collective-permute-start(bf16[96,512]{1,0:T(8,128)(2,1)S(1)} %get-tuple-element.150), channel_id=1, source_target_pairs={{0,1},{1,2},{2,3},{3,4},{4,5},{5,6},{6,7},{8,9},{9,10},{10,11},{11... | collective-permute-start | bytes 294920 | tf_op jit(solution)/shard_map/ppermute | solution.py:26
  36.7 2.7 %shard_map.331 = (bf16[320,512]{1,0:T(8,128)(2,1)S(1)}, bf16[320,256]{1,0:T(8,128)(2,1)S(1)}, f32[320,256]{1,0:T(8,128)S(1)}, f32[128,320]{1,0:T(8,128)S(1)}, f3...) custom-call(bf16[128,256]{1,0:T(8,128)(2,1)S(1)} %get-tuple-element.166.refs_0_.refs_3_, ...), custom_call_target="tpu_custom_call" | custom-call | flops 268435456 | bytes 4194304 | tf_op jit(solution)/shard_map/pallas_call | solution.py:557
  40.8 5.9 %shard_map.330 = (bf16[32,1024]{1,0:T(8,128)(2,1)S(1)}, bf16[32,3584]{1,0:T(8,128)(2,1)S(1)}, f32[1,512]{1,0:T(1,128)S(1)}, f32[32,1024]{1,0:T(8,128)S(1)}) custom-call(bf16[64,512]{1,0:T(8,128)(2,1)S(1)} %get-tuple-element.135.refs_0_, bf16[32,512]{1,0:T(8,128)(2,1)S(1)} %collective-permute-done.4.refs_1_, ...), custom_call_target="tpu_custom_call" | custom-call | flops 268435456 | bytes 4194304 | tf_op jit(solution)/shard_map/pallas_call | solution.py:557
  46.7 3.0 %shard_map.332 = (f32[128,256]{1,0:T(8,128)S(1)}, bf16[128,256]{1,0:T(8,128)(2,1)S(1)}, f32[224,512]{1,0:T(8,128)S(1)}, bf16[48,512]{1,0:T(8,128)(2,1)S(1)}, bf1...) custom-call(bf16[128,256]{1,0:T(8,128)(2,1)S(1)} %get-tuple-element., ...), custom_call_target="tpu_custom_call" | custom-call | flops 268435456 | bytes 4194304 | tf_op jit(solution)/shard_map/pallas_call | solution.py:557
  53.6 6.7 %all-to-all-start = ((bf16[8,240,512]{2,1,0:T(8,128)(2,1)}), bf16[8,240,512]{2,1,0:T(8,128)(2,1)}, u32[]{:S(2)}, u32[]{:S(2)}) async-start(bf16[8,240,512]{2,1,0:T(8,128)(2,1)} %shard_map.333), calls=%async_computation | async-start | bytes 3932160 | tf_op jit(solution)/shard_map/all_to_all | solution.py:600
  60.4 3.4 %collective-permute-start.10 = (bf16[48,512]{1,0:T(8,128)(2,1)S(1)}, bf16[48,512]{1,0:T(8,128)(2,1)S(1)}, u32[]{:S(2)}, u32[]{:S(2)}) collective-permute-start(bf16[48,512]{1,0:T(8,128)(2,1)S(1)} %get-tuple-element.183), channel_id=1, source_target_pairs={{0,1},{1,2},{2,3},{3,4},{4,5},{5,6},{6,7},{8,9},{9,10},{10,11},{11... | collective-permute-start | bytes 147464 | tf_op jit(solution)/shard_map/ppermute | solution.py:26
  65.0 21.2 %all-to-all-done = bf16[8,240,512]{2,1,0:T(8,128)(2,1)} async-done(((bf16[8,240,512]{2,1,0:T(8,128)(2,1)}), bf16[8,240,512]{2,1,0:T(8,128)(2,1)}, u32[]{:S(2)}, u32[]{:S(2)}) %all-to-all-start) | async-done | bytes 1966112 | tf_op jit(solution)/shard_map/all_to_all | solution.py:600
  88.9 21.7 %all_to_all.20 = bf16[16,15,512]{2,1,0:T(8,128)(2,1)S(1)} all-to-all(bf16[16,15,512]{2,1,0:T(8,128)(2,1)S(1)} %reshape.52), channel_id=1, replica_groups={{0,16,32,48,64,80,96,112,128,144,160,176,192,208,224,240},{8,24,40,56,7..., dimensions={0} | all-to-all | bytes 491520 | tf_op jit(solution)/shard_map/all_to_all | solution.py:607
  111.4 5.3 %all-to-all-start.2 = ((bf16[16,15,512]{2,1,0:T(8,128)(2,1)}), bf16[16,15,512]{2,1,0:T(8,128)(2,1)S(1)}, u32[]{:S(2)}, u32[]{:S(2)}) async-start(bf16[16,15,512]{2,1,0:T(8,128)(2,1)} %broadcast_in_dim.14), calls=%async_computation.2 | async-start | bytes 524288 | tf_op jit(solution)/shard_map/all_to_all | solution.py:607
  117.8 8.3 %all-to-all-done.2 = bf16[16,15,512]{2,1,0:T(8,128)(2,1)S(1)} async-done(((bf16[16,15,512]{2,1,0:T(8,128)(2,1)}), bf16[16,15,512]{2,1,0:T(8,128)(2,1)S(1)}, u32[]{:S(2)}, u32[]{:S(2)}) %all-to-all-start.2) | async-done | bytes 245792 | tf_op jit(solution)/shard_map/all_to_all | solution.py:607
  127.6 5.5 %all-to-all-start.3 = ((bf16[8,224,512]{2,1,0:T(8,128)(2,1)}), bf16[8,224,512]{2,1,0:T(8,128)(2,1)S(1)}, u32[]{:S(2)}, u32[]{:S(2)}) async-start(bf16[8,224,512]{2,1,0:T(8,128)(2,1)} %broadcast_in_dim.15), calls=%async_computation.3 | async-start | bytes 3670016 | tf_op jit(solution)/shard_map/all_to_all | solution.py:890
  133.1 4.7 %collective-permute-start.14 = (bf16[16,512]{1,0:T(8,128)(2,1)S(1)}, bf16[16,512]{1,0:T(8,128)(2,1)S(1)}, u32[]{:S(2)}, u32[]{:S(2)}) collective-permute-start(bf16[16,512]{1,0:T(8,128)(2,1)S(1)} %slice.13), channel_id=1, source_target_pairs={{0,8},{8,0},{16,24},{24,16},{32,40},{40,32},{48,56},{56,48},{64,72... | collective-permute-start | bytes 49160 | tf_op jit(solution)/shard_map/ppermute | solution.py:30
  137.7 3.4 %collective-permute-start.12 = (bf16[48,512]{1,0:T(8,128)(2,1)S(1)}, bf16[48,512]{1,0:T(8,128)(2,1)S(1)}, u32[]{:S(2)}, u32[]{:S(2)}) collective-permute-start(bf16[48,512]{1,0:T(8,128)(2,1)S(1)} %get-tuple-element.193), channel_id=1, source_target_pairs={{0,8},{8,16},{16,24},{24,32},{32,40},{40,48},{48,56},{56,64},{64,7... | collective-permute-start | bytes 147464 | tf_op jit(solution)/shard_map/ppermute | solution.py:26
  144.3 2.6 %collective-permute-done.13.refs_2_ = bf16[48,512]{1,0:T(8,128)(2,1)S(1)} collective-permute-done((bf16[48,512]{1,0:T(8,128)(2,1)S(1)}, bf16[48,512]{1,0:T(8,128)(2,1)S(1)}, u32[]{:S(2)}, u32[]{:S(2)}) %collective-permute-start.13) | collective-permute-done | bytes 49184 | tf_op jit(solution)/shard_map/ppermute | solution.py:26
  146.9 2.5 %shard_map.335 = bf16[128,256]{1,0:T(8,128)(2,1)} custom-call(f32[128,512]{1,0:T(8,128)S(1)} %get-tuple-element.192.refs_0_, bf16[48,512]{1,0:T(8,128)(2,1)S(1)} %collective-permute-done.12.refs_1_, bf16[48,512]{1,0:T(8,128)(2,1)S(1)} %collective-permute-done.13.refs_2_, bf16[128,48]{1,0:T(8,128)(2,1)} %constant.69.clone.refs_3_, ...), custom_call_target="tpu_custom_call" | custom-call | flops 268435456 | bytes 4194304 | tf_op jit(solution)/shard_map/pallas_call | solution.py:557
  149.3 8.0 %all-to-all-done.3.mine = bf16[8,224,512]{2,1,0:T(8,128)(2,1)S(1)} async-done(((bf16[8,224,512]{2,1,0:T(8,128)(2,1)}), bf16[8,224,512]{2,1,0:T(8,128)(2,1)S(1)}, u32[]{:S(2)}, u32[]{:S(2)}) %all-to-all-start.3) | async-done | bytes 1835040 | tf_op jit(solution)/shard_map/all_to_all | solution.py:890
  158.1 3.4 %collective-permute-done.15.other = bf16[8,224,512]{2,1,0:T(8,128)(2,1)S(1)} collective-permute-done((bf16[8,224,512]{2,1,0:T(8,128)(2,1)S(1)}, bf16[8,224,512]{2,1,0:T(8,128)(2,1)S(1)}, u32[]{:S(2)}, u32[]{:S(2)}) %collective-permute-start.15) | collective-permute-done | bytes 1835040 | tf_op jit(solution)/shard_map/ppermute | solution.py:30
  161.6 2.5 %shard_map.336 = (bf16[16,64,512]{2,1,0:T(8,128)(2,1)}, bf16[16,32,1536]{2,1,0:T(8,128)(2,1)}, bf16[16,32,512]{2,1,0:T(8,128)(2,1)}, bf16[16,16,768]{2,1,0:T(8,128)(2,1)}, bf16[16,16,256]{2,1,0:T(8,128)(2,1)}) custom-call(s32[4]{0:T(128)S(1)} %pad_add_fusion.refs_13_.refs_14_.refs_7_.refs_15_.where, bf16[8,224,512]{2,1,0:T(8,128)(2,1)S(1)} %all-to-all-done.3.mine, ...), custom_call_target="tpu_custom_call" | custom-call | tf_op jit(solution)/shard_map/pallas_call | solution.py:903
  (41 shorter events, 29.5 us)
Async XLA Ops:
  1.5 8.7 %collective-permute-start = (bf16[176,256]{1,0:T(8,128)(2,1)S(1)}, bf16[176,256]{1,0:T(8,128)(2,1)S(1)}, u32[]{:S(2)}, u32[]{:S(2)}) collective-permute-start(bf16[176,256]{1,0:T(8,128)(2,1)S(1)} %get-tuple-element.121), channel_id=1, source_target_pairs={{0,8},{8,16},{16,24},{24,32},{32,40},{40,48},{48,56},{56,64},{64,7... | collective-permute-start | bytes 270344 | tf_op jit(solution)/shard_map/ppermute | solution.py:26
  6.5 5.8 %collective-permute-start.1 = (bf16[176,256]{1,0:T(8,128)(2,1)S(1)}, bf16[176,256]{1,0:T(8,128)(2,1)S(1)}, u32[]{:S(2)}, u32[]{:S(2)}) collective-permute-start(bf16[176,256]{1,0:T(8,128)(2,1)S(1)} %get-tuple-element.107), channel_id=1, source_target_pairs={{8,0},{16,8},{24,16},{32,24},{40,32},{48,40},{56,48},{64,56},{72,6... | collective-permute-start | bytes 270344 | tf_op jit(solution)/shard_map/ppermute | solution.py:26
  12.5 4.5 %collective-permute-start.2 = (bf16[144,256]{1,0:T(8,128)(2,1)S(1)}, bf16[144,256]{1,0:T(8,128)(2,1)S(1)}, u32[]{:S(2)}, u32[]{:S(2)}) collective-permute-start(bf16[144,256]{1,0:T(8,128)(2,1)S(1)} %get-tuple-element.125), channel_id=1, source_target_pairs={{0,1},{1,2},{2,3},{3,4},{4,5},{5,6},{6,7},{8,9},{9,10},{10,11},{11... | collective-permute-start | bytes 221192 | tf_op jit(solution)/shard_map/ppermute | solution.py:26
  15.6 5.1 %collective-permute-start.3 = (bf16[144,256]{1,0:T(8,128)(2,1)S(1)}, bf16[144,256]{1,0:T(8,128)(2,1)S(1)}, u32[]{:S(2)}, u32[]{:S(2)}) collective-permute-start(bf16[144,256]{1,0:T(8,128)(2,1)S(1)} %get-tuple-element.126), channel_id=1, source_target_pairs={{1,0},{2,1},{3,2},{4,3},{5,4},{6,5},{7,6},{9,8},{10,9},{11,10},{12... | collective-permute-start | bytes 221192 | tf_op jit(solution)/shard_map/ppermute | solution.py:26
  23.5 7.4 %collective-permute-start.4 = (bf16[32,512]{1,0:T(8,128)(2,1)S(1)}, bf16[32,512]{1,0:T(8,128)(2,1)S(1)}, u32[]{:S(2)}, u32[]{:S(2)}) collective-permute-start(bf16[32,512]{1,0:T(8,128)(2,1)S(1)} %get-tuple-element.136), channel_id=1, source_target_pairs={{0,8},{8,16},{16,24},{24,32},{32,40},{40,48},{48,56},{56,64},{64,7... | collective-permute-start | bytes 98312 | tf_op jit(solution)/shard_map/ppermute | solution.py:26
  26.8 5.2 %collective-permute-start.5 = (bf16[32,512]{1,0:T(8,128)(2,1)S(1)}, bf16[32,512]{1,0:T(8,128)(2,1)S(1)}, u32[]{:S(2)}, u32[]{:S(2)}) collective-permute-start(bf16[32,512]{1,0:T(8,128)(2,1)S(1)} %get-tuple-element.137), channel_id=1, source_target_pairs={{8,0},{16,8},{24,16},{32,24},{40,32},{48,40},{56,48},{64,56},{72,6... | collective-permute-start | bytes 98312 | tf_op jit(solution)/shard_map/ppermute | solution.py:26
  32.2 8.6 %collective-permute-start.6 = (bf16[96,512]{1,0:T(8,128)(2,1)S(1)}, bf16[96,512]{1,0:T(8,128)(2,1)S(1)}, u32[]{:S(2)}, u32[]{:S(2)}) collective-permute-start(bf16[96,512]{1,0:T(8,128)(2,1)S(1)} %get-tuple-element.150), channel_id=1, source_target_pairs={{0,1},{1,2},{2,3},{3,4},{4,5},{5,6},{6,7},{8,9},{9,10},{10,11},{11... | collective-permute-start | bytes 294920 | tf_op jit(solution)/shard_map/ppermute | solution.py:26
  35.4 5.4 %collective-permute-start.7 = (bf16[96,512]{1,0:T(8,128)(2,1)S(1)}, bf16[96,512]{1,0:T(8,128)(2,1)S(1)}, u32[]{:S(2)}, u32[]{:S(2)}) collective-permute-start(bf16[96,512]{1,0:T(8,128)(2,1)S(1)} %get-tuple-element.151), channel_id=1, source_target_pairs={{1,0},{2,1},{3,2},{4,3},{5,4},{6,5},{7,6},{9,8},{10,9},{11,10},{12... | collective-permute-start | bytes 294920 | tf_op jit(solution)/shard_map/ppermute | solution.py:26
  49.7 2.0 %collective-permute-start.9 = (bf16[256,512]{1,0:T(8,128)(2,1)S(1)}, bf16[256,512]{1,0:T(8,128)(2,1)S(1)}, u32[]{:S(2)}, u32[]{:S(2)}) collective-permute-start(bf16[256,512]{1,0:T(8,128)(2,1)S(1)} %get-tuple-element.180), channel_id=1, source_target_pairs={{0,8},{8,0},{16,24},{24,16},{32,40},{40,32},{48,56},{56,48},{64,72... | collective-permute-start | bytes 786440 | tf_op jit(solution)/shard_map/ppermute | solution.py:30
  49.8 1.9 %collective-permute-start.8 = (bf16[32,3584]{1,0:T(8,128)(2,1)S(1)}, bf16[32,3584]{1,0:T(8,128)(2,1)S(1)}, u32[]{:S(2)}, u32[]{:S(2)}) collective-permute-start(bf16[32,3584]{1,0:T(8,128)(2,1)S(1)} %get-tuple-element.162.refs_1_), channel_id=1, source_target_pairs={{0,8},{8,0},{16,24},{24,16},{32,40},{40,32},{48,56},{56,48},{64,72... | collective-permute-start | bytes 688136 | tf_op jit(solution)/shard_map/ppermute | solution.py:30
  53.6 32.5 %all-to-all-start = ((bf16[8,240,512]{2,1,0:T(8,128)(2,1)}), bf16[8,240,512]{2,1,0:T(8,128)(2,1)}, u32[]{:S(2)}, u32[]{:S(2)}) async-start(bf16[8,240,512]{2,1,0:T(8,128)(2,1)} %shard_map.333), calls=%async_computation | async-start | bytes 3932160 | tf_op jit(solution)/shard_map/all_to_all | solution.py:600
  60.4 27.7 %collective-permute-start.10 = (bf16[48,512]{1,0:T(8,128)(2,1)S(1)}, bf16[48,512]{1,0:T(8,128)(2,1)S(1)}, u32[]{:S(2)}, u32[]{:S(2)}) collective-permute-start(bf16[48,512]{1,0:T(8,128)(2,1)S(1)} %get-tuple-element.183), channel_id=1, source_target_pairs={{0,1},{1,2},{2,3},{3,4},{4,5},{5,6},{6,7},{8,9},{9,10},{10,11},{11... | collective-permute-start | bytes 147464 | tf_op jit(solution)/shard_map/ppermute | solution.py:26
  63.7 25.1 %collective-permute-start.11 = (bf16[48,512]{1,0:T(8,128)(2,1)S(1)}, bf16[48,512]{1,0:T(8,128)(2,1)S(1)}, u32[]{:S(2)}, u32[]{:S(2)}) collective-permute-start(bf16[48,512]{1,0:T(8,128)(2,1)S(1)} %get-tuple-element.184), channel_id=1, source_target_pairs={{1,0},{2,1},{3,2},{4,3},{5,4},{6,5},{7,6},{9,8},{10,9},{11,10},{12... | collective-permute-start | bytes 147464 | tf_op jit(solution)/shard_map/ppermute | solution.py:26
  111.4 14.7 %all-to-all-start.2 = ((bf16[16,15,512]{2,1,0:T(8,128)(2,1)}), bf16[16,15,512]{2,1,0:T(8,128)(2,1)S(1)}, u32[]{:S(2)}, u32[]{:S(2)}) async-start(bf16[16,15,512]{2,1,0:T(8,128)(2,1)} %broadcast_in_dim.14), calls=%async_computation.2 | async-start | bytes 524288 | tf_op jit(solution)/shard_map/all_to_all | solution.py:607
  127.6 29.7 %all-to-all-start.3 = ((bf16[8,224,512]{2,1,0:T(8,128)(2,1)}), bf16[8,224,512]{2,1,0:T(8,128)(2,1)S(1)}, u32[]{:S(2)}, u32[]{:S(2)}) async-start(bf16[8,224,512]{2,1,0:T(8,128)(2,1)} %broadcast_in_dim.15), calls=%async_computation.3 | async-start | bytes 3670016 | tf_op jit(solution)/shard_map/all_to_all | solution.py:890
  133.1 10.0 %collective-permute-start.14 = (bf16[16,512]{1,0:T(8,128)(2,1)S(1)}, bf16[16,512]{1,0:T(8,128)(2,1)S(1)}, u32[]{:S(2)}, u32[]{:S(2)}) collective-permute-start(bf16[16,512]{1,0:T(8,128)(2,1)S(1)} %slice.13), channel_id=1, source_target_pairs={{0,8},{8,0},{16,24},{24,16},{32,40},{40,32},{48,56},{56,48},{64,72... | collective-permute-start | bytes 49160 | tf_op jit(solution)/shard_map/ppermute | solution.py:30
  137.7 6.5 %collective-permute-start.12 = (bf16[48,512]{1,0:T(8,128)(2,1)S(1)}, bf16[48,512]{1,0:T(8,128)(2,1)S(1)}, u32[]{:S(2)}, u32[]{:S(2)}) collective-permute-start(bf16[48,512]{1,0:T(8,128)(2,1)S(1)} %get-tuple-element.193), channel_id=1, source_target_pairs={{0,8},{8,16},{16,24},{24,32},{32,40},{40,48},{48,56},{56,64},{64,7... | collective-permute-start | bytes 147464 | tf_op jit(solution)/shard_map/ppermute | solution.py:26
  141.2 5.7 %collective-permute-start.13 = (bf16[48,512]{1,0:T(8,128)(2,1)S(1)}, bf16[48,512]{1,0:T(8,128)(2,1)S(1)}, u32[]{:S(2)}, u32[]{:S(2)}) collective-permute-start(bf16[48,512]{1,0:T(8,128)(2,1)S(1)} %get-tuple-element.194), channel_id=1, source_target_pairs={{8,0},{16,8},{24,16},{32,24},{40,32},{48,40},{56,48},{64,56},{72,6... | collective-permute-start | bytes 147464 | tf_op jit(solution)/shard_map/ppermute | solution.py:26
  157.3 4.3 %collective-permute-start.15 = (bf16[8,224,512]{2,1,0:T(8,128)(2,1)S(1)}, bf16[8,224,512]{2,1,0:T(8,128)(2,1)S(1)}, u32[]{:S(2)}, u32[]{:S(2)}) collective-permute-start(bf16[8,224,512]{2,1,0:T(8,128)(2,1)S(1)} %all-to-all-done.3.mine), channel_id=1, source_target_pairs={{0,8},{8,0},{16,24},{24,16},{32,40},{40,32},{48,56},{56,48},{64,72... | collective-permute-start | bytes 5505032 | tf_op jit(solution)/shard_map/ppermute | solution.py:30
